TPU v7x, 512 devices: a whole 4x8x8 slice. The times are simulated.
512 devices in a mesh: seq: 128 (over y, x, z_lo, core), tp: 4 (over z_hi).
Axes of the slice: x: 4, y: 8, z: 8 (z_hi: 4, z_lo: 2; z = z_hi * 2 + z_lo), core: 2. Of those that a mesh axis runs over, the one named last changes fastest.
Arguments:
- tokens: bfloat16 [16384, 2048], P('seq', 'tp'), may hold values from -6 to 6
- norm_gain: float32 [2048], replicated, may hold values from 0.25 to 1.75
- in_weight: bfloat16 [2048, 3, 2048], P('seq', None, 'tp'), may hold values from -0.125 to 0.125
- short_taps: float32 [3, 3, 2048], P(None, None, 'tp'), may hold values from -3.5 to 3.5
- filter_response: float32 [16384, 2048], P('seq', 'tp'), may hold values from -1.1 to 1.1
- skip_gain: float32 [2048], P('tp'), may hold values from -4 to 4
- out_weight: bfloat16 [2048, 2048], P('seq', 'tp'), may hold values from -0.125 to 0.125
Outputs:
- hyena_out: bfloat16 [16384, 2048], P('seq', 'tp')
All inputs are finite; a program needn't handle non-finite values.
Results may differ from a plain program's by a relative error of at most 0.017.
Values may be sent and summed in bfloat16 or wider, within the bound.
No kernel may reach another device: no remote copies, remote signals or barrier semaphores. Data moves between devices by JAX's collectives and lax.ppermute only.
A program may use at most 64 MiB of HBM per device.

v0:
```python
import math

import jax
import jax.numpy as jnp
from jax import lax
from jax.sharding import PartitionSpec as P

HIGHEST = lax.Precision.HIGHEST


def for_sending(value):

    def short(part):
        return part.astype(jnp.bfloat16) if part.dtype == jnp.float32 else part

    return jax.tree.map(short, value)


def shifted(value, axis, steps):
    count = lax.axis_size(axis)
    first, last = (max(0, -steps), min(count, count - steps))
    return lax.ppermute(value, axis, [(source, source + steps) for source in range(first, last)])


def phase_table(count_out, count_in, period):
    left_side = jnp.arange(count_out, dtype=jnp.int32)[:, None]
    right_side = jnp.arange(count_in, dtype=jnp.int32)[None, :]
    angles = (left_side * right_side % period).astype(jnp.float32) * (2.0 * math.pi / period)
    return (jnp.cos(angles), jnp.sin(angles))


def forward_transform(series, seq_ways, seq_place):
    length = series.shape[0]
    chan_count = series.shape[1]
    per_way = length // seq_ways
    total_len = 2 * seq_ways * length
    blocks = lax.all_to_all(
        series[None].astype(jnp.bfloat16), "seq", split_axis=1, concat_axis=0, tiled=True
    ).astype(jnp.float32)
    cos_far, sin_far = phase_table(2 * seq_ways, seq_ways, 2 * seq_ways)
    flat_rows = blocks.reshape(seq_ways, per_way * chan_count)
    real_part = jnp.dot(cos_far, flat_rows, precision=HIGHEST).reshape(
        2 * seq_ways, per_way, chan_count
    )
    imag_part = -jnp.dot(sin_far, flat_rows, precision=HIGHEST).reshape(
        2 * seq_ways, per_way, chan_count
    )
    freq_ids = jnp.arange(2 * seq_ways, dtype=jnp.int32)[:, None]
    pos_ids = seq_place * per_way + jnp.arange(per_way, dtype=jnp.int32)[None, :]
    twist_angle = (freq_ids * pos_ids % total_len).astype(jnp.float32) * (2.0 * math.pi / total_len)
    cos_twist = jnp.cos(twist_angle)[:, :, None]
    sin_twist = jnp.sin(twist_angle)[:, :, None]
    turned = jnp.stack(
        [
            real_part * cos_twist + imag_part * sin_twist,
            imag_part * cos_twist - real_part * sin_twist,
        ]
    )
    spectrum = lax.all_to_all(
        for_sending(turned), "seq", split_axis=1, concat_axis=2, tiled=True
    ).astype(turned.dtype)
    cos_near, sin_near = phase_table(length, length, length)
    real_in = spectrum[0]
    imag_in = spectrum[1]
    real_out = jnp.einsum("lj,kjc->klc", cos_near, real_in, precision=HIGHEST) + jnp.einsum(
        "lj,kjc->klc", sin_near, imag_in, precision=HIGHEST
    )
    imag_out = jnp.einsum("lj,kjc->klc", cos_near, imag_in, precision=HIGHEST) - jnp.einsum(
        "lj,kjc->klc", sin_near, real_in, precision=HIGHEST
    )
    result = jnp.stack([real_out, imag_out])
    result = lax.all_to_all(
        for_sending(result), "seq", split_axis=2, concat_axis=1, tiled=True
    ).astype(result.dtype)
    return result


def inverse_transform(product, seq_ways, seq_place):
    product = lax.all_to_all(
        for_sending(product), "seq", split_axis=1, concat_axis=2, tiled=True
    ).astype(product.dtype)
    length = product.shape[2]
    chan_count = product.shape[3]
    per_way = length // seq_ways
    total_len = 2 * seq_ways * length
    cos_near, sin_near = phase_table(length, length, length)
    real_in = product[0]
    imag_in = product[1]
    real_back = jnp.einsum("jl,klc->kjc", cos_near, real_in, precision=HIGHEST) - jnp.einsum(
        "jl,klc->kjc", sin_near, imag_in, precision=HIGHEST
    )
    imag_back = jnp.einsum("jl,klc->kjc", cos_near, imag_in, precision=HIGHEST) + jnp.einsum(
        "jl,klc->kjc", sin_near, real_in, precision=HIGHEST
    )
    freq_ids = 2 * seq_place + jnp.arange(2, dtype=jnp.int32)[:, None]
    pos_ids = jnp.arange(length, dtype=jnp.int32)[None, :]
    twist_angle = (freq_ids * pos_ids % total_len).astype(jnp.float32) * (2.0 * math.pi / total_len)
    cos_twist = jnp.cos(twist_angle)[:, :, None]
    sin_twist = jnp.sin(twist_angle)[:, :, None]
    turned = jnp.stack(
        [
            real_back * cos_twist - imag_back * sin_twist,
            real_back * sin_twist + imag_back * cos_twist,
        ]
    )
    gathered_freq = lax.all_to_all(
        for_sending(turned), "seq", split_axis=2, concat_axis=1, tiled=True
    ).astype(turned.dtype)
    cos_far, sin_far = phase_table(seq_ways, 2 * seq_ways, 2 * seq_ways)
    real_flat = gathered_freq[0].reshape(2 * seq_ways, per_way * chan_count)
    imag_flat = gathered_freq[1].reshape(2 * seq_ways, per_way * chan_count)
    series = (
        jnp.dot(cos_far, real_flat, precision=HIGHEST)
        - jnp.dot(sin_far, imag_flat, precision=HIGHEST)
    ) / total_len
    series = series.reshape(seq_ways, per_way, chan_count)
    back_rows = lax.all_to_all(
        for_sending(series), "seq", split_axis=0, concat_axis=1, tiled=True
    ).astype(series.dtype)
    return back_rows[0]


def shards(tokens, norm_gain, in_weight, short_taps, filter_response, skip_gain, out_weight):
    length = tokens.shape[0]
    chan_count = skip_gain.shape[0]
    seq_ways = lax.axis_size("seq")
    seq_place = lax.axis_index("seq")
    features = lax.all_gather(tokens, "tp", axis=1, tiled=True).astype(jnp.float32)
    mean_square = jnp.mean(features * features, axis=1, keepdims=True)
    normed = (features * lax.rsqrt(mean_square + 1e-05) * norm_gain).astype(jnp.bfloat16)
    weight_piece = lax.all_gather(in_weight, "seq", axis=0, tiled=True)
    row_count = weight_piece.shape[0]
    columns = normed
    flat_piece = weight_piece.reshape(row_count, 3 * chan_count)
    summed = jnp.dot(columns, flat_piece, preferred_element_type=jnp.float32)
    projected = summed.reshape(length, 3, chan_count).astype(jnp.bfloat16)
    previous = shifted(projected[length - 2 :], "seq", 1)
    padded = jnp.concatenate([previous, projected], axis=0).astype(jnp.float32)
    shortconv = (
        short_taps[0] * padded[2:]
        + short_taps[1] * padded[1 : length + 1]
        + short_taps[2] * padded[:length]
    )
    query_part = shortconv[:, 0]
    signal = shortconv[:, 1] * shortconv[:, 2]
    kernel_spec = forward_transform(filter_response, seq_ways, seq_place)
    spectrum = forward_transform(signal, seq_ways, seq_place)
    product = jnp.stack(
        [
            spectrum[0] * kernel_spec[0] - spectrum[1] * kernel_spec[1],
            spectrum[0] * kernel_spec[1] + spectrum[1] * kernel_spec[0],
        ]
    )
    convolved = inverse_transform(product, seq_ways, seq_place)
    mixed_sum = convolved + skip_gain * signal
    gated_rows = (query_part * mixed_sum).astype(jnp.bfloat16)
    gated_all = lax.all_gather(gated_rows, "tp", axis=1, tiled=True)
    weight_piece = lax.all_gather(out_weight, "seq", axis=0, tiled=True)
    columns = gated_all
    result = jnp.dot(columns, weight_piece, preferred_element_type=jnp.float32)
    return result.astype(jnp.bfloat16)


def solution(mesh):
    placed = (
        P("seq", "tp"),
        P(),
        P("seq", None, "tp"),
        P(None, None, "tp"),
        P("seq", "tp"),
        P("tp"),
        P("seq", "tp"),
    )
    return jax.shard_map(
        shards, mesh=mesh, in_specs=placed, out_specs=P("seq", "tp"), check_vma=False
    )
```

profile of v0, /device:TPU:1, one launch (start us, length us, event | category | flops | bytes accessed | tf_op | source)
XLA Modules:
  0.0 628.5 jit_solution(6823505251968891567)
XLA Ops:
  9.0 1.4 reduce.1
  11.1 14.2 %all-to-all-start.3 = ((bf16[128,2,256]{2,1,0:T(2,128)(2,1)}), bf16[128,2,256]{2,1,0:T(2,128)(2,1)S(1)}, u32[]{:S(2)}, u32[]{:S(2)}) async-start(bf16[128,2,256]{2,1,0:T(2,128)(2,1)} %reshape.378), calls=%async_computation.3 | async-start | bytes 262144 | tf_op jit(solution)/shard_map/all_to_all | solution.py:37
  25.3 20.2 %all_gather.12 = bf16[128,2048]{1,0:T(8,128)(2,1)S(1)} all-gather(bf16[128,512]{1,0:T(8,128)(2,1)} %param.7), channel_id=1, replica_groups=mesh['seq'=128,'tp'=4] {'tp'}, dimensions={1}, use_global_device_ids=true | all-gather | bytes 655360 | tf_op jit(solution)/shard_map/all_gather | solution.py:128
  46.5 188.0 %all-gather.3.cloned.1.call-done = bf16[2048,3,512]{2,0,1:T(8,128)(2,1)} async-done(((bf16[16,3,512]{2,0,1:T(8,128)(2,1)}), bf16[2048,3,512]{2,0,1:T(8,128)(2,1)}) %all-gather.3.cloned.1.call-update) | async-done | bytes 6291472 | tf_op jit(solution)/shard_map/all_gather | solution.py:131
  234.5 8.9 %copy.44 = bf16[2048,3,512]{0,2,1:T(8,128)(2,1)} copy(bf16[2048,3,512]{2,0,1:T(8,128)(2,1)} %all-gather.3.cloned.1.call-done) | data formatting | bytes 12582912 | tf_op jit(solution)/shard_map/all_gather | solution.py:131
  243.4 5.0 fusion.2
  248.4 4.3 collective-permute-start
  254.1 1.4 reduce
  256.1 14.0 %all-to-all-start = ((bf16[128,2,256]{2,1,0:T(2,128)(2,1)}), bf16[128,2,256]{2,1,0:T(2,128)(2,1)S(1)}, u32[]{:S(2)}, u32[]{:S(2)}) async-start(bf16[128,2,256]{2,1,0:T(2,128)(2,1)} %reshape.380), calls=%async_computation | async-start | bytes 262144 | tf_op jit(solution)/shard_map/all_to_all | solution.py:37
  271.8 9.7 %all-to-all-done = bf16[128,2,256]{2,1,0:T(2,128)(2,1)S(1)} async-done(((bf16[128,2,256]{2,1,0:T(2,128)(2,1)}), bf16[128,2,256]{2,1,0:T(2,128)(2,1)S(1)}, u32[]{:S(2)}, u32[]{:S(2)}) %all-to-all-start) | async-done | bytes 131104 | tf_op jit(solution)/shard_map/all_to_all | solution.py:37
  282.4 1.0 fusion.25
  283.5 1.3 copy.50
  284.8 6.3 %all-to-all-start.4 = ((bf16[2,256,1,512]{3,0,2,1:T(2,128)(2,1)}), bf16[2,256,1,512]{3,0,2,1:T(2,128)(2,1)S(1)}, u32[]{:S(2)}, u32[]{:S(2)}) async-start(bf16[2,256,1,512]{3,0,2,1:T(2,128)(2,1)} %copy.50), calls=%async_computation.4 | async-start | bytes 1048576 | tf_op jit(solution)/shard_map/all_to_all | solution.py:59
  291.2 1.3 copy.46
  292.6 17.4 %all-to-all-done.4 = bf16[2,256,1,512]{3,0,2,1:T(2,128)(2,1)S(1)} async-done(((bf16[2,256,1,512]{3,0,2,1:T(2,128)(2,1)}), bf16[2,256,1,512]{3,0,2,1:T(2,128)(2,1)S(1)}, u32[]{:S(2)}, u32[]{:S(2)}) %all-to-all-start.4) | async-done | bytes 524320 | tf_op jit(solution)/shard_map/all_to_all | solution.py:59
  310.0 7.3 %all-to-all-start.1 = ((bf16[2,256,1,512]{3,0,2,1:T(2,128)(2,1)}), bf16[2,256,1,512]{3,0,2,1:T(2,128)(2,1)S(1)}, u32[]{:S(2)}, u32[]{:S(2)}) async-start(bf16[2,256,1,512]{3,0,2,1:T(2,128)(2,1)} %copy.46), calls=%async_computation.1 | async-start | bytes 1048576 | tf_op jit(solution)/shard_map/all_to_all | solution.py:59
  320.4 1.1 copy.52
  321.5 14.5 %all-to-all-done.1 = bf16[2,256,1,512]{3,0,2,1:T(2,128)(2,1)S(1)} async-done(((bf16[2,256,1,512]{3,0,2,1:T(2,128)(2,1)}), bf16[2,256,1,512]{3,0,2,1:T(2,128)(2,1)S(1)}, u32[]{:S(2)}, u32[]{:S(2)}) %all-to-all-start.1) | async-done | bytes 524320 | tf_op jit(solution)/shard_map/all_to_all | solution.py:59
  336.0 7.4 %all-to-all-start.5 = ((bf16[2,2,128,512]{3,1,0,2:T(2,128)(2,1)}), bf16[2,2,128,512]{3,1,0,2:T(2,128)(2,1)S(1)}, u32[]{:S(2)}, u32[]{:S(2)}) async-start(bf16[2,2,128,512]{3,1,0,2:T(2,128)(2,1)} %copy.52), calls=%async_computation.5 | async-start | bytes 1048576 | tf_op jit(solution)/shard_map/all_to_all | solution.py:72
  346.6 1.1 copy.48
  347.8 14.5 %all-to-all-done.5 = bf16[2,2,128,512]{3,1,0,2:T(2,128)(2,1)S(1)} async-done(((bf16[2,2,128,512]{3,1,0,2:T(2,128)(2,1)}), bf16[2,2,128,512]{3,1,0,2:T(2,128)(2,1)S(1)}, u32[]{:S(2)}, u32[]{:S(2)}) %all-to-all-start.5) | async-done | bytes 524320 | tf_op jit(solution)/shard_map/all_to_all | solution.py:72
  362.3 7.3 %all-to-all-start.2 = ((bf16[2,2,128,512]{3,1,0,2:T(2,128)(2,1)}), bf16[2,2,128,512]{3,1,0,2:T(2,128)(2,1)S(1)}, u32[]{:S(2)}, u32[]{:S(2)}) async-start(bf16[2,2,128,512]{3,1,0,2:T(2,128)(2,1)} %copy.48), calls=%async_computation.2 | async-start | bytes 1048576 | tf_op jit(solution)/shard_map/all_to_all | solution.py:72
  369.9 18.4 %all-to-all-done.2 = bf16[2,2,128,512]{3,1,0,2:T(2,128)(2,1)S(1)} async-done(((bf16[2,2,128,512]{3,1,0,2:T(2,128)(2,1)}), bf16[2,2,128,512]{3,1,0,2:T(2,128)(2,1)S(1)}, u32[]{:S(2)}, u32[]{:S(2)}) %all-to-all-start.2) | async-done | bytes 524320 | tf_op jit(solution)/shard_map/all_to_all | solution.py:72
  388.7 1.1 subtract_convert_fusion.1
  390.1 1.3 copy.53
  391.4 7.2 %all-to-all-start.6 = ((bf16[2,256,1,512]{3,0,2,1:T(2,128)(2,1)}), bf16[2,256,1,512]{3,0,2,1:T(2,128)(2,1)S(1)}, u32[]{:S(2)}, u32[]{:S(2)}) async-start(bf16[2,256,1,512]{3,0,2,1:T(2,128)(2,1)} %copy.53), calls=%async_computation.6 | async-start | bytes 1048576 | tf_op jit(solution)/shard_map/all_to_all | solution.py:79
  399.6 17.9 %all-to-all-done.6 = bf16[2,256,1,512]{3,0,2,1:T(2,128)(2,1)S(1)} async-done(((bf16[2,256,1,512]{3,0,2,1:T(2,128)(2,1)}), bf16[2,256,1,512]{3,0,2,1:T(2,128)(2,1)S(1)}, u32[]{:S(2)}, u32[]{:S(2)}) %all-to-all-start.6) | async-done | bytes 524320 | tf_op jit(solution)/shard_map/all_to_all | solution.py:79
  421.3 25.6 %all_to_all.105 = bf16[2,2,128,512]{3,1,0,2:T(2,128)(2,1)S(1)} all-to-all(bf16[2,2,128,512]{3,1,0,2:T(2,128)(2,1)S(1)} %copy.55), channel_id=1, replica_groups=mesh['seq'=128,'tp'=4] {'seq'}, dimensions={2} | all-to-all | bytes 1048576 | tf_op jit(solution)/shard_map/all_to_all | solution.py:106
  449.7 18.4 %all_to_all.106 = bf16[128,2,256]{2,1,0:T(2,128)(2,1)S(1)} all-to-all(bf16[128,2,256]{2,1,0:T(2,128)(2,1)S(1)} %reshape.382), channel_id=1, replica_groups=mesh['seq'=128,'tp'=4] {'seq'}, dimensions={0} | all-to-all | bytes 262144 | tf_op jit(solution)/shard_map/all_to_all | solution.py:117
  468.2 17.3 %all_gather.14 = bf16[128,2048]{1,0:T(8,128)(2,1)S(1)} all-gather(bf16[128,512]{1,0:T(8,128)(2,1)S(1)} %fusion.32), channel_id=1, replica_groups=mesh['seq'=128,'tp'=4] {'tp'}, dimensions={1}, use_global_device_ids=true | all-gather | bytes 655360 | tf_op jit(solution)/shard_map/all_gather | solution.py:157
  485.5 133.2 %all-gather.5.cloned.1.call-done = bf16[2048,512]{1,0:T(8,128)(2,1)} async-done(((bf16[16,512]{1,0:T(8,128)(2,1)}), bf16[2048,512]{1,0:T(8,128)(2,1)}) %all-gather.5.cloned.1.call-update) | async-done | bytes 2097168 | tf_op jit(solution)/shard_map/all_gather | solution.py:158
  618.7 2.7 convolution_convert_fusion
  (66 shorter events, 23.4 us)
Async XLA Ops:
  6.5 228.0 %all-gather.3.cloned.1.call-start = ((), (), s32[]{:S(2)}) async-start(), calls=%async_computation.9 | async-start | bytes 6340608 | tf_op jit(solution)/shard_map/all_gather | solution.py:131
  11.1 241.7 %all-to-all-start.3 = ((bf16[128,2,256]{2,1,0:T(2,128)(2,1)}), bf16[128,2,256]{2,1,0:T(2,128)(2,1)S(1)}, u32[]{:S(2)}, u32[]{:S(2)}) async-start(bf16[128,2,256]{2,1,0:T(2,128)(2,1)} %reshape.378), calls=%async_computation.3 | async-start | bytes 262144 | tf_op jit(solution)/shard_map/all_to_all | solution.py:37
  46.5 196.9 %copy-start = (f32[2048]{0:T(1024)S(1)}, f32[2048]{0:T(1024)}, u32[]{:S(2)}) copy-start(f32[2048]{0:T(1024)} %param.8) | copy-start | bytes 24580
  248.4 5.0 collective-permute-start
  256.1 25.3 %all-to-all-start = ((bf16[128,2,256]{2,1,0:T(2,128)(2,1)}), bf16[128,2,256]{2,1,0:T(2,128)(2,1)S(1)}, u32[]{:S(2)}, u32[]{:S(2)}) async-start(bf16[128,2,256]{2,1,0:T(2,128)(2,1)} %reshape.380), calls=%async_computation | async-start | bytes 262144 | tf_op jit(solution)/shard_map/all_to_all | solution.py:37
  284.8 25.2 %all-to-all-start.4 = ((bf16[2,256,1,512]{3,0,2,1:T(2,128)(2,1)}), bf16[2,256,1,512]{3,0,2,1:T(2,128)(2,1)S(1)}, u32[]{:S(2)}, u32[]{:S(2)}) async-start(bf16[2,256,1,512]{3,0,2,1:T(2,128)(2,1)} %copy.50), calls=%async_computation.4 | async-start | bytes 1048576 | tf_op jit(solution)/shard_map/all_to_all | solution.py:59
  310.0 26.1 %all-to-all-start.1 = ((bf16[2,256,1,512]{3,0,2,1:T(2,128)(2,1)}), bf16[2,256,1,512]{3,0,2,1:T(2,128)(2,1)S(1)}, u32[]{:S(2)}, u32[]{:S(2)}) async-start(bf16[2,256,1,512]{3,0,2,1:T(2,128)(2,1)} %copy.46), calls=%async_computation.1 | async-start | bytes 1048576 | tf_op jit(solution)/shard_map/all_to_all | solution.py:59
  336.0 26.3 %all-to-all-start.5 = ((bf16[2,2,128,512]{3,1,0,2:T(2,128)(2,1)}), bf16[2,2,128,512]{3,1,0,2:T(2,128)(2,1)S(1)}, u32[]{:S(2)}, u32[]{:S(2)}) async-start(bf16[2,2,128,512]{3,1,0,2:T(2,128)(2,1)} %copy.52), calls=%async_computation.5 | async-start | bytes 1048576 | tf_op jit(solution)/shard_map/all_to_all | solution.py:72
  362.3 26.1 %all-to-all-start.2 = ((bf16[2,2,128,512]{3,1,0,2:T(2,128)(2,1)}), bf16[2,2,128,512]{3,1,0,2:T(2,128)(2,1)S(1)}, u32[]{:S(2)}, u32[]{:S(2)}) async-start(bf16[2,2,128,512]{3,1,0,2:T(2,128)(2,1)} %copy.48), calls=%async_computation.2 | async-start | bytes 1048576 | tf_op jit(solution)/shard_map/all_to_all | solution.py:72
  391.4 26.1 %all-to-all-start.6 = ((bf16[2,256,1,512]{3,0,2,1:T(2,128)(2,1)}), bf16[2,256,1,512]{3,0,2,1:T(2,128)(2,1)S(1)}, u32[]{:S(2)}, u32[]{:S(2)}) async-start(bf16[2,256,1,512]{3,0,2,1:T(2,128)(2,1)} %copy.53), calls=%async_computation.6 | async-start | bytes 1048576 | tf_op jit(solution)/shard_map/all_to_all | solution.py:79
  398.7 220.0 %all-gather.5.cloned.1.call-start = ((), (), s32[]{:S(2)}) async-start(), calls=%async_computation.10 | async-start | bytes 2113536 | tf_op jit(solution)/shard_map/all_gather | solution.py:158
  418.0 50.1 %copy-start.1 = (f32[512]{0:T(512)S(1)}, f32[512]{0:T(512)}, u32[]{:S(2)}) copy-start(f32[512]{0:T(512)} %param.12) | copy-start | bytes 6148
Sparse Core Ops, SparseCore 0:
  9.5 224.9 all-gather.2
  401.7 216.9 all-gather.4
where the time goes:
time: 637 us; the launch traced here: 628 us
  waiting for transfers between devices  416 us (65%)
  blocking collectives  81.5 us (13%)
  starting transfers between devices  68.3 us (11%)
  local copies, waits for them, and re-layouts  21.5 us (3%)
  matrix products  20.2 us (3%)
  between operations  14.1 us (2%)
  other arithmetic  7.34 us (1%)
    all_gather x1, waiting for transfers between devices, shards(): weight_piece = lax.all_gather(in_weight, 'seq', axis=0, tiled=True)  188 us
    all_gather x1, waiting for transfers between devices, shards(): weight_piece = lax.all_gather(out_weight, 'seq', axis=0, tiled=True)  133 us
    all_to_all x2, waiting for transfers between devices, forward_transform(): lax.all_to_all(for_sending(result), 'seq', split_axis=2, concat_axis=1, t...  33 us
    all_to_all x2, waiting for transfers between devices, forward_transform(): lax.all_to_all(for_sending(turned), 'seq', split_axis=1, concat_axis=2, t...  31.9 us
    all_to_all x2, starting transfers between devices, forward_transform(): lax.all_to_all(series[None].astype(jnp.bfloat16), 'seq', split_axis=1, co...  28.2 us
    all_to_all x1, blocking collectives, inverse_transform(): lax.all_to_all(for_sending(turned), 'seq', split_axis=2, concat_axis=1, t...  25.6 us
    all_gather x1, blocking collectives, shards(): lax.all_gather(tokens, 'tp', axis=1, tiled=True).astype(jnp.float32)  20.2 us
    all_to_all x1, blocking collectives, inverse_transform(): lax.all_to_all(for_sending(series), 'seq', split_axis=0, concat_axis=1, t...  18.4 us
  transfers between devices with their start and end apart: 10, of which 9 were waited for; matrix products, arithmetic and copies ran while one was open for 6% of the time, Pallas kernels for 0%

commit v1 on v0

v1 whole, which is shorter than its diff:
```python
import functools
import math

import jax
import jax.numpy as jnp
import numpy as np
from jax import lax
from jax.experimental import pallas as pl
from jax.experimental.pallas import tpu as pltpu
from jax.sharding import Mesh
from jax.sharding import PartitionSpec as P

F32 = jnp.float32
BF16 = jnp.bfloat16
LANES = 128
HALO = 16
OUTER = ("y", "x")
INNER = ("zl", "co")
SEQ = OUTER + INNER


def call(body, out_shape, *args, limit=48):
    return pl.pallas_call(
        body,
        out_shape=out_shape,
        compiler_params=pltpu.CompilerParams(vmem_limit_bytes=limit * 1024 * 1024),
    )(*args)


def transform_tables(length, chans, outer, inner):
    blocks = length // LANES
    row = np.arange(blocks)
    lane = np.arange(LANES)
    far = np.exp(-2j * np.pi * (row[:, None] * (4 * row[None, :] + 1) % (4 * blocks)) / (4 * blocks))
    near = np.exp(-2j * np.pi * (lane[:, None] * lane[None, :] % LANES) / LANES)
    turn = np.exp(-2j * np.pi * ((4 * row[:, None] + 1) * lane[None, :] % (4 * length)) / (4 * length))
    eye = np.eye(chans)
    into = np.einsum("bf,cd->cfbd", far, eye).reshape(chans * blocks, blocks * chans)
    into = np.concatenate([into.real, into.imag], axis=0)
    back = np.einsum("bf,cd->bdcf", far.conj(), eye).reshape(blocks * chans, chans * blocks) / length
    back = np.concatenate([back.real, -back.imag], axis=1)
    near_in = np.block([[near.real, near.imag], [-near.imag, near.real]])
    near_out = np.block([[near.real, -near.imag], [near.imag, near.real]])
    turn = np.stack([np.tile(turn.real, (chans, 1)), np.tile(turn.imag, (chans, 1))])
    as_short = lambda table: jnp.asarray(table.astype(np.float32)).astype(BF16)
    return {
        "into": as_short(into),
        "back": as_short(back),
        "near_in": as_short(near_in),
        "near_out": as_short(near_out),
        "turn": jnp.asarray(turn.astype(np.float32)),
    }


def forward_points(block, into, near_in, turn):
    half = into.shape[0] // 2
    far = jnp.dot(into, block, preferred_element_type=F32)
    real, imag = far[:half], far[half:]
    cos, sin = turn[0], turn[1]
    pair = jnp.concatenate([real * cos - imag * sin, real * sin + imag * cos], axis=1)
    return jnp.dot(pair.astype(BF16), near_in, preferred_element_type=F32)


def filter_body(taps_ref, into_ref, near_ref, turn_ref, out_ref):
    out_ref[...] = forward_points(taps_ref[...], into_ref[...], near_ref[...], turn_ref[...])


def conv_body(sig_ref, spec_ref, into_ref, near_in_ref, turn_ref, near_out_ref, back_ref, out_ref):
    groups, rows, lanes = sig_ref.shape
    block = sig_ref[...].reshape(groups * rows, lanes)
    turn = turn_ref[...]
    points = forward_points(block, into_ref[...], near_in_ref[...], turn)
    spec = spec_ref[...]
    real, imag = points[:, :lanes], points[:, lanes:]
    sreal, simag = spec[:, :lanes], spec[:, lanes:]
    pair = jnp.concatenate([real * sreal - imag * simag, real * simag + imag * sreal], axis=1)
    near = jnp.dot(pair.astype(BF16), near_out_ref[...], preferred_element_type=F32)
    real, imag = near[:, :lanes], near[:, lanes:]
    cos, sin = turn[0], turn[1]
    stacked = jnp.concatenate([real * cos + imag * sin, imag * cos - real * sin], axis=0)
    result = jnp.dot(back_ref[...], stacked.astype(BF16), preferred_element_type=F32)
    out_ref[...] = result.astype(BF16).reshape(groups, rows, lanes)


def norm_body(tok_ref, halo_ref, gain_ref, out_ref):
    inner, tp, length, feats = tok_ref.shape
    width = tp * feats

    def put(parts, at, rows):
        total = sum(jnp.sum(part * part, axis=1, keepdims=True) for part in parts)
        scale = lax.rsqrt(total / width + 1e-05)
        for p, part in enumerate(parts):
            gain = gain_ref[:, p * feats : (p + 1) * feats]
            out_ref[at : at + rows, p * feats : (p + 1) * feats] = (part * scale * gain).astype(BF16)

    put([halo_ref[p].astype(F32) for p in range(tp)], 0, HALO)
    for s in range(inner):
        put([tok_ref[s, p].astype(F32) for p in range(tp)], HALO + s * length, length)


def project_body(x_ref, w_ref, taps_ref, query_ref, signal_ref, send_ref):
    _, parts, _, chans = w_ref.shape
    depth = x_ref.shape[1]
    groups, rows, lanes = send_ref.shape
    inner = query_ref.shape[0] // lanes
    per = rows // inner
    weight = jnp.concatenate([w_ref[:, s].reshape(depth, chans) for s in range(parts)], axis=1)
    proj = jnp.dot(x_ref[...], weight, preferred_element_type=F32).astype(BF16).astype(F32)
    short = taps_ref[0:1] * proj
    for lag in range(1, taps_ref.shape[0]):
        short = short + taps_ref[lag : lag + 1] * pltpu.roll(proj, lag, 0)
    short = short[HALO:]
    query_ref[...] = short[:, :chans]
    signal = short[:, chans : 2 * chans] * short[:, 2 * chans :]
    signal_ref[...] = signal
    pieces = [signal[b * lanes : (b + 1) * lanes].T.reshape(groups, per, lanes) for b in range(inner)]
    send_ref[...] = jnp.concatenate(pieces, axis=1).astype(BF16)


def gate_body(conv_ref, query_ref, signal_ref, skip_ref, out_ref):
    groups, rows, lanes = conv_ref.shape
    inner = query_ref.shape[0] // lanes
    per = rows // inner
    conv = conv_ref[...].astype(F32)
    for b in range(inner):
        piece = conv[:, b * per : (b + 1) * per].reshape(groups * per, lanes).T
        at = slice(b * lanes, (b + 1) * lanes)
        mixed = piece + skip_ref[...] * signal_ref[at]
        out_ref[at] = (query_ref[at] * mixed).astype(BF16)


def out_body(gated_ref, w_ref, out_ref):
    inner, tp, rows, chans = gated_ref.shape
    x = jnp.concatenate([gated_ref[s, p] for p in range(tp) for s in range(inner)], axis=1)
    out_ref[...] = jnp.dot(x, w_ref[...], preferred_element_type=F32).astype(BF16)


def shape(dims, dtype):
    return jax.ShapeDtypeStruct(dims, dtype)


def shards(ways, tables, tokens, norm_gain, in_weight, short_taps, filter_response, skip_gain, out_weight):
    outer = ways["y"] * ways["x"]
    inner = ways["zl"] * ways["co"]
    tp = ways["tp"]
    length, feats = tokens.shape
    chans = skip_gain.shape[0] // inner
    per = chans // outer
    depth, parts = in_weight.shape[0], in_weight.shape[1]
    rows = inner * per
    place = lax.axis_index(INNER)

    with jax.named_scope("weight_gather"):
        split = in_weight.reshape(depth, parts, inner, chans).transpose(2, 1, 0, 3)
        swapped = lax.all_to_all(split, INNER, 0, 0)
        weight = lax.all_gather(swapped, OUTER, axis=0)
        weight = weight.reshape(outer * inner, parts, depth, chans)
    with jax.named_scope("token_gather"):
        tok = lax.all_gather(tokens, INNER + ("tp",), axis=0).reshape(inner, tp, length, feats)
        halo = lax.ppermute(
            tok[inner - 1, :, length - HALO :], OUTER, [(i, i + 1) for i in range(outer - 1)]
        )
    with jax.named_scope("filter_points"):
        taps = filter_response.astype(BF16).T.reshape(inner, outer, per, length)
        taps = taps.transpose(1, 0, 2, 3).reshape(outer * inner, per, length)
        taps = lax.all_to_all(taps, SEQ, 0, 0).reshape(outer * inner * per, length)
        spec = call(
            filter_body,
            shape((per * outer * inner, 2 * LANES), F32),
            taps,
            tables["into"],
            tables["near_in"],
            tables["turn"],
        )
    with jax.named_scope("out_weight_gather"):
        out_w = lax.all_to_all(
            jnp.broadcast_to(out_weight[None], (outer * inner,) + out_weight.shape), SEQ, 0, 0
        ).reshape(outer * inner * out_weight.shape[0], out_weight.shape[1])
    with jax.named_scope("norm"):
        x = call(
            norm_body,
            shape((HALO + inner * length, tp * feats), BF16),
            tok,
            halo,
            norm_gain.reshape(1, tp * feats),
        )
    with jax.named_scope("project"):
        own_taps = lax.dynamic_slice_in_dim(short_taps, place * chans, chans, 2)
        query, signal, send = call(
            project_body,
            (
                shape((inner * length, chans), F32),
                shape((inner * length, chans), F32),
                shape((outer, rows, LANES), BF16),
            ),
            x,
            weight,
            own_taps.reshape(short_taps.shape[0], parts * chans),
        )
    with jax.named_scope("conv"):
        blocks = lax.all_to_all(send, OUTER, 0, 0)
        conv = call(
            conv_body,
            shape((outer, rows, LANES), BF16),
            blocks,
            spec,
            tables["into"],
            tables["near_in"],
            tables["turn"],
            tables["near_out"],
            tables["back"],
        )
        conv = lax.all_to_all(conv, OUTER, 0, 0)
    with jax.named_scope("gate"):
        own_skip = lax.dynamic_slice_in_dim(skip_gain, place * chans, chans, 0)
        gated = call(
            gate_body,
            shape((inner * length, chans), BF16),
            conv,
            query,
            signal,
            own_skip.reshape(1, chans),
        )
    with jax.named_scope("gated_gather"):
        gated = jnp.broadcast_to(
            gated.reshape(inner, 1, length, chans), (inner, tp, length, chans)
        ).reshape(inner * tp, length, chans)
        gated = lax.all_to_all(gated, INNER + ("tp",), 0, 0).reshape(inner, tp, length, chans)
    with jax.named_scope("out_project"):
        return call(out_body, shape((length, out_w.shape[1]), BF16), gated, out_w)


def solution(mesh):
    seq, tp = mesh.shape["seq"], mesh.shape["tp"]
    ways = {"y": seq // 16, "x": 4, "zl": 2, "co": 2, "tp": tp}
    fine = Mesh(mesh.devices.reshape(tuple(ways.values())), tuple(ways))
    placed = (
        P(SEQ, "tp"),
        P(),
        P(SEQ, None, "tp"),
        P(None, None, "tp"),
        P(SEQ, "tp"),
        P("tp"),
        P(SEQ, "tp"),
    )

    def run(*args):
        tokens, skip = args[0], args[5]
        inner = ways["zl"] * ways["co"]
        per = skip.shape[0] // (tp * seq)
        tables = transform_tables(tokens.shape[0], per, seq // inner, inner)
        body = functools.partial(shards, ways, tables)
        return jax.shard_map(
            body, mesh=fine, in_specs=placed, out_specs=P(SEQ, "tp"), check_vma=False
        )(*args)

    return run
```

time: 637 us -> 315 us (0.49); the launches traced: 628 us -> 314 us
  waiting for transfers between devices: 416 us -> 200 us
  starting transfers between devices: 68.3 us -> 28.6 us
  blocking collectives: 81.5 us -> 51.5 us
  matrix products: 20.2 us -> 0 us
  other arithmetic: 7.34 us -> 0 us
    all_gather x2, waiting for transfers between devices: 321 us -> 141 us  [the longest x1 74.3 us: shards(): weight = lax.all_gather(swapped, OUTER, axis=0)]
    all_gather x2 -> x0, blocking collectives: 37.5 us -> none  [the longest x1 20.2 us: shards(): lax.all_gather(tokens, 'tp', axis=1, tiled=True).astype(jnp.float32)]
    all_to_all x7 -> x3, starting transfers between devices: 63.7 us -> 26.3 us  [the longest x1 13.7 us: shards(): lax.all_to_all(jnp.broadcast_to(out_weight[None], (outer * inner,) + out_...]
    all_to_all x7 -> x3, waiting for transfers between devices: 92.5 us -> 57 us  [the longest x1 49.3 us: shards(): lax.all_to_all(jnp.broadcast_to(out_weight[None], (outer * inner,) + out_...]
    dot_general x20 -> x0, matrix products: 20.2 us -> none  [the longest x1 5 us: shards(): summed = jnp.dot(columns, flat_piece, preferred_element_type=jnp.float32)]
    all_gather x1 -> x0, local copies, waits for them, and re-layouts: 8.87 us -> none  [shards(): weight_piece = lax.all_gather(in_weight, 'seq', axis=0, tiled=True)]
    unnamed x11 -> x35, local copies, waits for them, and re-layouts: 2.29 us -> 10.2 us
    all_to_all x2 -> x3, blocking collectives: 44 us -> 51.5 us  [the longest x1 26 us: shards(): lax.all_to_all(gated, INNER + ('tp',), 0, 0)]
  transfers between devices with their start and end apart: 10 -> 6, of which waited for: 9 -> 5; matrix products, arithmetic and copies ran while one was open for 6% -> 1% of each run, Pallas kernels for 0% -> 1%
where the time goes in v1:
time: 315 us; the launch traced here: 314 us
  waiting for transfers between devices  200 us (63%)
  blocking collectives  51.5 us (16%)
  starting transfers between devices  28.6 us (9%)
  local copies, waits for them, and re-layouts  15.2 us (5%)
  between operations  13.6 us (4%)
  Pallas kernels  5.71 us (2%)
    all_gather x1, waiting for transfers between devices, shards(): weight = lax.all_gather(swapped, OUTER, axis=0)  74.3 us
    all_gather x1, waiting for transfers between devices, shards(): lax.all_gather(tokens, INNER + ('tp',), axis=0)  66.5 us
    all_to_all x1, waiting for transfers between devices, shards(): lax.all_to_all(jnp.broadcast_to(out_weight[None], (outer * inner,) + out_...  49.3 us
    all_to_all x1, blocking collectives, shards(): lax.all_to_all(gated, INNER + ('tp',), 0, 0)  26 us
    all_to_all x1, starting transfers between devices, shards(): lax.all_to_all(jnp.broadcast_to(out_weight[None], (outer * inner,) + out_...  13.7 us
    all_to_all x1, blocking collectives, shards(): swapped = lax.all_to_all(split, INNER, 0, 0)  13.1 us
    all_to_all x1, blocking collectives, shards(): conv = lax.all_to_all(conv, OUTER, 0, 0)  12.4 us
    unnamed x35, local copies, waits for them, and re-layouts  10.2 us
  transfers between devices with their start and end apart: 6, of which 5 were waited for; matrix products, arithmetic and copies ran while one was open for 1% of the time, Pallas kernels for 1%

profile of v1, /device:TPU:1, one launch (start us, length us, event | category | flops | bytes accessed | tf_op | source)
XLA Modules:
  0.0 314.4 jit_solution(10506895864283076383)
XLA Ops:
  6.5 0.7 all-gather.5.cloned.1.call-update
  7.3 0.8 reshape.41
  8.1 13.1 %all_to_all.30 = bf16[4,3,16,128]{3,2,1,0:T(8,128)(2,1)} all-to-all(bf16[4,3,16,128]{3,2,1,0:T(8,128)(2,1)S(1)} %copy.24), channel_id=1, replica_groups=mesh['y'=8,'x'=4,'zl'=2,'co'=2,'tp'=4] {'zl','co'}, dimensions={0} | all-to-all | bytes 98304 | tf_op jit(solution)/shard_map/weight_gather/all_to_all | solution.py:155
  21.3 1.1 copy.25
  22.5 0.8 copy.27
  23.2 6.9 %all-to-all-start.2 = ((bf16[128,4,128]{2,1,0:T(4,128)(2,1)}), bf16[128,4,128]{2,1,0:T(4,128)(2,1)S(1)}, u32[]{:S(2)}, u32[]{:S(2)}) async-start(bf16[128,4,128]{2,1,0:T(4,128)(2,1)} %copy.27), calls=%async_computation.2 | async-start | bytes 262144 | tf_op jit(solution)/shard_map/filter_points/all_to_all | solution.py:166
  30.1 66.5 %all-gather.5.cloned.1.call-done = bf16[2048,512]{1,0:T(8,128)(2,1)} async-done(((bf16[128,512]{1,0:T(8,128)(2,1)}), bf16[2048,512]{1,0:T(8,128)(2,1)}) %all-gather.5.cloned.1.call-update) | async-done | bytes 2097168 | tf_op jit(solution)/shard_map/token_gather/all_gather | solution.py:159
  96.6 0.8 slice_bitcast_fusion
  97.5 2.3 collective-permute-start
  99.8 1.3 collective-permute-done.halo_ref
  101.1 1.6 copy-done.2
  102.7 0.7 copy-done.14
  103.4 0.8 norm.1.x_ref
  104.2 74.3 %all-gather.7.cloned.1.call-done.w_ref = bf16[128,3,16,128]{3,2,1,0:T(8,128)(2,1)} async-done(((bf16[4,3,16,128]{3,2,1,0:T(8,128)(2,1)}), bf16[128,3,16,128]{3,2,1,0:T(8,128)(2,1)}) %all-gather.7.cloned.1.call-update) | async-done | bytes 1572880 | tf_op jit(solution)/shard_map/weight_gather/all_gather | solution.py:156
  178.5 1.4 copy-done.5
  179.9 1.5 project.1
  181.5 0.7 copy-done.8
  182.2 0.7 copy-done.10
  182.9 0.7 copy-done.13
  183.5 5.7 %all-to-all-start.1 = ((bf16[32,16,128]{2,1,0:T(8,128)(2,1)}), bf16[32,16,128]{2,1,0:T(8,128)(2,1)S(1)}, u32[]{:S(2)}, u32[]{:S(2)}) async-start(bf16[32,16,128]{2,1,0:T(8,128)(2,1)} %copy-done.13), calls=%async_computation.1 | async-start | bytes 262144 | tf_op jit(solution)/shard_map/conv/all_to_all | solution.py:201
  189.3 1.0 copy-done.3
  190.9 7.7 %all-to-all-done.1.sig_ref = bf16[32,16,128]{2,1,0:T(8,128)(2,1)S(1)} async-done(((bf16[32,16,128]{2,1,0:T(8,128)(2,1)}), bf16[32,16,128]{2,1,0:T(8,128)(2,1)S(1)}, u32[]{:S(2)}, u32[]{:S(2)}) %all-to-all-start.1) | async-done | bytes 131104 | tf_op jit(solution)/shard_map/conv/all_to_all | solution.py:201
  198.6 1.0 copy-done.4
  199.6 1.2 copy-done.6
  200.9 1.5 conv.1
  202.4 12.4 %all_to_all.31.conv_ref = bf16[32,16,128]{2,1,0:T(8,128)(2,1)S(1)} all-to-all(bf16[32,16,128]{2,1,0:T(8,128)(2,1)S(1)} %conv.1), channel_id=1, replica_groups=mesh['y'=8,'x'=4,'zl'=2,'co'=2,'tp'=4] {'y','x'}, dimensions={0} | all-to-all | bytes 262144 | tf_op jit(solution)/shard_map/conv/all_to_all | solution.py:213
  214.8 1.6 broadcast_in_dim.15
  216.4 13.7 %all-to-all-start.5 = ((bf16[128,16,512]{2,1,0:T(8,128)(2,1)}), bf16[128,16,512]{2,1,0:T(8,128)(2,1)S(1)}, u32[]{:S(2)}, u32[]{:S(2)}) async-start(bf16[128,16,512]{2,1,0:T(8,128)(2,1)} %broadcast_in_dim.15), calls=%async_computation.5 | async-start | bytes 4194304 | tf_op jit(solution)/shard_map/out_weight_gather/all_to_all | solution.py:176
  230.1 0.8 dynamic-slice_bitcast_fusion.1.skip_ref
  231.0 49.3 %all-to-all-done.5 = bf16[128,16,512]{2,1,0:T(8,128)(2,1)S(1)} async-done(((bf16[128,16,512]{2,1,0:T(8,128)(2,1)}), bf16[128,16,512]{2,1,0:T(8,128)(2,1)S(1)}, u32[]{:S(2)}, u32[]{:S(2)}) %all-to-all-start.5) | async-done | bytes 2097184 | tf_op jit(solution)/shard_map/out_weight_gather/all_to_all | solution.py:176
  280.4 26.0 %all_to_all.32 = bf16[16,128,128]{2,1,0:T(8,128)(2,1)S(1)} all-to-all(bf16[16,128,128]{2,1,0:T(8,128)(2,1)S(1)} %bitcast.33), channel_id=1, replica_groups=mesh['y'=8,'x'=4,'zl'=2,'co'=2,'tp'=4] {'zl','co','tp'}, dimensions={0} | all-to-all | bytes 1048576 | tf_op jit(solution)/shard_map/gated_gather/all_to_all | solution.py:228
  306.4 1.1 out_project.1
  (34 shorter events, 1.1 us)
Async XLA Ops:
  6.5 93.3 %copy-start = (f32[3,3,512]{2,1,0:T(4,128)S(1)}, f32[3,3,512]{2,1,0:T(4,128)}, u32[]{:S(2)}) copy-start(f32[3,3,512]{2,1,0:T(4,128)} %param.15) | copy-start | bytes 55300
  6.5 90.1 %all-gather.5.cloned.1.call-start = ((), (), s32[]{:S(2)}) async-start(), calls=%async_computation.6 | async-start | bytes 2228224 | tf_op jit(solution)/shard_map/token_gather/all_gather | solution.py:159
  7.3 171.3 %all-gather.7.cloned.1.call-start = ((), (), s32[]{:S(2)}) async-start(), calls=%async_computation.7 | async-start | bytes 1622016 | tf_op jit(solution)/shard_map/weight_gather/all_gather | solution.py:156
  23.2 160.3 %all-to-all-start.2 = ((bf16[128,4,128]{2,1,0:T(4,128)(2,1)}), bf16[128,4,128]{2,1,0:T(4,128)(2,1)S(1)}, u32[]{:S(2)}, u32[]{:S(2)}) async-start(bf16[128,4,128]{2,1,0:T(4,128)(2,1)} %copy.27), calls=%async_computation.2 | async-start | bytes 262144 | tf_op jit(solution)/shard_map/filter_points/all_to_all | solution.py:166
  97.5 3.6 %collective-permute-start = (bf16[4,16,512]{2,1,0:T(8,128)(2,1)S(1)}, bf16[4,16,512]{2,1,0:T(8,128)(2,1)S(1)}, u32[]{:S(2)}, u32[]{:S(2)}) collective-permute-start(bf16[4,16,512]{2,1,0:T(8,128)(2,1)S(1)} %slice_bitcast_fusion), channel_id=1, source_target_pairs={{0,16},{16,32},{32,48},{48,64},{64,80},{80,96},{96,112},{112,128},... | collective-permute-start | bytes 196616 | tf_op jit(solution)/shard_map/token_gather/ppermute | solution.py:160
  101.1 1.6 copy-start.2
  102.7 0.7 copy-start.14
  103.4 85.8 %copy-start.7 = (bf16[256,256]{1,0:T(8,128)(2,1)S(1)}, bf16[256,256]{1,0:T(8,128)(2,1)}, u32[]{:S(2)}) copy-start(bf16[256,256]{1,0:T(8,128)(2,1)} %constant.31.clone.near_ref.near_in_ref) | copy-start | bytes 393220
  104.2 85.0 %copy-start.1 = (bf16[1024,512]{1,0:T(8,128)(2,1)S(1)}, bf16[1024,512]{1,0:T(8,128)(2,1)}, u32[]{:S(2)}) copy-start(bf16[1024,512]{1,0:T(8,128)(2,1)} %constant.30.clone.into_ref) | copy-start | bytes 3145732
  178.5 1.4 copy-start.5
  181.5 0.7 copy-start.8
  182.2 0.7 copy-start.10
  182.9 0.7 copy-start.13
  183.5 15.1 %copy-start.12 = (bf16[256,256]{1,0:T(8,128)(2,1)S(1)}, bf16[256,256]{1,0:T(8,128)(2,1)}, u32[]{:S(2)}) copy-start(bf16[256,256]{1,0:T(8,128)(2,1)} %constant.33.clone.near_out_ref) | copy-start | bytes 393220
  183.5 15.0 %all-to-all-start.1 = ((bf16[32,16,128]{2,1,0:T(8,128)(2,1)}), bf16[32,16,128]{2,1,0:T(8,128)(2,1)S(1)}, u32[]{:S(2)}, u32[]{:S(2)}) async-start(bf16[32,16,128]{2,1,0:T(8,128)(2,1)} %copy-done.13), calls=%async_computation.1 | async-start | bytes 262144 | tf_op jit(solution)/shard_map/conv/all_to_all | solution.py:201
  189.3 1.0 copy-start.3
  198.6 1.0 copy-start.4
  199.6 1.2 copy-start.6
  200.9 13.9 %copy-start.15 = (bf16[16,512]{1,0:T(8,128)(2,1)S(1)}, bf16[16,512]{1,0:T(8,128)(2,1)}, u32[]{:S(2)}) copy-start(bf16[16,512]{1,0:T(8,128)(2,1)} %param.18) | copy-start | bytes 49156
  216.4 14.5 %copy-start.9 = (f32[512,128]{1,0:T(8,128)S(1)}, f32[512,128]{1,0:T(8,128)}, u32[]{:S(2)}) copy-start(f32[512,128]{1,0:T(8,128)} %copy-done.8) | copy-start | bytes 786436
  216.4 14.5 %copy-start.11 = (f32[512,128]{1,0:T(8,128)S(1)}, f32[512,128]{1,0:T(8,128)}, u32[]{:S(2)}) copy-start(f32[512,128]{1,0:T(8,128)} %copy-done.10) | copy-start | bytes 786436
  216.4 63.9 %all-to-all-start.5 = ((bf16[128,16,512]{2,1,0:T(8,128)(2,1)}), bf16[128,16,512]{2,1,0:T(8,128)(2,1)S(1)}, u32[]{:S(2)}, u32[]{:S(2)}) async-start(bf16[128,16,512]{2,1,0:T(8,128)(2,1)} %broadcast_in_dim.15), calls=%async_computation.5 | async-start | bytes 4194304 | tf_op jit(solution)/shard_map/out_weight_gather/all_to_all | solution.py:176
Sparse Core Ops, SparseCore 0:
  9.4 87.1 all-gather.4
  99.8 78.6 all-gather.6

commit v2 on v1

--- a/solution.py
+++ b/solution.py
@@ -19,11 +19,15 @@
 SEQ = OUTER + INNER
 
 
-def call(body, out_shape, *args, limit=48):
+def call(body, out_shape, *args, scalars=0, scratch=()):
+    specs = [pl.BlockSpec(memory_space=pltpu.SMEM)] * scalars
+    specs += [pl.BlockSpec(memory_space=pltpu.VMEM)] * (len(args) - scalars)
     return pl.pallas_call(
         body,
         out_shape=out_shape,
-        compiler_params=pltpu.CompilerParams(vmem_limit_bytes=limit * 1024 * 1024),
+        in_specs=specs,
+        scratch_shapes=scratch,
+        compiler_params=pltpu.CompilerParams(vmem_limit_bytes=20 * 1024 * 1024),
     )(*args)
 
 
@@ -82,34 +86,118 @@
     out_ref[...] = result.astype(BF16).reshape(groups, rows, lanes)
 
 
-def norm_body(tok_ref, halo_ref, gain_ref, out_ref):
-    inner, tp, length, feats = tok_ref.shape
-    width = tp * feats
-
-    def put(parts, at, rows):
-        total = sum(jnp.sum(part * part, axis=1, keepdims=True) for part in parts)
-        scale = lax.rsqrt(total / width + 1e-05)
-        for p, part in enumerate(parts):
-            gain = gain_ref[:, p * feats : (p + 1) * feats]
-            out_ref[at : at + rows, p * feats : (p + 1) * feats] = (part * scale * gain).astype(BF16)
-
-    put([halo_ref[p].astype(F32) for p in range(tp)], 0, HALO)
+def pack_body(weight_ref, out_w_ref, taps_ref, send_ref):
+    parts = weight_ref.shape[0]
+    lanes = send_ref.shape[3]
+    inner = out_w_ref.shape[1] // lanes
+    ways = send_ref.shape[0] // inner
+    rows = send_ref.shape[2]
     for s in range(inner):
-        put([tok_ref[s, p].astype(F32) for p in range(tp)], HALO + s * length, length)
-
-
-def project_body(x_ref, w_ref, taps_ref, query_ref, signal_ref, send_ref):
-    _, parts, _, chans = w_ref.shape
-    depth = x_ref.shape[1]
-    groups, rows, lanes = send_ref.shape
+        at = slice(s * lanes, (s + 1) * lanes)
+        taps = taps_ref[:, at].T.reshape(ways, rows, lanes).astype(BF16)
+        for way in range(ways):
+            to = way * inner + s
+            for part in range(parts):
+                send_ref[to, part] = weight_ref[part, :, at]
+            send_ref[to, parts] = out_w_ref[:, at]
+            send_ref[to, parts + 1] = taps[way]
+
+
+def repack_body(got_ref, send_ref):
+    sources, kinds, rows, lanes = got_ref.shape
+    ways, tiles = send_ref.shape[0], send_ref.shape[1]
+    parts = kinds - 1
+    taps = got_ref[:, parts].astype(F32)
+    per = rows // ways
+    for way in range(ways):
+        for part in range(parts):
+            send_ref[way, part * sources : (part + 1) * sources] = got_ref[:, part]
+        piece = taps[:, way * per : (way + 1) * per].reshape(tiles - parts * sources, rows, lanes)
+        send_ref[way, parts * sources :] = piece.astype(BF16)
+
+
+def scaled(parts, gain_ref):
+    width = gain_ref.shape[1]
+    total = sum(jnp.sum(part * part, axis=1, keepdims=True) for part in parts)
+    scale = lax.rsqrt(total / width + 1e-05)
+    feats = width // len(parts)
+    return [
+        (part * scale * gain_ref[:, p * feats : (p + 1) * feats]).astype(BF16)
+        for p, part in enumerate(parts)
+    ]
+
+
+def norm_body(tok_ref, gain_ref, out_ref):
+    count, length, feats = tok_ref.shape
+    tp = out_ref.shape[1] // feats
+    for block in range(count // tp):
+        parts = [tok_ref[block * tp + p].astype(F32) for p in range(tp)]
+        for p, part in enumerate(scaled(parts, gain_ref)):
+            out_ref[block * length : (block + 1) * length, p * feats : (p + 1) * feats] = part
+
+
+def project_body(
+    cores,
+    core_ref,
+    own_ref,
+    other_ref,
+    halo_own_ref,
+    halo_other_ref,
+    gain_ref,
+    got_ref,
+    taps_ref,
+    query_ref,
+    signal_ref,
+    send_ref,
+    out_w_ref,
+    filter_ref,
+    proj_ref,
+):
+    core = core_ref[0, 0]
+    parts = 3
+    ways, tiles, rows, lanes = got_ref.shape
+    groups = send_ref.shape[0]
+    outer = groups // ways
     inner = query_ref.shape[0] // lanes
-    per = rows // inner
-    weight = jnp.concatenate([w_ref[:, s].reshape(depth, chans) for s in range(parts)], axis=1)
-    proj = jnp.dot(x_ref[...], weight, preferred_element_type=F32).astype(BF16).astype(F32)
-    short = taps_ref[0:1] * proj
+    chans = query_ref.shape[1]
+    per = send_ref.shape[1] // inner
+    sources = outer * inner
+
+    def column(part):
+        pieces = [
+            got_ref[x, part * sources + y * inner : part * sources + (y + 1) * inner].reshape(
+                inner * rows, lanes
+            )
+            for y in range(outer)
+            for x in range(ways)
+        ]
+        return jnp.concatenate(pieces, axis=0)
+
+    weight = jnp.concatenate([column(part) for part in range(parts)], axis=1)
+    out_w_ref[...] = column(parts)
+    first = (parts + 1) * sources
+    for y in range(outer):
+        for x in range(ways):
+            at = (y * ways + x) * rows
+            filter_ref[at : at + rows] = got_ref[x, first + y]
+
+    def project(block):
+        got = jnp.dot(block, weight, preferred_element_type=F32)
+        return got.astype(BF16).astype(F32)
+
+    halo = jnp.where(core == cores - 1, halo_own_ref[...].astype(F32), halo_other_ref[...].astype(F32))
+    halo = scaled([halo[p] for p in range(halo.shape[0])], gain_ref)
+    proj_ref[:HALO] = project(jnp.concatenate(halo, axis=1))
+    for ref, at_core in ((own_ref, core), (other_ref, 1 - core)):
+        got = project(ref[...])
+        for z in range(inner // cores):
+            at = pl.multiple_of(HALO + (z * cores + at_core) * lanes, HALO)
+            proj_ref[pl.ds(at, lanes)] = got[z * lanes : (z + 1) * lanes]
+
+    count = query_ref.shape[0]
+    short = taps_ref[0:1] * proj_ref[HALO:]
     for lag in range(1, taps_ref.shape[0]):
-        short = short + taps_ref[lag : lag + 1] * pltpu.roll(proj, lag, 0)
-    short = short[HALO:]
+        short = short + taps_ref[lag : lag + 1] * proj_ref[HALO - lag : HALO - lag + count]
     query_ref[...] = short[:, :chans]
     signal = short[:, chans : 2 * chans] * short[:, 2 * chans :]
     signal_ref[...] = signal
@@ -126,22 +214,34 @@
         piece = conv[:, b * per : (b + 1) * per].reshape(groups * per, lanes).T
         at = slice(b * lanes, (b + 1) * lanes)
         mixed = piece + skip_ref[...] * signal_ref[at]
-        out_ref[at] = (query_ref[at] * mixed).astype(BF16)
-
-
-def out_body(gated_ref, w_ref, out_ref):
+        gated = (query_ref[at] * mixed).astype(BF16)
+        for p in range(out_ref.shape[1]):
+            out_ref[b, p] = gated
+
+
+def out_body(place_ref, gated_ref, own_ref, near_ref, across_ref, out_ref):
+    place = place_ref[0, 0]
     inner, tp, rows, chans = gated_ref.shape
     x = jnp.concatenate([gated_ref[s, p] for p in range(tp) for s in range(inner)], axis=1)
-    out_ref[...] = jnp.dot(x, w_ref[...], preferred_element_type=F32).astype(BF16)
+    weight = jnp.concatenate([own_ref[...], near_ref[...], across_ref[0], across_ref[1]], axis=1)
+    out = jnp.dot(x, weight, preferred_element_type=F32).astype(BF16)
+    for k, flip in enumerate((0, 2, 1, 3)):
+        at = pl.multiple_of((place ^ flip) * chans, chans)
+        out_ref[:, pl.ds(at, chans)] = out[:, k * chans : (k + 1) * chans]
 
 
 def shape(dims, dtype):
     return jax.ShapeDtypeStruct(dims, dtype)
 
 
+def swap(value, axis):
+    return lax.ppermute(value, axis, [(0, 1), (1, 0)])
+
+
 def shards(ways, tables, tokens, norm_gain, in_weight, short_taps, filter_response, skip_gain, out_weight):
     outer = ways["y"] * ways["x"]
-    inner = ways["zl"] * ways["co"]
+    cores = ways["co"]
+    inner = ways["zl"] * cores
     tp = ways["tp"]
     length, feats = tokens.shape
     chans = skip_gain.shape[0] // inner
@@ -149,21 +249,61 @@
     depth, parts = in_weight.shape[0], in_weight.shape[1]
     rows = inner * per
     place = lax.axis_index(INNER)
-
+    core = lax.axis_index("co")
+    as_scalar = lambda value: value.astype(jnp.int32).reshape(1, 1)
+    gain = norm_gain.reshape(1, tp * feats)
+
+    with jax.named_scope("token_gather"):
+        own = lax.all_gather(tokens, ("zl", "tp"), axis=0)
+        other = swap(own, "co")
+        tail = own[own.shape[0] - tp :, length - HALO :]
+        halo_own = lax.ppermute(tail, OUTER, [(i, i + 1) for i in range(outer - 1)])
+        halo_other = lax.ppermute(
+            tail,
+            OUTER + ("co",),
+            [(i * cores + cores - 1, (i + 1) * cores) for i in range(outer - 1)],
+        )
     with jax.named_scope("weight_gather"):
-        split = in_weight.reshape(depth, parts, inner, chans).transpose(2, 1, 0, 3)
-        swapped = lax.all_to_all(split, INNER, 0, 0)
-        weight = lax.all_gather(swapped, OUTER, axis=0)
-        weight = weight.reshape(outer * inner, parts, depth, chans)
-    with jax.named_scope("token_gather"):
-        tok = lax.all_gather(tokens, INNER + ("tp",), axis=0).reshape(inner, tp, length, feats)
-        halo = lax.ppermute(
-            tok[inner - 1, :, length - HALO :], OUTER, [(i, i + 1) for i in range(outer - 1)]
-        )
-    with jax.named_scope("filter_points"):
-        taps = filter_response.astype(BF16).T.reshape(inner, outer, per, length)
-        taps = taps.transpose(1, 0, 2, 3).reshape(outer * inner, per, length)
-        taps = lax.all_to_all(taps, SEQ, 0, 0).reshape(outer * inner * per, length)
+        kinds = parts + 2
+        send = call(
+            pack_body,
+            shape((ways["y"] * inner, kinds, depth, LANES), BF16),
+            in_weight.transpose(1, 0, 2),
+            out_weight,
+            filter_response,
+        )
+        got = lax.all_to_all(send, ("y",) + INNER, 0, 0)
+        tiles = (kinds - 1) * ways["y"] * inner + ways["y"] * inner // ways["x"]
+        send = call(repack_body, shape((ways["x"], tiles, depth, LANES), BF16), got)
+        got = lax.all_to_all(send, "x", 0, 0)
+    with jax.named_scope("norm"):
+        normed = shape((ways["zl"] * length, tp * feats), BF16)
+        x_own = call(norm_body, normed, own, gain)
+        x_other = call(norm_body, normed, other, gain)
+    with jax.named_scope("project"):
+        own_taps = lax.dynamic_slice_in_dim(short_taps, place * chans, chans, 2)
+        query, signal, send, out_w, taps = call(
+            functools.partial(project_body, cores),
+            (
+                shape((inner * length, chans), F32),
+                shape((inner * length, chans), F32),
+                shape((outer, rows, LANES), BF16),
+                shape((outer * inner * depth, chans), BF16),
+                shape((outer * rows, LANES), BF16),
+            ),
+            as_scalar(core),
+            x_own,
+            x_other,
+            halo_own,
+            halo_other,
+            gain,
+            got,
+            own_taps.reshape(short_taps.shape[0], parts * chans),
+            scalars=1,
+            scratch=[pltpu.VMEM((HALO + inner * length, parts * chans), F32)],
+        )
+    with jax.named_scope("conv"):
+        blocks = lax.all_to_all(send, OUTER, 0, 0)
         spec = call(
             filter_body,
             shape((per * outer * inner, 2 * LANES), F32),
@@ -172,33 +312,6 @@
             tables["near_in"],
             tables["turn"],
         )
-    with jax.named_scope("out_weight_gather"):
-        out_w = lax.all_to_all(
-            jnp.broadcast_to(out_weight[None], (outer * inner,) + out_weight.shape), SEQ, 0, 0
-        ).reshape(outer * inner * out_weight.shape[0], out_weight.shape[1])
-    with jax.named_scope("norm"):
-        x = call(
-            norm_body,
-            shape((HALO + inner * length, tp * feats), BF16),
-            tok,
-            halo,
-            norm_gain.reshape(1, tp * feats),
-        )
-    with jax.named_scope("project"):
-        own_taps = lax.dynamic_slice_in_dim(short_taps, place * chans, chans, 2)
-        query, signal, send = call(
-            project_body,
-            (
-                shape((inner * length, chans), F32),
-                shape((inner * length, chans), F32),
-                shape((outer, rows, LANES), BF16),
-            ),
-            x,
-            weight,
-            own_taps.reshape(short_taps.shape[0], parts * chans),
-        )
-    with jax.named_scope("conv"):
-        blocks = lax.all_to_all(send, OUTER, 0, 0)
         conv = call(
             conv_body,
             shape((outer, rows, LANES), BF16),
@@ -211,23 +324,33 @@
             tables["back"],
         )
         conv = lax.all_to_all(conv, OUTER, 0, 0)
+    with jax.named_scope("out_weight_swap"):
+        near_w = swap(out_w, "zl")
+        across_w = swap(jnp.stack([out_w, near_w]), "co")
     with jax.named_scope("gate"):
         own_skip = lax.dynamic_slice_in_dim(skip_gain, place * chans, chans, 0)
         gated = call(
             gate_body,
-            shape((inner * length, chans), BF16),
+            shape((inner, tp, length, chans), BF16),
             conv,
             query,
             signal,
             own_skip.reshape(1, chans),
         )
-    with jax.named_scope("gated_gather"):
-        gated = jnp.broadcast_to(
-            gated.reshape(inner, 1, length, chans), (inner, tp, length, chans)
-        ).reshape(inner * tp, length, chans)
-        gated = lax.all_to_all(gated, INNER + ("tp",), 0, 0).reshape(inner, tp, length, chans)
+        gated = lax.all_to_all(
+            gated.reshape(inner * tp, length, chans), INNER + ("tp",), 0, 0
+        ).reshape(inner, tp, length, chans)
     with jax.named_scope("out_project"):
-        return call(out_body, shape((length, out_w.shape[1]), BF16), gated, out_w)
+        return call(
+            out_body,
+            shape((length, out_weight.shape[1]), BF16),
+            as_scalar(place),
+            gated,
+            out_w,
+            near_w,
+            across_w,
+            scalars=1,
+        )
 
 
 def solution(mesh):

time: 315 us -> 176 us (0.56)
  waiting for transfers between devices: 200 us -> 56.4 us
  blocking collectives: 51.5 us -> 24.7 us
  starting transfers between devices: 28.6 us -> 46.7 us
  local copies, waits for them, and re-layouts: 15.2 us -> 22.3 us
  Pallas kernels: 5.71 us -> 9.7 us
    all_gather x2 -> x1, waiting for transfers between devices: 141 us -> 26.9 us  [shards(): own = lax.all_gather(tokens, ('zl', 'tp'), axis=0)]
    all_to_all x2 -> x3, waiting for transfers between devices: 49.3 us -> 22 us  [the longest x1 18.9 us: shards(): got = lax.all_to_all(send, ('y',) + INNER, 0, 0)]
    all_to_all x3 -> x1, blocking collectives: 51.5 us -> 24.7 us  [shards(): lax.all_to_all(gated.reshape(inner * tp, length, chans), INNER + ('tp',),...]
    ppermute x1 -> x5, starting transfers between devices: 2.32 us -> 18.8 us  [the longest x3 13.2 us: swap(): return lax.ppermute(value, axis, [(0, 1), (1, 0)])]
    unnamed x35 -> x54, local copies, waits for them, and re-layouts: 10.2 us -> 20.7 us
    pallas_call x6 -> x9, Pallas kernels: 5.71 us -> 9.7 us  [call(): pl.pallas_call(body, out_shape=out_shape, in_specs=specs, scratch_shapes=...]
    all_to_all x1, starting transfers between devices: 5.7 us -> 9.29 us  [shards(): blocks = lax.all_to_all(send, OUTER, 0, 0)]
    all_to_all x2 -> x3, starting transfers between devices: 20.6 us -> 18.6 us  [the longest x1 10.6 us: shards(): got = lax.all_to_all(send, ('y',) + INNER, 0, 0)]
  transfers between devices with their start and end apart: 6 -> 10, of which waited for: 5 -> 4; matrix products, arithmetic and copies ran while one was open for 1% -> 2% of each run, Pallas kernels for 1% -> 2%
where the time goes in v2:
time: 176 us; the launch traced here: 175 us
  waiting for transfers between devices  56.4 us (32%)
  starting transfers between devices  46.7 us (27%)
  blocking collectives  24.7 us (14%)
  local copies, waits for them, and re-layouts  22.3 us (13%)
  between operations  13.6 us (8%)
  Pallas kernels  9.7 us (6%)
    all_gather x1, waiting for transfers between devices, shards(): own = lax.all_gather(tokens, ('zl', 'tp'), axis=0)  26.9 us
    all_to_all x1, blocking collectives, shards(): lax.all_to_all(gated.reshape(inner * tp, length, chans), INNER + ('tp',),...  24.7 us
    unnamed x54, local copies, waits for them, and re-layouts  20.7 us
    all_to_all x1, waiting for transfers between devices, shards(): got = lax.all_to_all(send, ('y',) + INNER, 0, 0)  18.9 us
    ppermute x3, starting transfers between devices, swap(): return lax.ppermute(value, axis, [(0, 1), (1, 0)])  13.2 us
    all_to_all x1, starting transfers between devices, shards(): got = lax.all_to_all(send, ('y',) + INNER, 0, 0)  10.6 us
    pallas_call x9, Pallas kernels, call(): pl.pallas_call(body, out_shape=out_shape, in_specs=specs, scratch_shapes=...  9.7 us
    all_to_all x1, starting transfers between devices, shards(): blocks = lax.all_to_all(send, OUTER, 0, 0)  9.29 us
  transfers between devices with their start and end apart: 10, of which 4 were waited for; matrix products, arithmetic and copies ran while one was open for 2% of the time, Pallas kernels for 2%

profile of v2, /device:TPU:1, one launch (start us, length us, event | category | flops | bytes accessed | tf_op | source)
XLA Modules:
  0.0 174.5 jit_solution(11822317968344173965)
XLA Ops:
  6.5 1.0 copy-done.12
  9.0 1.0 weight_gather.2
  10.0 10.6 %all-to-all-start = ((bf16[32,5,16,128]{3,2,1,0:T(8,128)(2,1)}), bf16[32,5,16,128]{3,2,1,0:T(8,128)(2,1)S(1)}, u32[]{:S(2)}, u32[]{:S(2)}) async-start(bf16[32,5,16,128]{3,2,1,0:T(8,128)(2,1)} %weight_gather.2), calls=%async_computation | async-start | bytes 1310720 | tf_op jit(solution)/shard_map/weight_gather/all_to_all | solution.py:275
  21.3 18.9 %all-to-all-done.got_ref = bf16[32,5,16,128]{3,2,1,0:T(8,128)(2,1)S(1)} async-done(((bf16[32,5,16,128]{3,2,1,0:T(8,128)(2,1)}), bf16[32,5,16,128]{3,2,1,0:T(8,128)(2,1)S(1)}, u32[]{:S(2)}, u32[]{:S(2)}) %all-to-all-start) | async-done | bytes 655392 | tf_op jit(solution)/shard_map/weight_gather/all_to_all | solution.py:275
  40.3 1.4 copy-done.1
  41.7 4.1 %all-to-all-start.1 = ((bf16[4,136,16,128]{3,2,1,0:T(8,128)(2,1)}), bf16[4,136,16,128]{3,2,1,0:T(8,128)(2,1)S(1)}, u32[]{:S(2)}, u32[]{:S(2)}) async-start(bf16[4,136,16,128]{3,2,1,0:T(8,128)(2,1)} %copy-done.1), calls=%async_computation.1 | async-start | bytes 4456448 | tf_op jit(solution)/shard_map/weight_gather/all_to_all | solution.py:278
  45.8 26.9 %all-gather.3.cloned.1.call-done = bf16[1024,512]{1,0:T(8,128)(2,1)} async-done(((bf16[128,512]{1,0:T(8,128)(2,1)}), bf16[1024,512]{1,0:T(8,128)(2,1)}) %all-gather.3.cloned.1.call-update) | async-done | bytes 1048592 | tf_op jit(solution)/shard_map/token_gather/all_gather | solution.py:257
  72.8 6.5 %collective-permute-start = (bf16[8,128,512]{2,1,0:T(8,128)(2,1)}, bf16[8,128,512]{2,1,0:T(8,128)(2,1)S(1)}, u32[]{:S(2)}, u32[]{:S(2)}) collective-permute-start(bf16[8,128,512]{2,1,0:T(8,128)(2,1)} %bitcast.19), channel_id=1, source_target_pairs={{0,4},{4,0},{1,5},{5,1},{2,6},{6,2},{3,7},{7,3},{8,12},{12,8},{9,1... | collective-permute-start | bytes 3145736 | tf_op jit(solution)/shard_map/token_gather/ppermute | solution.py:238
  80.1 2.6 %collective-permute-start.1 = (bf16[4,16,512]{2,1,0:T(8,128)(2,1)S(1)}, bf16[4,16,512]{2,1,0:T(8,128)(2,1)S(1)}, u32[]{:S(2)}, u32[]{:S(2)}) collective-permute-start(bf16[4,16,512]{2,1,0:T(8,128)(2,1)S(1)} %slice.4), channel_id=1, source_target_pairs={{0,16},{16,32},{32,48},{48,64},{64,80},{80,96},{96,112},{112,128},... | collective-permute-start | bytes 196616 | tf_op jit(solution)/shard_map/token_gather/ppermute | solution.py:260
  82.7 3.0 %collective-permute-start.2 = (bf16[4,16,512]{2,1,0:T(8,128)(2,1)S(1)}, bf16[4,16,512]{2,1,0:T(8,128)(2,1)S(1)}, u32[]{:S(2)}, u32[]{:S(2)}) collective-permute-start(bf16[4,16,512]{2,1,0:T(8,128)(2,1)S(1)} %slice.4), channel_id=1, source_target_pairs={{4,16},{20,32},{36,48},{52,64},{68,80},{84,96},{100,112},{116,128}... | collective-permute-start | bytes 196616 | tf_op jit(solution)/shard_map/token_gather/ppermute | solution.py:261
  85.8 1.2 copy-done.9
  87.5 1.0 copy-done.3
  88.8 1.0 copy-done.5
  90.4 1.2 copy-done.4
  91.7 1.2 copy-done.6
  93.7 2.7 %project.1 = (f32[512,128]{1,0:T(8,128)S(1)}, f32[512,128]{1,0:T(8,128)S(1)}, bf16[32,16,128]{2,1,0:T(8,128)(2,1)S(1)}, bf16[2048,128]{1,0:T(8,128)(2,1)}, bf16[512,128]{1,0:T(8,128)(2,1)S(1)}) custom-call(s32[1,1]{1,0:T(1,128)} %bitcast.1.core_ref, bf16[256,2048]{1,0:T(8,128)(2,1)S(1)} %copy-done.4, bf16[256,2048]{1,0:T(8,128)(2,1)S(1)} %copy-done.6, ...), custom_call_target="tpu_custom_call" | custom-call | tf_op jit(solution)/shard_map/project/pallas_call | solution.py:25
  99.2 2.4 %collective-permute-start.3 = (bf16[2048,128]{1,0:T(8,128)(2,1)}, bf16[2048,128]{1,0:T(8,128)(2,1)S(1)}, u32[]{:S(2)}, u32[]{:S(2)}) collective-permute-start(bf16[2048,128]{1,0:T(8,128)(2,1)} %get-tuple-element.14.own_ref), channel_id=1, source_target_pairs={{0,8},{8,0},{1,9},{9,1},{2,10},{10,2},{3,11},{11,3},{4,12},{12,4},... | collective-permute-start | bytes 1572872 | tf_op jit(solution)/shard_map/out_weight_swap/ppermute | solution.py:238
  101.5 9.3 %all-to-all-start.2 = ((bf16[32,16,128]{2,1,0:T(8,128)(2,1)}), bf16[32,16,128]{2,1,0:T(8,128)(2,1)S(1)}, u32[]{:S(2)}, u32[]{:S(2)}) async-start(bf16[32,16,128]{2,1,0:T(8,128)(2,1)} %copy-done.20), calls=%async_computation.2 | async-start | bytes 262144 | tf_op jit(solution)/shard_map/conv/all_to_all | solution.py:306
  110.9 1.0 copy-done.7
  111.9 0.9 copy-done.19
  113.4 6.8 %all-to-all-done.2.sig_ref = bf16[32,16,128]{2,1,0:T(8,128)(2,1)S(1)} async-done(((bf16[32,16,128]{2,1,0:T(8,128)(2,1)}), bf16[32,16,128]{2,1,0:T(8,128)(2,1)S(1)}, u32[]{:S(2)}, u32[]{:S(2)}) %all-to-all-start.2) | async-done | bytes 131104 | tf_op jit(solution)/shard_map/conv/all_to_all | solution.py:306
  120.2 1.0 copy-done.8
  121.2 1.2 copy-done.10
  123.3 2.2 %conv.3 = bf16[32,16,128]{2,1,0:T(8,128)(2,1)} custom-call(bf16[32,16,128]{2,1,0:T(8,128)(2,1)S(1)} %all-to-all-done.2.sig_ref, f32[512,256]{1,0:T(8,128)S(1)} %conv.2.spec_ref, bf16[1024,512]{1,0:T(8,128)(2,1)S(1)} %copy-done.2, bf16[256,256]{1,0:T(8,128)(2,1)S(1)} %copy-done.11, f32[2,512,128]{2,1,0:T(8,128)S(1)} %copy-done.8, ...), custom_call_target="tpu_custom_call" | custom-call | tf_op jit(solution)/shard_map/conv/pallas_call | solution.py:25
  125.5 3.9 %all-to-all-start.3 = ((bf16[32,16,128]{2,1,0:T(8,128)(2,1)}), bf16[32,16,128]{2,1,0:T(8,128)(2,1)S(1)}, u32[]{:S(2)}, u32[]{:S(2)}) async-start(bf16[32,16,128]{2,1,0:T(8,128)(2,1)} %conv.3), calls=%async_computation.3 | async-start | bytes 262144 | tf_op jit(solution)/shard_map/conv/all_to_all | solution.py:326
  129.4 1.1 pad_maximum_fusion
  130.6 4.3 %collective-permute-start.4 = (bf16[2,2048,128]{2,1,0:T(8,128)(2,1)S(1)}, bf16[2,2048,128]{2,1,0:T(8,128)(2,1)S(1)}, u32[]{:S(2)}, u32[]{:S(2)}) collective-permute-start(bf16[2,2048,128]{2,1,0:T(8,128)(2,1)S(1)} %pad_maximum_fusion), channel_id=1, source_target_pairs={{0,4},{4,0},{1,5},{5,1},{2,6},{6,2},{3,7},{7,3},{8,12},{12,8},{9,1... | collective-permute-start | bytes 3145736 | tf_op jit(solution)/shard_map/out_weight_swap/ppermute | solution.py:238
  135.7 3.2 %all-to-all-done.3.conv_ref = bf16[32,16,128]{2,1,0:T(8,128)(2,1)S(1)} async-done(((bf16[32,16,128]{2,1,0:T(8,128)(2,1)}), bf16[32,16,128]{2,1,0:T(8,128)(2,1)S(1)}, u32[]{:S(2)}, u32[]{:S(2)}) %all-to-all-start.3) | async-done | bytes 131104 | tf_op jit(solution)/shard_map/conv/all_to_all | solution.py:326
  138.8 0.9 copy-done.14
  139.8 0.9 copy-done.16
  140.8 24.7 %all_to_all.25 = bf16[16,128,128]{2,1,0:T(8,128)(2,1)S(1)} all-to-all(bf16[16,128,128]{2,1,0:T(8,128)(2,1)S(1)} %bitcast.16), channel_id=1, replica_groups=mesh['y'=8,'x'=4,'zl'=2,'co'=2,'tp'=4] {'zl','co','tp'}, dimensions={0} | all-to-all | bytes 1048576 | tf_op jit(solution)/shard_map/gate/all_to_all | solution.py:340
  165.5 2.2 %out_project.1 = bf16[128,512]{1,0:T(8,128)(2,1)} custom-call(s32[1,1]{1,0:T(1,128)} %bitcast.place_ref, bf16[4,4,128,128]{3,2,1,0:T(8,128)(2,1)S(1)} %bitcast.17, bf16[2048,128]{1,0:T(8,128)(2,1)} %get-tuple-element.14.own_ref, bf16[2048,128]{1,0:T(8,128)(2,1)S(1)} %collective-permute-done.3.near_ref, ...), custom_call_target="tpu_custom_call" | custom-call | tf_op jit(solution)/shard_map/out_project/pallas_call | solution.py:25
  (56 shorter events, 10.7 us)
Async XLA Ops:
  6.5 79.2 %copy-start = (f32[3,3,512]{2,1,0:T(4,128)S(1)}, f32[3,3,512]{2,1,0:T(4,128)}, u32[]{:S(2)}) copy-start(f32[3,3,512]{2,1,0:T(4,128)} %param.15) | copy-start | bytes 55300
  6.5 1.0 copy-start.12
  7.5 0.8 copy-start.24
  8.3 0.7 copy-start.25
  10.0 30.2 %all-to-all-start = ((bf16[32,5,16,128]{3,2,1,0:T(8,128)(2,1)}), bf16[32,5,16,128]{3,2,1,0:T(8,128)(2,1)S(1)}, u32[]{:S(2)}, u32[]{:S(2)}) async-start(bf16[32,5,16,128]{3,2,1,0:T(8,128)(2,1)} %weight_gather.2), calls=%async_computation | async-start | bytes 1310720 | tf_op jit(solution)/shard_map/weight_gather/all_to_all | solution.py:275
  20.5 52.2 %all-gather.3.cloned.1.call-start = ((), (), s32[]{:S(2)}) async-start(), calls=%async_computation.5 | async-start | bytes 1179648 | tf_op jit(solution)/shard_map/token_gather/all_gather | solution.py:257
  40.3 1.4 copy-start.1
  41.7 44.1 %copy-start.21 = (f32[2048]{0:T(1024)S(1)}, f32[2048]{0:T(1024)}, u32[]{:S(2)}) copy-start(f32[2048]{0:T(1024)} %param.13) | copy-start | bytes 24580
  41.7 48.7 %all-to-all-start.1 = ((bf16[4,136,16,128]{3,2,1,0:T(8,128)(2,1)}), bf16[4,136,16,128]{3,2,1,0:T(8,128)(2,1)S(1)}, u32[]{:S(2)}, u32[]{:S(2)}) async-start(bf16[4,136,16,128]{3,2,1,0:T(8,128)(2,1)} %copy-done.1), calls=%async_computation.1 | async-start | bytes 4456448 | tf_op jit(solution)/shard_map/weight_gather/all_to_all | solution.py:278
  72.8 15.6 %collective-permute-start = (bf16[8,128,512]{2,1,0:T(8,128)(2,1)}, bf16[8,128,512]{2,1,0:T(8,128)(2,1)S(1)}, u32[]{:S(2)}, u32[]{:S(2)}) collective-permute-start(bf16[8,128,512]{2,1,0:T(8,128)(2,1)} %bitcast.19), channel_id=1, source_target_pairs={{0,4},{4,0},{1,5},{5,1},{2,6},{6,2},{3,7},{7,3},{8,12},{12,8},{9,1... | collective-permute-start | bytes 3145736 | tf_op jit(solution)/shard_map/token_gather/ppermute | solution.py:238
  80.1 9.7 %collective-permute-start.1 = (bf16[4,16,512]{2,1,0:T(8,128)(2,1)S(1)}, bf16[4,16,512]{2,1,0:T(8,128)(2,1)S(1)}, u32[]{:S(2)}, u32[]{:S(2)}) collective-permute-start(bf16[4,16,512]{2,1,0:T(8,128)(2,1)S(1)} %slice.4), channel_id=1, source_target_pairs={{0,16},{16,32},{32,48},{48,64},{64,80},{80,96},{96,112},{112,128},... | collective-permute-start | bytes 196616 | tf_op jit(solution)/shard_map/token_gather/ppermute | solution.py:260
  82.7 7.1 %collective-permute-start.2 = (bf16[4,16,512]{2,1,0:T(8,128)(2,1)S(1)}, bf16[4,16,512]{2,1,0:T(8,128)(2,1)S(1)}, u32[]{:S(2)}, u32[]{:S(2)}) collective-permute-start(bf16[4,16,512]{2,1,0:T(8,128)(2,1)S(1)} %slice.4), channel_id=1, source_target_pairs={{4,16},{20,32},{36,48},{52,64},{68,80},{84,96},{100,112},{116,128}... | collective-permute-start | bytes 196616 | tf_op jit(solution)/shard_map/token_gather/ppermute | solution.py:261
  85.8 1.2 copy-start.9
  87.4 1.0 copy-start.3
  88.8 1.0 copy-start.5
  90.4 1.2 copy-start.4
  91.7 1.2 copy-start.6
  92.9 0.8 copy-start.23
  93.7 17.1 %copy-start.2 = (bf16[1024,512]{1,0:T(8,128)(2,1)S(1)}, bf16[1024,512]{1,0:T(8,128)(2,1)}, u32[]{:S(2)}) copy-start(bf16[1024,512]{1,0:T(8,128)(2,1)} %constant.30.clone.into_ref) | copy-start | bytes 3145732
  93.7 17.1 %copy-start.11 = (bf16[256,256]{1,0:T(8,128)(2,1)S(1)}, bf16[256,256]{1,0:T(8,128)(2,1)}, u32[]{:S(2)}) copy-start(bf16[256,256]{1,0:T(8,128)(2,1)} %constant.31.clone.near_ref.near_in_ref) | copy-start | bytes 393220
  97.1 0.7 copy-start.15
  99.2 30.3 %collective-permute-start.3 = (bf16[2048,128]{1,0:T(8,128)(2,1)}, bf16[2048,128]{1,0:T(8,128)(2,1)S(1)}, u32[]{:S(2)}, u32[]{:S(2)}) collective-permute-start(bf16[2048,128]{1,0:T(8,128)(2,1)} %get-tuple-element.14.own_ref), channel_id=1, source_target_pairs={{0,8},{8,0},{1,9},{9,1},{2,10},{10,2},{3,11},{11,3},{4,12},{12,4},... | collective-permute-start | bytes 1572872 | tf_op jit(solution)/shard_map/out_weight_swap/ppermute | solution.py:238
  101.5 18.6 %all-to-all-start.2 = ((bf16[32,16,128]{2,1,0:T(8,128)(2,1)}), bf16[32,16,128]{2,1,0:T(8,128)(2,1)S(1)}, u32[]{:S(2)}, u32[]{:S(2)}) async-start(bf16[32,16,128]{2,1,0:T(8,128)(2,1)} %copy-done.20), calls=%async_computation.2 | async-start | bytes 262144 | tf_op jit(solution)/shard_map/conv/all_to_all | solution.py:306
  110.8 1.0 copy-start.7
  111.9 0.9 copy-start.19
  120.2 1.0 copy-start.8
  121.2 1.2 copy-start.10
  122.4 0.9 copy-start.17
  125.5 13.3 %all-to-all-start.3 = ((bf16[32,16,128]{2,1,0:T(8,128)(2,1)}), bf16[32,16,128]{2,1,0:T(8,128)(2,1)S(1)}, u32[]{:S(2)}, u32[]{:S(2)}) async-start(bf16[32,16,128]{2,1,0:T(8,128)(2,1)} %conv.3), calls=%async_computation.3 | async-start | bytes 262144 | tf_op jit(solution)/shard_map/conv/all_to_all | solution.py:326
  130.6 35.0 %collective-permute-start.4 = (bf16[2,2048,128]{2,1,0:T(8,128)(2,1)S(1)}, bf16[2,2048,128]{2,1,0:T(8,128)(2,1)S(1)}, u32[]{:S(2)}, u32[]{:S(2)}) collective-permute-start(bf16[2,2048,128]{2,1,0:T(8,128)(2,1)S(1)} %pad_maximum_fusion), channel_id=1, source_target_pairs={{0,4},{4,0},{1,5},{5,1},{2,6},{6,2},{3,7},{7,3},{8,12},{12,8},{9,1... | collective-permute-start | bytes 3145736 | tf_op jit(solution)/shard_map/out_weight_swap/ppermute | solution.py:238
  138.8 1.0 copy-start.14
  139.8 0.9 copy-start.16
  (4 other events, 2.6 us)
Sparse Core Ops, SparseCore 0:
  23.5 49.2 all-gather.2

commit v3 on v1

v3 whole, which is shorter than its diff:
```python
import functools
import math

import jax
import jax.numpy as jnp
import numpy as np
from jax import lax
from jax.experimental import pallas as pl
from jax.experimental.pallas import tpu as pltpu
from jax.sharding import Mesh
from jax.sharding import PartitionSpec as P

F32 = jnp.float32
BF16 = jnp.bfloat16
LANES = 128
HALO = 16
KERNEL_VMEM = 60 * 1024 * 1024
OUTER = ("y", "x")
INNER = ("zl", "co")
SEQ = OUTER + INNER


def call(body, out_shape, places, args, scratch=()):
    spaces = {"h": pltpu.HBM, "v": pltpu.VMEM, "s": pltpu.SMEM}
    specs = [pl.BlockSpec(memory_space=spaces[place]) for place in places]
    single = not isinstance(out_shape, tuple)
    outs = specs[len(args) :]
    return pl.pallas_call(
        body,
        out_shape=out_shape,
        in_specs=specs[: len(args)],
        out_specs=outs[0] if single else tuple(outs),
        scratch_shapes=scratch,
        compiler_params=pltpu.CompilerParams(vmem_limit_bytes=KERNEL_VMEM),
    )(*args)


def started(pairs, sems, first=0):
    copies = [
        pltpu.make_async_copy(source, target, sems.at[first + k])
        for k, (source, target) in enumerate(pairs)
    ]
    for copy in copies:
        copy.start()
    return copies


def finish(copies):
    for copy in copies:
        copy.wait()


def transform_tables(length, chans, outer, inner):
    blocks = length // LANES
    row = np.arange(blocks)
    lane = np.arange(LANES)
    far = np.exp(-2j * np.pi * (row[:, None] * (4 * row[None, :] + 1) % (4 * blocks)) / (4 * blocks))
    near = np.exp(-2j * np.pi * (lane[:, None] * lane[None, :] % LANES) / LANES)
    turn = np.exp(-2j * np.pi * ((4 * row[:, None] + 1) * lane[None, :] % (4 * length)) / (4 * length))
    eye = np.eye(chans)
    into = np.einsum("bf,cd->cfbd", far, eye).reshape(chans * blocks, blocks * chans)
    into = np.concatenate([into.real, into.imag], axis=0)
    back = np.einsum("bf,cd->bdcf", far.conj(), eye).reshape(blocks * chans, chans * blocks) / length
    back = np.concatenate([back.real, -back.imag], axis=1)
    near_in = np.block([[near.real, near.imag], [-near.imag, near.real]])
    near_out = np.block([[near.real, -near.imag], [near.imag, near.real]])
    turn = np.stack([turn.real, turn.imag])
    as_short = lambda table: jnp.asarray(table.astype(np.float32)).astype(BF16)
    return {
        "into": as_short(into),
        "back": as_short(back),
        "near_in": as_short(near_in),
        "near_out": as_short(near_out),
        "turn": jnp.asarray(turn.astype(np.float32)),
    }


def times(real, imag, cos, sin):
    return real * cos - imag * sin, real * sin + imag * cos


def turned(pair, turn_ref, sign, axis):
    chans = pair[0].shape[0] // turn_ref.shape[1]
    cos = jnp.concatenate([turn_ref[0]] * chans, axis=0)
    sin = jnp.concatenate([turn_ref[1]] * chans, axis=0) * sign
    return jnp.concatenate(times(*pair, cos, sin), axis=axis).astype(BF16)


def halves(value, axis):
    half = value.shape[axis] // 2
    return lax.slice_in_dim(value, 0, half, axis=axis), lax.slice_in_dim(value, half, 2 * half, axis=axis)


def filter_body(got_ref, into_hbm, near_hbm, turn_hbm, out_hbm, into_ref, near_ref, turn_ref, out_ref, sems):
    copies = started([(into_hbm, into_ref), (turn_hbm, turn_ref), (near_hbm, near_ref)], sems)
    ways, outer = got_ref.shape[:2]
    block = jnp.concatenate([got_ref[x, y] for y in range(outer) for x in range(ways)], axis=0)
    copies[0].wait()
    far = jnp.dot(into_ref[...], block, preferred_element_type=F32)
    copies[1].wait()
    pair = turned(halves(far, 0), turn_ref, 1.0, 1)
    copies[2].wait()
    out_ref[...] = jnp.dot(pair, near_ref[...], preferred_element_type=F32)
    finish(started([(out_ref, out_hbm)], sems, len(copies)))


def conv_body(
    sig_ref,
    spec_hbm,
    into_hbm,
    near_in_hbm,
    turn_hbm,
    near_out_hbm,
    back_hbm,
    out_hbm,
    spec_ref,
    into_ref,
    near_in_ref,
    turn_ref,
    near_out_ref,
    back_ref,
    out_ref,
    sems,
):
    copies = started(
        [
            (into_hbm, into_ref),
            (turn_hbm, turn_ref),
            (near_in_hbm, near_in_ref),
            (spec_hbm, spec_ref),
            (near_out_hbm, near_out_ref),
            (back_hbm, back_ref),
        ],
        sems,
    )
    groups, rows, lanes = sig_ref.shape
    block = sig_ref[...].reshape(groups * rows, lanes)
    copies[0].wait()
    far = jnp.dot(into_ref[...], block, preferred_element_type=F32)
    copies[1].wait()
    pair = turned(halves(far, 0), turn_ref, 1.0, 1)
    copies[2].wait()
    points = jnp.dot(pair, near_in_ref[...], preferred_element_type=F32)
    copies[3].wait()
    product = times(*halves(points, 1), *halves(spec_ref[...], 1))
    pair = jnp.concatenate(product, axis=1).astype(BF16)
    copies[4].wait()
    near = jnp.dot(pair, near_out_ref[...], preferred_element_type=F32)
    pair = turned(halves(near, 1), turn_ref, -1.0, 0)
    copies[5].wait()
    result = jnp.dot(back_ref[...], pair, preferred_element_type=F32)
    out_ref[...] = result.astype(BF16).reshape(groups, rows, lanes)
    finish(started([(out_ref, out_hbm)], sems, len(copies)))


def pack_body(weight_hbm, out_w_hbm, taps_hbm, send_hbm, weight_ref, out_w_ref, taps_ref, send_ref, sems):
    copies = started([(taps_hbm, taps_ref), (weight_hbm, weight_ref), (out_w_hbm, out_w_ref)], sems)
    parts = weight_ref.shape[0]
    total, _, rows, lanes = send_ref.shape
    inner = out_w_ref.shape[1] // lanes
    ways = total // inner
    copies[0].wait()
    for s in range(inner):
        taps = taps_ref[:, s * lanes : (s + 1) * lanes].T.reshape(ways, rows, lanes).astype(BF16)
        for way in range(ways):
            send_ref[way * inner + s, parts + 1] = taps[way]
    finish(copies[1:])
    for s in range(inner):
        at = slice(s * lanes, (s + 1) * lanes)
        for way in range(ways):
            for part in range(parts):
                send_ref[way * inner + s, part] = weight_ref[part, :, at]
            send_ref[way * inner + s, parts] = out_w_ref[:, at]
    finish(started([(send_ref, send_hbm)], sems, len(copies)))


def repack_body(got_ref, weight_hbm, taps_hbm, taps_ref, sems):
    kinds, rows, lanes = got_ref.shape[1:]
    parts = kinds - 1
    copies = started([(got_ref.at[:, :parts], weight_hbm)], sems)
    ways, outer = taps_ref.shape[:2]
    taps = got_ref[:, parts].astype(F32)
    per = rows // ways
    for way in range(ways):
        piece = taps[:, way * per : (way + 1) * per].reshape(outer, rows, lanes)
        taps_ref[way] = piece.astype(BF16)
    finish(copies + started([(taps_ref, taps_hbm)], sems, len(copies)))


def project_body(
    cores,
    place_ref,
    own_hbm,
    other_hbm,
    halo_own_hbm,
    halo_other_hbm,
    gain_ref,
    taps_ref,
    here_hbm,
    before_hbm,
    after_hbm,
    across_low_hbm,
    across_high_hbm,
    spec_hbm,
    query_hbm,
    signal_hbm,
    send_hbm,
    out_w_hbm,
    tok_ref,
    halo_ref,
    x_ref,
    w_ref,
    proj_ref,
    query_ref,
    signal_ref,
    send_ref,
    sems,
):
    core, x = place_ref[0, 0], place_ref[0, 1]
    tokens = started(
        [
            (own_hbm, tok_ref.at[0]),
            (other_hbm, tok_ref.at[1]),
            (halo_own_hbm, halo_ref.at[0]),
            (halo_other_hbm, halo_ref.at[1]),
        ],
        sems,
    )
    parts, outer, ways = w_ref.shape[0], w_ref.shape[1], w_ref.shape[2]
    half = outer // 2
    pairs = []
    for source, step, low, count in (
        (here_hbm, 0, 0, outer),
        (before_hbm, ways - 1, 0, outer),
        (after_hbm, 1, 0, outer),
        (across_low_hbm, 2, 0, half),
        (across_high_hbm, 2, half, half),
    ):
        to = lax.rem(x + step, ways)
        for part in range(parts):
            pairs.append((source.at[:, :, part], w_ref.at[part, pl.ds(low, count), to]))
        pairs.append((source.at[:, :, parts], out_w_hbm.at[pl.ds(low, count), to]))
    weights = started(pairs, sems, len(tokens))

    _, blocks, length, feats = tok_ref.shape
    tp = x_ref.shape[1] // feats
    inner = (x_ref.shape[0] - HALO) // length

    def put(pieces, at):
        total = sum(jnp.sum(piece * piece, axis=1, keepdims=True) for piece in pieces)
        scale = lax.rsqrt(total / (tp * feats) + 1e-05)
        for p, piece in enumerate(pieces):
            gain = gain_ref[:, p * feats : (p + 1) * feats]
            x_ref[at, p * feats : (p + 1) * feats] = (piece * scale * gain).astype(BF16)

    zs = inner // cores
    for side in range(2):
        tokens[side].wait()
        at_core = core if side == 0 else cores - 1 - core
        for z in range(zs):
            at = pl.multiple_of(HALO + (z * cores + at_core) * length, HALO)
            put([tok_ref[side, p * zs + z].astype(F32) for p in range(tp)], pl.ds(at, length))
    finish(tokens[2:])
    put(
        [
            jnp.where(core == cores - 1, halo_ref[0, p].astype(F32), halo_ref[1, p].astype(F32))
            for p in range(tp)
        ],
        slice(0, HALO),
    )
    finish(weights)
    depth = x_ref.shape[1]
    chans = query_ref.shape[1]
    weight = jnp.concatenate([w_ref[part].reshape(depth, chans) for part in range(parts)], axis=1)
    proj = jnp.dot(x_ref[...], weight, preferred_element_type=F32)
    proj_ref[...] = proj.astype(BF16).astype(F32)

    count = query_ref.shape[0]
    short = taps_ref[0:1] * proj_ref[HALO:]
    for lag in range(1, taps_ref.shape[0]):
        short = short + taps_ref[lag : lag + 1] * proj_ref[HALO - lag : HALO - lag + count]
    signal = short[:, chans : 2 * chans] * short[:, 2 * chans :]
    groups, rows, lanes = send_ref.shape
    pieces = [
        signal[b * lanes : (b + 1) * lanes].T.reshape(groups, rows // inner, lanes) for b in range(inner)
    ]
    send_ref[...] = jnp.concatenate(pieces, axis=1).astype(BF16)
    first = len(tokens) + len(weights)
    copies = started([(send_ref, send_hbm)], sems, first)
    query_ref[...] = short[:, :chans]
    signal_ref[...] = signal
    copies += started([(query_ref, query_hbm), (signal_ref, signal_hbm)], sems, first + 1)
    finish(copies)


def gate_body(conv_ref, query_hbm, signal_hbm, skip_ref, out_ref, query_ref, signal_ref, sems):
    copies = started([(query_hbm, query_ref), (signal_hbm, signal_ref)], sems)
    groups, rows, lanes = conv_ref.shape
    inner = query_ref.shape[0] // lanes
    per = rows // inner
    conv = conv_ref[...].astype(F32)
    pieces = [conv[:, b * per : (b + 1) * per].reshape(groups * per, lanes).T for b in range(inner)]
    finish(copies)
    for b, piece in enumerate(pieces):
        at = slice(b * lanes, (b + 1) * lanes)
        mixed = piece + skip_ref[...] * signal_ref[at]
        gated = (query_ref[at] * mixed).astype(BF16)
        for p in range(out_ref.shape[1]):
            out_ref[b, p] = gated


def out_body(gated_ref, w_hbm, out_ref, w_ref, sems):
    inner, tp, rows, chans = gated_ref.shape
    copies = started([(w_hbm.at[s], w_ref.at[s]) for s in range(inner)], sems)
    x = jnp.concatenate([gated_ref[s, p] for p in range(tp) for s in range(inner)], axis=1)
    finish(copies)
    weight = jnp.concatenate([w_ref[s] for s in range(inner)], axis=1)
    out_ref[...] = jnp.dot(x, weight, preferred_element_type=F32).astype(BF16)


def shape(dims, dtype):
    return jax.ShapeDtypeStruct(dims, dtype)


def swap(value, axis):
    return lax.ppermute(value, axis, [(0, 1), (1, 0)])


def ring(value, axis, count, step):
    return lax.ppermute(value, axis, [(i, (i + step) % count) for i in range(count)])


def held(*arrays):
    return [pltpu.VMEM(array.shape, array.dtype) for array in arrays]


def copies_of(count):
    return [pltpu.SemaphoreType.DMA((count,))]


def shards(ways, tables, tokens, norm_gain, in_weight, short_taps, filter_response, skip_gain, out_weight):
    along, across = ways["y"], ways["x"]
    outer = along * across
    cores = ways["co"]
    inner = ways["zl"] * cores
    tp = ways["tp"]
    length, feats = tokens.shape
    chans = skip_gain.shape[0] // inner
    per = chans // outer
    depth, parts = in_weight.shape[0], in_weight.shape[1]
    rows = inner * per
    place = lax.axis_index(INNER)
    where = jnp.stack([lax.axis_index("co"), lax.axis_index("x")]).astype(jnp.int32).reshape(1, 2)

    with jax.named_scope("token_gather"):
        own = lax.all_gather(tokens, ("tp", "zl"), axis=0)
    with jax.named_scope("weight_gather"):
        first = shape((along * inner, parts + 2, depth, LANES), BF16)
        weight = in_weight.transpose(1, 0, 2)
        send = call(
            pack_body,
            first,
            "hhhh",
            (weight, out_weight, filter_response),
            held(weight, out_weight, filter_response, first) + copies_of(4),
        )
        got = lax.all_to_all(send, ("y",) + INNER, 0, 0)
        second = shape((across, along, rows, LANES), BF16)
        here, taps = call(
            repack_body,
            (shape((along * inner, parts + 1, depth, LANES), BF16), second),
            "vhh",
            (got,),
            held(second) + copies_of(2),
        )
        here = here.reshape(along, inner, parts + 1, depth, LANES)
        before = ring(here, "x", across, 1)
        after = ring(here, "x", across, -1)
    with jax.named_scope("token_swap"):
        own, before, after = lax.optimization_barrier((own, before, after))
        other = swap(own, "co")
        tail = own.reshape(tp, ways["zl"], length, feats)[:, -1, length - HALO :]
        halo_own = lax.ppermute(tail, OUTER, [(i, i + 1) for i in range(outer - 1)])
        halo_other = lax.ppermute(
            tail,
            OUTER + ("co",),
            [(i * cores + cores - 1, (i + 1) * cores) for i in range(outer - 1)],
        )
    with jax.named_scope("weight_gather"):
        far_low = ring(before[: along // 2], "x", across, 1)
        far_high = ring(after[along // 2 :], "x", across, -1)
    with jax.named_scope("filter_points"):
        taps = lax.all_to_all(taps, "x", 0, 0)
        points = shape((per * outer * inner, 2 * LANES), F32)
        spec = call(
            filter_body,
            points,
            "vhhhh",
            (taps, tables["into"], tables["near_in"], tables["turn"]),
            held(tables["into"], tables["near_in"], tables["turn"], points) + copies_of(4),
        )
    with jax.named_scope("project"):
        own_taps = lax.dynamic_slice_in_dim(short_taps, place * chans, chans, 2)
        own_taps = own_taps.reshape(short_taps.shape[0], parts * chans)
        stream = shape((inner * length, chans), F32)
        blocks = shape((outer, rows, LANES), BF16)
        out_w = shape((along, across, inner, depth, LANES), BF16)
        held_w = shape((parts,) + out_w.shape, BF16)
        wide = shape((HALO + inner * length, tp * feats), BF16)
        proj = shape((HALO + inner * length, parts * chans), F32)
        query, signal, send, out_w = call(
            functools.partial(project_body, cores),
            (stream, stream, blocks, out_w),
            "shhhhvv" + "h" * 10,
            (where, own, other, halo_own, halo_other, norm_gain.reshape(1, tp * feats), own_taps)
            + (here, before, after, far_low, far_high, spec),
            [pltpu.VMEM((2,) + own.shape, BF16), pltpu.VMEM((2,) + tail.shape, BF16)]
            + held(wide, held_w, proj, stream, stream, blocks)
            + copies_of(4 + 5 * (parts + 1) + 3),
        )
    with jax.named_scope("conv"):
        got = lax.all_to_all(send, OUTER, 0, 0)
        names = ("into", "near_in", "turn", "near_out", "back")
        operands = [spec] + [tables[name] for name in names]
        conv = call(
            conv_body,
            blocks,
            "v" + "h" * (len(operands) + 1),
            (got, *operands),
            held(*operands, blocks) + copies_of(len(operands) + 1),
        )
        conv = lax.all_to_all(conv, OUTER, 0, 0)
    with jax.named_scope("out_weight_gather"):
        out_w = lax.all_gather(out_w.reshape(outer * inner * depth, LANES), INNER, axis=0)
    with jax.named_scope("gate"):
        own_skip = lax.dynamic_slice_in_dim(skip_gain, place * chans, chans, 0)
        gated = call(
            gate_body,
            shape((inner, tp, length, chans), BF16),
            "vhhvv",
            (conv, query, signal, own_skip.reshape(1, chans)),
            held(stream, stream) + copies_of(2),
        )
        gated = lax.all_to_all(
            gated.reshape(inner * tp, length, chans), INNER + ("tp",), 0, 0
        ).reshape(inner, tp, length, chans)
    with jax.named_scope("out_project"):
        return call(
            out_body,
            shape((length, out_weight.shape[1]), BF16),
            "vhv",
            (gated, out_w),
            held(out_w) + copies_of(inner),
        )


def solution(mesh):
    seq, tp = mesh.shape["seq"], mesh.shape["tp"]
    ways = {"y": seq // 16, "x": 4, "zl": 2, "co": 2, "tp": tp}
    fine = Mesh(mesh.devices.reshape(tuple(ways.values())), tuple(ways))
    placed = (
        P(SEQ, "tp"),
        P(),
        P(SEQ, None, "tp"),
        P(None, None, "tp"),
        P(SEQ, "tp"),
        P("tp"),
        P(SEQ, "tp"),
    )

    def run(*args):
        tokens, skip = args[0], args[5]
        inner = ways["zl"] * ways["co"]
        per = skip.shape[0] // (tp * seq)
        tables = transform_tables(tokens.shape[0], per, seq // inner, inner)
        body = functools.partial(shards, ways, tables)
        return jax.shard_map(
            body, mesh=fine, in_specs=placed, out_specs=P(SEQ, "tp"), check_vma=False
        )(*args)

    return run
```

time: 315 us -> 188 us (0.60)
  waiting for transfers between devices: 200 us -> 22 us
  Pallas kernels: 5.71 us -> 39.8 us
  blocking collectives: 51.5 us -> 76.1 us
  local copies, waits for them, and re-layouts: 15.2 us -> 5.21 us
    all_gather x2, waiting for transfers between devices: 141 us -> 0.01 us  [the longest x1 0.01 us: shards(): own = lax.all_gather(tokens, ('tp', 'zl'), axis=0)]
    all_to_all x3 -> x2, waiting for transfers between devices: 57 us -> 8.08 us  [the longest x1 8.08 us: shards(): conv = lax.all_to_all(conv, OUTER, 0, 0)]
    pallas_call x6 -> x7, Pallas kernels: 5.71 us -> 39.8 us  [call(): pl.pallas_call(body, out_shape=out_shape, in_specs=specs[:len(args)], out...]
    all_to_all x3, blocking collectives: 51.5 us -> 76.1 us  [the longest x1 30.9 us: shards(): got = lax.all_to_all(send, ('y',) + INNER, 0, 0)]
    ppermute x1 -> x7, starting transfers between devices: 2.32 us -> 22.6 us  [the longest x4 12.2 us: ring(): lax.ppermute(value, axis, [(i, (i + step) % count) for i in range(count)])]
    all_to_all x3 -> x2, starting transfers between devices: 26.3 us -> 7.2 us  [the longest x1 3.88 us: shards(): conv = lax.all_to_all(conv, OUTER, 0, 0)]
    ppermute x1 -> x7, waiting for transfers between devices: 1.27 us -> 13.2 us  [the longest x4 13.2 us: ring(): lax.ppermute(value, axis, [(i, (i + step) % count) for i in range(count)])]
    unnamed x35 -> x22, local copies, waits for them, and re-layouts: 10.2 us -> 2.99 us
  transfers between devices with their start and end apart: 6 -> 11, of which waited for: 5 -> 3; matrix products, arithmetic and copies ran while one was open for 1% -> 2% of each run, Pallas kernels for 1% -> 8%
where the time goes in v3:
time: 188 us; the launch traced here: 187 us
  blocking collectives  76.1 us (40%)
  Pallas kernels  39.8 us (21%)
  starting transfers between devices  29.8 us (16%)
  waiting for transfers between devices  22 us (12%)
  between operations  13.7 us (7%)
  local copies, waits for them, and re-layouts  5.21 us (3%)
    pallas_call x7, Pallas kernels, call(): pl.pallas_call(body, out_shape=out_shape, in_specs=specs[:len(args)], out...  39.8 us
    all_to_all x1, blocking collectives, shards(): got = lax.all_to_all(send, ('y',) + INNER, 0, 0)  30.9 us
    all_to_all x1, blocking collectives, shards(): lax.all_to_all(gated.reshape(inner * tp, length, chans), INNER + ('tp',),...  29.4 us
    all_to_all x1, blocking collectives, shards(): got = lax.all_to_all(send, OUTER, 0, 0)  15.8 us
    ppermute x4, waiting for transfers between devices, ring(): lax.ppermute(value, axis, [(i, (i + step) % count) for i in range(count)])  13.2 us
    ppermute x4, starting transfers between devices, ring(): lax.ppermute(value, axis, [(i, (i + step) % count) for i in range(count)])  12.2 us
    all_to_all x1, waiting for transfers between devices, shards(): conv = lax.all_to_all(conv, OUTER, 0, 0)  8.08 us
    ppermute x1, starting transfers between devices, swap(): return lax.ppermute(value, axis, [(0, 1), (1, 0)])  4.44 us
  transfers between devices with their start and end apart: 11, of which 3 were waited for; matrix products, arithmetic and copies ran while one was open for 2% of the time, Pallas kernels for 8%

profile of v3, /device:TPU:1, one launch (start us, length us, event | category | flops | bytes accessed | tf_op | source)
XLA Modules:
  0.0 187.2 jit_solution(1229009329077949629)
XLA Ops:
  6.5 0.7 all-gather.6.cloned.1.call-update
  7.3 2.0 %weight_gather.2 = bf16[32,5,16,128]{3,2,1,0:T(8,128)(2,1)} custom-call(bf16[3,16,512]{2,1,0:T(8,128)(2,1)} %bitcast.32, bf16[16,512]{1,0:T(8,128)(2,1)} %out_w_hbm.1, f32[128,512]{1,0:T(8,128)} %taps_hbm.1), custom_call_target="tpu_custom_call" | custom-call | tf_op jit(solution)/shard_map/weight_gather/pallas_call | solution.py:28
  9.3 30.9 %all_to_all.25.got_ref = bf16[32,5,16,128]{3,2,1,0:T(8,128)(2,1)} all-to-all(bf16[32,5,16,128]{3,2,1,0:T(8,128)(2,1)} %weight_gather.2), channel_id=1, replica_groups=mesh['y'=8,'x'=4,'zl'=2,'co'=2,'tp'=4] {'y','zl','co'}, dimensions={0} | all-to-all | bytes 1310720 | tf_op jit(solution)/shard_map/weight_gather/all_to_all | solution.py:367
  40.2 1.9 %weight_gather.3 = (bf16[32,4,16,128]{3,2,1,0:T(8,128)(2,1)}, bf16[4,8,16,128]{3,2,1,0:T(8,128)(2,1)}) custom-call(bf16[32,5,16,128]{3,2,1,0:T(8,128)(2,1)} %all_to_all.25.got_ref), custom_call_target="tpu_custom_call" | custom-call | tf_op jit(solution)/shard_map/weight_gather/pallas_call | solution.py:28
  42.1 3.8 %collective-permute-start.1 = (bf16[8,4,4,16,128]{4,3,2,1,0:T(8,128)(2,1)}, bf16[8,4,4,16,128]{4,3,2,1,0:T(8,128)(2,1)S(1)}, u32[]{:S(2)}, u32[]{:S(2)}) collective-permute-start(bf16[8,4,4,16,128]{4,3,2,1,0:T(8,128)(2,1)} %bitcast.29), channel_id=1, source_target_pairs={{0,48},{16,0},{32,16},{48,32},{1,49},{17,1},{33,17},{49,33},{2,50}... | collective-permute-start | bytes 1572872 | tf_op jit(solution)/shard_map/weight_gather/ppermute | solution.py:330
  45.9 1.9 %collective-permute-start = (bf16[8,4,4,16,128]{4,3,2,1,0:T(8,128)(2,1)}, bf16[8,4,4,16,128]{4,3,2,1,0:T(8,128)(2,1)S(1)}, u32[]{:S(2)}, u32[]{:S(2)}) collective-permute-start(bf16[8,4,4,16,128]{4,3,2,1,0:T(8,128)(2,1)} %bitcast.30), channel_id=1, source_target_pairs={{0,16},{16,32},{32,48},{48,0},{1,17},{17,33},{33,49},{49,1},{2,18}... | collective-permute-start | bytes 1572872 | tf_op jit(solution)/shard_map/weight_gather/ppermute | solution.py:330
  47.9 8.5 %collective-permute-done.1.after_hbm = bf16[8,4,4,16,128]{4,3,2,1,0:T(8,128)(2,1)S(1)} collective-permute-done((bf16[8,4,4,16,128]{4,3,2,1,0:T(8,128)(2,1)}, bf16[8,4,4,16,128]{4,3,2,1,0:T(8,128)(2,1)S(1)}, u32[]{:S(2)}, u32[]{:S(2)}) %collective-permute-start.1) | collective-permute-done | bytes 524320 | tf_op jit(solution)/shard_map/weight_gather/ppermute | solution.py:330
  56.3 4.7 %collective-permute-done.before_hbm = bf16[8,4,4,16,128]{4,3,2,1,0:T(8,128)(2,1)S(1)} collective-permute-done((bf16[8,4,4,16,128]{4,3,2,1,0:T(8,128)(2,1)}, bf16[8,4,4,16,128]{4,3,2,1,0:T(8,128)(2,1)S(1)}, u32[]{:S(2)}, u32[]{:S(2)}) %collective-permute-start) | collective-permute-done | bytes 524320 | tf_op jit(solution)/shard_map/weight_gather/ppermute | solution.py:330
  61.0 4.4 %collective-permute-start.2 = (bf16[8,128,512]{2,1,0:T(8,128)(2,1)}, bf16[8,128,512]{2,1,0:T(8,128)(2,1)S(1)}, u32[]{:S(2)}, u32[]{:S(2)}) collective-permute-start(bf16[8,128,512]{2,1,0:T(8,128)(2,1)} %bitcast.25), channel_id=1, source_target_pairs={{0,4},{4,0},{1,5},{5,1},{2,6},{6,2},{3,7},{7,3},{8,12},{12,8},{9,1... | collective-permute-start | bytes 3145736 | tf_op jit(solution)/shard_map/token_swap/ppermute | solution.py:326
  65.5 0.6 copy.18
  66.1 3.3 %all-to-all-start.1 = ((bf16[4,8,16,128]{3,2,1,0:T(8,128)(2,1)}), bf16[4,8,16,128]{3,2,1,0:T(8,128)(2,1)S(1)}, u32[]{:S(2)}, u32[]{:S(2)}) async-start(bf16[4,8,16,128]{3,2,1,0:T(8,128)(2,1)} %get-tuple-element.18), calls=%async_computation.1 | async-start | bytes 262144 | tf_op jit(solution)/shard_map/filter_points/all_to_all | solution.py:393
  69.6 4.5 %collective-permute-start.6 = (bf16[4,4,4,16,128]{4,3,2,1,0:T(8,128)(2,1)S(1)}, bf16[4,4,4,16,128]{4,3,2,1,0:T(8,128)(2,1)S(1)}, u32[]{:S(2)}, u32[]{:S(2)}) collective-permute-start(bf16[4,4,4,16,128]{4,3,2,1,0:T(8,128)(2,1)S(1)} %slice.11), channel_id=1, source_target_pairs={{0,48},{16,0},{32,16},{48,32},{1,49},{17,1},{33,17},{49,33},{2,50}... | collective-permute-start | bytes 786440 | tf_op jit(solution)/shard_map/weight_gather/ppermute | solution.py:330
  74.1 1.9 %collective-permute-start.5 = (bf16[4,4,4,16,128]{4,3,2,1,0:T(8,128)(2,1)S(1)}, bf16[4,4,4,16,128]{4,3,2,1,0:T(8,128)(2,1)S(1)}, u32[]{:S(2)}, u32[]{:S(2)}) collective-permute-start(bf16[4,4,4,16,128]{4,3,2,1,0:T(8,128)(2,1)S(1)} %slice.10), channel_id=1, source_target_pairs={{0,16},{16,32},{32,48},{48,0},{1,17},{17,33},{33,49},{49,1},{2,18}... | collective-permute-start | bytes 786440 | tf_op jit(solution)/shard_map/weight_gather/ppermute | solution.py:330
  76.0 0.8 slice_bitcast_fusion
  76.8 2.9 %collective-permute-start.4 = (bf16[4,16,512]{2,1,0:T(8,128)(2,1)S(1)}, bf16[4,16,512]{2,1,0:T(8,128)(2,1)S(1)}, u32[]{:S(2)}, u32[]{:S(2)}) collective-permute-start(bf16[4,16,512]{2,1,0:T(8,128)(2,1)S(1)} %slice_bitcast_fusion), channel_id=1, source_target_pairs={{4,16},{20,32},{36,48},{52,64},{68,80},{84,96},{100,112},{116,128}... | collective-permute-start | bytes 196616 | tf_op jit(solution)/shard_map/token_swap/ppermute | solution.py:384
  79.7 3.1 %collective-permute-start.3 = (bf16[4,16,512]{2,1,0:T(8,128)(2,1)S(1)}, bf16[4,16,512]{2,1,0:T(8,128)(2,1)S(1)}, u32[]{:S(2)}, u32[]{:S(2)}) collective-permute-start(bf16[4,16,512]{2,1,0:T(8,128)(2,1)S(1)} %slice_bitcast_fusion), channel_id=1, source_target_pairs={{0,16},{16,32},{32,48},{48,64},{64,80},{80,96},{96,112},{112,128},... | collective-permute-start | bytes 196616 | tf_op jit(solution)/shard_map/token_swap/ppermute | solution.py:383
  82.8 0.7 add_bitcast_fusion.place_ref
  83.5 0.7 copy-done.5
  84.1 3.9 %filter_points.1.spec_hbm = f32[512,256]{1,0:T(8,128)} custom-call(bf16[4,8,16,128]{3,2,1,0:T(8,128)(2,1)} %copy-done.5, bf16[1024,512]{1,0:T(8,128)(2,1)} %constant.34.clone.into_hbm, bf16[256,256]{1,0:T(8,128)(2,1)} %constant.35.clone.near_hbm.near_in_hbm, f32[2,128,128]{2,1,0:T(8,128)} %constant.36.clone.turn_hbm), custom_call_target="tpu_custom_call" | custom-call | tf_op jit(solution)/shard_map/filter_points/pallas_call | solution.py:28
  88.2 0.5 copy-done.8
  88.8 0.1 copy-done.7
  88.9 0.3 copy-done.3
  89.2 20.4 %project.1 = (f32[512,128]{1,0:T(8,128)}, f32[512,128]{1,0:T(8,128)}, bf16[32,16,128]{2,1,0:T(8,128)(2,1)}, bf16[8,4,4,16,128]{4,3,2,1,0:T(8,128)(2,1)}) custom-call(s32[1,2]{1,0:T(1,128)} %add_bitcast_fusion.place_ref, bf16[8,128,512]{2,1,0:T(8,128)(2,1)} %bitcast.27, bf16[8,128,512]{2,1,0:T(8,128)(2,1)} %copy-done.3, bf16[4,16,512]{2,1,0:T(8,128)(2,1)} %copy-done.9, ...), custom_call_target="tpu_custom_call" | custom-call | tf_op jit(solution)/shard_map/project/pallas_call | solution.py:28
  109.6 15.8 %all_to_all.26.sig_ref = bf16[32,16,128]{2,1,0:T(8,128)(2,1)} all-to-all(bf16[32,16,128]{2,1,0:T(8,128)(2,1)} %get-tuple-element.19), channel_id=1, replica_groups=mesh['y'=8,'x'=4,'zl'=2,'co'=2,'tp'=4] {'y','x'}, dimensions={0} | all-to-all | bytes 262144 | tf_op jit(solution)/shard_map/conv/all_to_all | solution.py:422
  125.4 5.1 %conv.1 = bf16[32,16,128]{2,1,0:T(8,128)(2,1)} custom-call(bf16[32,16,128]{2,1,0:T(8,128)(2,1)} %all_to_all.26.sig_ref, f32[512,256]{1,0:T(8,128)} %filter_points.1.spec_hbm, bf16[1024,512]{1,0:T(8,128)(2,1)} %constant.34.clone.into_hbm, bf16[256,256]{1,0:T(8,128)(2,1)} %constant.35.clone.near_hbm.near_in_hbm, f32[2,128,128]{2,1,0:T(8,128)} %constant.36.clone.turn_hbm, ...), custom_call_target="tpu_custom_call" | custom-call | tf_op jit(solution)/shard_map/conv/pallas_call | solution.py:28
  130.5 3.9 %all-to-all-start.3 = ((bf16[32,16,128]{2,1,0:T(8,128)(2,1)}), bf16[32,16,128]{2,1,0:T(8,128)(2,1)S(1)}, u32[]{:S(2)}, u32[]{:S(2)}) async-start(bf16[32,16,128]{2,1,0:T(8,128)(2,1)} %conv.1), calls=%async_computation.3 | async-start | bytes 262144 | tf_op jit(solution)/shard_map/conv/all_to_all | solution.py:432
  134.4 1.3 dynamic-slice_bitcast_fusion.1.skip_ref
  135.7 8.1 %all-to-all-done.3.conv_ref = bf16[32,16,128]{2,1,0:T(8,128)(2,1)S(1)} async-done(((bf16[32,16,128]{2,1,0:T(8,128)(2,1)}), bf16[32,16,128]{2,1,0:T(8,128)(2,1)S(1)}, u32[]{:S(2)}, u32[]{:S(2)}) %all-to-all-start.3) | async-done | bytes 131104 | tf_op jit(solution)/shard_map/conv/all_to_all | solution.py:432
  143.8 0.7 copy-done.4
  144.5 2.8 %gate.1 = bf16[4,4,128,128]{3,2,1,0:T(8,128)(2,1)} custom-call(bf16[32,16,128]{2,1,0:T(8,128)(2,1)} %copy-done.4, f32[512,128]{1,0:T(8,128)} %get-tuple-element.20.query_hbm, f32[512,128]{1,0:T(8,128)} %get-tuple-element.21.signal_hbm, f32[1,128]{1,0:T(1,128)} %dynamic-slice_bitcast_fusion.1.skip_ref), custom_call_target="tpu_custom_call" | custom-call | tf_op jit(solution)/shard_map/gate/pallas_call | solution.py:28
  147.3 29.4 %all_to_all.27 = bf16[16,128,128]{2,1,0:T(8,128)(2,1)} all-to-all(bf16[16,128,128]{2,1,0:T(8,128)(2,1)} %bitcast.23), channel_id=1, replica_groups=mesh['y'=8,'x'=4,'zl'=2,'co'=2,'tp'=4] {'zl','co','tp'}, dimensions={0} | all-to-all | bytes 1048576 | tf_op jit(solution)/shard_map/gate/all_to_all | solution.py:444
  176.7 3.7 %out_project.1 = bf16[128,512]{1,0:T(8,128)(2,1)} custom-call(bf16[4,4,128,128]{3,2,1,0:T(8,128)(2,1)} %bitcast.24, bf16[4,2048,128]{2,1,0:T(8,128)(2,1)} %all-gather.4.cloned.1.call-done.w_hbm), custom_call_target="tpu_custom_call" | custom-call | tf_op jit(solution)/shard_map/out_project/pallas_call | solution.py:28
  (29 shorter events, 0.3 us)
Async XLA Ops:
  6.5 59.0 %copy-start = (f32[3,3,512]{2,1,0:T(4,128)S(1)}, f32[3,3,512]{2,1,0:T(4,128)}, u32[]{:S(2)}) copy-start(f32[3,3,512]{2,1,0:T(4,128)} %param.15) | copy-start | bytes 55300
  6.5 54.5 %all-gather.6.cloned.1.call-start = ((), (), s32[]{:S(2)}) async-start(), calls=%async_computation.6 | async-start | bytes 1179648 | tf_op jit(solution)/shard_map/token_gather/all_gather | solution.py:356
  42.1 14.2 %collective-permute-start.1 = (bf16[8,4,4,16,128]{4,3,2,1,0:T(8,128)(2,1)}, bf16[8,4,4,16,128]{4,3,2,1,0:T(8,128)(2,1)S(1)}, u32[]{:S(2)}, u32[]{:S(2)}) collective-permute-start(bf16[8,4,4,16,128]{4,3,2,1,0:T(8,128)(2,1)} %bitcast.29), channel_id=1, source_target_pairs={{0,48},{16,0},{32,16},{48,32},{1,49},{17,1},{33,17},{49,33},{2,50}... | collective-permute-start | bytes 1572872 | tf_op jit(solution)/shard_map/weight_gather/ppermute | solution.py:330
  45.9 15.1 %collective-permute-start = (bf16[8,4,4,16,128]{4,3,2,1,0:T(8,128)(2,1)}, bf16[8,4,4,16,128]{4,3,2,1,0:T(8,128)(2,1)S(1)}, u32[]{:S(2)}, u32[]{:S(2)}) collective-permute-start(bf16[8,4,4,16,128]{4,3,2,1,0:T(8,128)(2,1)} %bitcast.30), channel_id=1, source_target_pairs={{0,16},{16,32},{32,48},{48,0},{1,17},{17,33},{33,49},{49,1},{2,18}... | collective-permute-start | bytes 1572872 | tf_op jit(solution)/shard_map/weight_gather/ppermute | solution.py:330
  56.3 31.8 %copy-start.1 = (bf16[8,4,4,16,128]{4,3,2,1,0:T(8,128)(2,1)}, bf16[8,4,4,16,128]{4,3,2,1,0:T(8,128)(2,1)S(1)}, u32[]{:S(2)}) copy-start(bf16[8,4,4,16,128]{4,3,2,1,0:T(8,128)(2,1)S(1)} %collective-permute-done.1.after_hbm) | copy-start | bytes 1572868
  61.0 27.1 %copy-start.2 = (bf16[8,4,4,16,128]{4,3,2,1,0:T(8,128)(2,1)}, bf16[8,4,4,16,128]{4,3,2,1,0:T(8,128)(2,1)S(1)}, u32[]{:S(2)}) copy-start(bf16[8,4,4,16,128]{4,3,2,1,0:T(8,128)(2,1)S(1)} %collective-permute-done.before_hbm) | copy-start | bytes 1572868
  61.0 27.1 %collective-permute-start.2 = (bf16[8,128,512]{2,1,0:T(8,128)(2,1)}, bf16[8,128,512]{2,1,0:T(8,128)(2,1)S(1)}, u32[]{:S(2)}, u32[]{:S(2)}) collective-permute-start(bf16[8,128,512]{2,1,0:T(8,128)(2,1)} %bitcast.25), channel_id=1, source_target_pairs={{0,4},{4,0},{1,5},{5,1},{2,6},{6,2},{3,7},{7,3},{8,12},{12,8},{9,1... | collective-permute-start | bytes 3145736 | tf_op jit(solution)/shard_map/token_swap/ppermute | solution.py:326
  66.1 17.4 %all-to-all-start.1 = ((bf16[4,8,16,128]{3,2,1,0:T(8,128)(2,1)}), bf16[4,8,16,128]{3,2,1,0:T(8,128)(2,1)S(1)}, u32[]{:S(2)}, u32[]{:S(2)}) async-start(bf16[4,8,16,128]{3,2,1,0:T(8,128)(2,1)} %get-tuple-element.18), calls=%async_computation.1 | async-start | bytes 262144 | tf_op jit(solution)/shard_map/filter_points/all_to_all | solution.py:393
  69.5 107.2 %all-gather.4.cloned.1.call-start = ((), (), s32[]{:S(2)}) async-start(), calls=%async_computation.5 | async-start | bytes 2621440 | tf_op jit(solution)/shard_map/out_weight_gather/all_gather | solution.py:434
  69.6 18.5 %collective-permute-start.6 = (bf16[4,4,4,16,128]{4,3,2,1,0:T(8,128)(2,1)S(1)}, bf16[4,4,4,16,128]{4,3,2,1,0:T(8,128)(2,1)S(1)}, u32[]{:S(2)}, u32[]{:S(2)}) collective-permute-start(bf16[4,4,4,16,128]{4,3,2,1,0:T(8,128)(2,1)S(1)} %slice.11), channel_id=1, source_target_pairs={{0,48},{16,0},{32,16},{48,32},{1,49},{17,1},{33,17},{49,33},{2,50}... | collective-permute-start | bytes 786440 | tf_op jit(solution)/shard_map/weight_gather/ppermute | solution.py:330
  74.1 14.0 %collective-permute-start.5 = (bf16[4,4,4,16,128]{4,3,2,1,0:T(8,128)(2,1)S(1)}, bf16[4,4,4,16,128]{4,3,2,1,0:T(8,128)(2,1)S(1)}, u32[]{:S(2)}, u32[]{:S(2)}) collective-permute-start(bf16[4,4,4,16,128]{4,3,2,1,0:T(8,128)(2,1)S(1)} %slice.10), channel_id=1, source_target_pairs={{0,16},{16,32},{32,48},{48,0},{1,17},{17,33},{33,49},{49,1},{2,18}... | collective-permute-start | bytes 786440 | tf_op jit(solution)/shard_map/weight_gather/ppermute | solution.py:330
  76.8 11.2 %collective-permute-start.4 = (bf16[4,16,512]{2,1,0:T(8,128)(2,1)S(1)}, bf16[4,16,512]{2,1,0:T(8,128)(2,1)S(1)}, u32[]{:S(2)}, u32[]{:S(2)}) collective-permute-start(bf16[4,16,512]{2,1,0:T(8,128)(2,1)S(1)} %slice_bitcast_fusion), channel_id=1, source_target_pairs={{4,16},{20,32},{36,48},{52,64},{68,80},{84,96},{100,112},{116,128}... | collective-permute-start | bytes 196616 | tf_op jit(solution)/shard_map/token_swap/ppermute | solution.py:384
  79.7 8.3 %collective-permute-start.3 = (bf16[4,16,512]{2,1,0:T(8,128)(2,1)S(1)}, bf16[4,16,512]{2,1,0:T(8,128)(2,1)S(1)}, u32[]{:S(2)}, u32[]{:S(2)}) collective-permute-start(bf16[4,16,512]{2,1,0:T(8,128)(2,1)S(1)} %slice_bitcast_fusion), channel_id=1, source_target_pairs={{0,16},{16,32},{32,48},{48,64},{64,80},{80,96},{96,112},{112,128},... | collective-permute-start | bytes 196616 | tf_op jit(solution)/shard_map/token_swap/ppermute | solution.py:383
  83.5 0.7 copy-start.5
  88.0 0.6 copy-start.8
  88.1 0.6 copy-start.9
  88.1 0.7 copy-start.6
  88.1 0.8 copy-start.7
  88.1 1.1 copy-start.3
  130.5 13.3 %all-to-all-start.3 = ((bf16[32,16,128]{2,1,0:T(8,128)(2,1)}), bf16[32,16,128]{2,1,0:T(8,128)(2,1)S(1)}, u32[]{:S(2)}, u32[]{:S(2)}) async-start(bf16[32,16,128]{2,1,0:T(8,128)(2,1)} %conv.1), calls=%async_computation.3 | async-start | bytes 262144 | tf_op jit(solution)/shard_map/conv/all_to_all | solution.py:432
  143.8 0.7 copy-start.4
Sparse Core Ops, SparseCore 0:
  9.4 44.6 all-gather.5
  109.8 34.6 all-gather.3

commit v4 on v2

v4 whole, which is shorter than its diff:
```python
import functools
import math

import jax
import jax.numpy as jnp
import numpy as np
from jax import lax
from jax.experimental import pallas as pl
from jax.experimental.pallas import tpu as pltpu
from jax.sharding import Mesh
from jax.sharding import PartitionSpec as P

F32 = jnp.float32
BF16 = jnp.bfloat16
LANES = 128
HALO = 16
MIB = 1024 * 1024
OUTER = ("y", "x")
INNER = ("zl", "co")
SEQ = OUTER + INNER


def call(body, out_shape, places, args, scratch=(), limit=16):
    spaces = {"h": pltpu.HBM, "v": pltpu.VMEM, "s": pltpu.SMEM}
    specs = [pl.BlockSpec(memory_space=spaces[place]) for place in places]
    single = not isinstance(out_shape, tuple)
    outs = specs[len(args) :]
    return pl.pallas_call(
        body,
        out_shape=out_shape,
        in_specs=specs[: len(args)],
        out_specs=outs[0] if single else tuple(outs),
        scratch_shapes=scratch,
        compiler_params=pltpu.CompilerParams(vmem_limit_bytes=limit * MIB),
    )(*args)


def started(pairs, sems, first=0):
    copies = [
        pltpu.make_async_copy(source, target, sems.at[first + k])
        for k, (source, target) in enumerate(pairs)
    ]
    for copy in copies:
        copy.start()
    return copies


def finish(copies):
    for copy in copies:
        copy.wait()


def transform_tables(length, chans, outer, inner):
    blocks = length // LANES
    row = np.arange(blocks)
    lane = np.arange(LANES)
    far = np.exp(-2j * np.pi * (row[:, None] * (4 * row[None, :] + 1) % (4 * blocks)) / (4 * blocks))
    near = np.exp(-2j * np.pi * (lane[:, None] * lane[None, :] % LANES) / LANES)
    turn = np.exp(-2j * np.pi * ((4 * row[:, None] + 1) * lane[None, :] % (4 * length)) / (4 * length))
    eye = np.eye(chans)
    into = np.einsum("bf,cd->cfbd", far, eye).reshape(chans * blocks, blocks * chans)
    into = np.concatenate([into.real, into.imag], axis=0)
    back = np.einsum("bf,cd->bdcf", far.conj(), eye).reshape(blocks * chans, chans * blocks) / length
    back = np.concatenate([back.real, -back.imag], axis=1)
    near_in = np.block([[near.real, near.imag], [-near.imag, near.real]])
    near_out = np.block([[near.real, -near.imag], [near.imag, near.real]])
    turn = np.stack([turn.real, turn.imag])
    as_short = lambda table: jnp.asarray(table.astype(np.float32)).astype(BF16)
    return {
        "into": as_short(into),
        "back": as_short(back),
        "near_in": as_short(near_in),
        "near_out": as_short(near_out),
        "turn": jnp.asarray(turn.astype(np.float32)),
    }


def times(real, imag, cos, sin):
    return real * cos - imag * sin, real * sin + imag * cos


def turned(pair, turn_ref, sign, axis):
    chans = pair[0].shape[0] // turn_ref.shape[1]
    cos = jnp.concatenate([turn_ref[0]] * chans, axis=0)
    sin = jnp.concatenate([turn_ref[1]] * chans, axis=0) * sign
    return jnp.concatenate(times(*pair, cos, sin), axis=axis).astype(BF16)


def halves(value, axis):
    half = value.shape[axis] // 2
    return lax.slice_in_dim(value, 0, half, axis=axis), lax.slice_in_dim(value, half, 2 * half, axis=axis)


def conv_body(sig_ref, taps_ref, into_ref, near_in_ref, turn_ref, near_out_ref, back_ref, out_ref):
    groups, rows, lanes = sig_ref.shape
    both = jnp.concatenate([sig_ref[...].reshape(groups * rows, lanes), taps_ref[...]], axis=1)
    far = halves(jnp.dot(into_ref[...], both, preferred_element_type=F32), 0)
    sides = [(far[0][:, :lanes], far[1][:, :lanes]), (far[0][:, lanes:], far[1][:, lanes:])]
    pair = jnp.concatenate([turned(side, turn_ref, 1.0, 1) for side in sides], axis=0)
    points = halves(jnp.dot(pair, near_in_ref[...], preferred_element_type=F32), 0)
    product = times(*halves(points[0], 1), *halves(points[1], 1))
    pair = jnp.concatenate(product, axis=1).astype(BF16)
    near = jnp.dot(pair, near_out_ref[...], preferred_element_type=F32)
    pair = turned(halves(near, 1), turn_ref, -1.0, 0)
    result = jnp.dot(back_ref[...], pair, preferred_element_type=F32)
    out_ref[...] = result.astype(BF16).reshape(groups, rows, lanes)


def pack_body(weight_hbm, out_w_hbm, taps_hbm, send_hbm, weight_ref, out_w_ref, taps_ref, send_ref, sems):
    copies = started([(taps_hbm, taps_ref), (weight_hbm, weight_ref), (out_w_hbm, out_w_ref)], sems)
    parts = weight_ref.shape[0]
    total, _, rows, lanes = send_ref.shape
    inner = out_w_ref.shape[1] // lanes
    ways = total // inner
    copies[0].wait()
    for s in range(inner):
        taps = taps_ref[:, s * lanes : (s + 1) * lanes].T.reshape(ways, rows, lanes).astype(BF16)
        for way in range(ways):
            send_ref[way * inner + s, parts + 1] = taps[way]
    finish(copies[1:])
    for s in range(inner):
        at = slice(s * lanes, (s + 1) * lanes)
        for way in range(ways):
            for part in range(parts):
                send_ref[way * inner + s, part] = weight_ref[part, :, at]
            send_ref[way * inner + s, parts] = out_w_ref[:, at]
    finish(started([(send_ref, send_hbm)], sems, len(copies)))


def repack_body(got_ref, send_ref):
    sources, kinds, rows, lanes = got_ref.shape
    ways, tiles = send_ref.shape[0], send_ref.shape[1]
    parts = kinds - 1
    taps = got_ref[:, parts].astype(F32)
    per = rows // ways
    for way in range(ways):
        for part in range(parts):
            send_ref[way, part * sources : (part + 1) * sources] = got_ref[:, part]
        piece = taps[:, way * per : (way + 1) * per].reshape(tiles - parts * sources, rows, lanes)
        send_ref[way, parts * sources :] = piece.astype(BF16)


def project_body(
    cores,
    place_ref,
    own_ref,
    other_ref,
    halo_own_ref,
    halo_other_ref,
    gain_ref,
    taps_ref,
    skip_ref,
    got_ref,
    gates_ref,
    send_ref,
    out_w_ref,
    filter_ref,
    x_ref,
    proj_ref,
):
    core = place_ref[0, 0]
    parts = 3
    ways, _, rows, lanes = got_ref.shape
    groups = send_ref.shape[0]
    outer = groups // ways
    count, chans = gates_ref.shape[0], gates_ref.shape[1] // 2
    inner = count // lanes
    sources = outer * inner

    def column(part):
        pieces = [
            got_ref[x, part * sources + y * inner : part * sources + (y + 1) * inner].reshape(
                inner * rows, lanes
            )
            for y in range(outer)
            for x in range(ways)
        ]
        return jnp.concatenate(pieces, axis=0)

    out_w_ref[...] = column(parts)
    first = (parts + 1) * sources
    for y in range(outer):
        for x in range(ways):
            at = (y * ways + x) * rows
            filter_ref[at : at + rows] = got_ref[x, first + y]

    blocks, length, feats = own_ref.shape
    tp = x_ref.shape[1] // feats

    def put(pieces, at):
        total = sum(jnp.sum(piece * piece, axis=1, keepdims=True) for piece in pieces)
        scale = lax.rsqrt(total / (tp * feats) + 1e-05)
        for p, piece in enumerate(pieces):
            gain = gain_ref[:, p * feats : (p + 1) * feats]
            x_ref[at, p * feats : (p + 1) * feats] = (piece * scale * gain).astype(BF16)

    zs = blocks // tp
    for ref, at_core in ((own_ref, core), (other_ref, cores - 1 - core)):
        for z in range(zs):
            at = pl.multiple_of(HALO + (z * cores + at_core) * length, HALO)
            put([ref[p * zs + z].astype(F32) for p in range(tp)], pl.ds(at, length))
    last = core == cores - 1
    put(
        [jnp.where(last, halo_own_ref[p].astype(F32), halo_other_ref[p].astype(F32)) for p in range(tp)],
        slice(0, HALO),
    )
    weight = jnp.concatenate([column(part) for part in range(parts)], axis=1)
    proj = jnp.dot(x_ref[...], weight, preferred_element_type=F32)
    proj_ref[...] = proj.astype(BF16).astype(F32)

    short = taps_ref[0:1] * proj_ref[HALO:]
    for lag in range(1, taps_ref.shape[0]):
        short = short + taps_ref[lag : lag + 1] * proj_ref[HALO - lag : HALO - lag + count]
    signal = short[:, chans : 2 * chans] * short[:, 2 * chans :]
    gates_ref[:, :chans] = short[:, :chans]
    gates_ref[:, chans:] = skip_ref[...] * signal
    per = send_ref.shape[1] // inner
    pieces = [signal[b * lanes : (b + 1) * lanes].T.reshape(groups, per, lanes) for b in range(inner)]
    send_ref[...] = jnp.concatenate(pieces, axis=1).astype(BF16)


def gate_body(conv_ref, gates_ref, out_ref):
    groups, rows, lanes = conv_ref.shape
    inner = gates_ref.shape[0] // lanes
    per = rows // inner
    chans = groups * per
    conv = conv_ref[...].astype(F32)
    for b in range(inner):
        piece = conv[:, b * per : (b + 1) * per].reshape(chans, lanes).T
        at = slice(b * lanes, (b + 1) * lanes)
        gated = (gates_ref[at, :chans] * (piece + gates_ref[at, chans:])).astype(BF16)
        for p in range(out_ref.shape[1]):
            out_ref[b, p] = gated


def out_body(place_ref, gated_ref, own_ref, near_ref, across_ref, far_ref, out_ref):
    place = place_ref[0, 0]
    inner, tp, rows, chans = gated_ref.shape
    x = jnp.concatenate([gated_ref[s, p] for p in range(tp) for s in range(inner)], axis=1)
    weight = jnp.concatenate([own_ref[...], near_ref[...], across_ref[...], far_ref[...]], axis=1)
    out = jnp.dot(x, weight, preferred_element_type=F32).astype(BF16)
    for k, flip in enumerate((0, 2, 1, 3)):
        at = pl.multiple_of((place ^ flip) * chans, chans)
        out_ref[:, pl.ds(at, chans)] = out[:, k * chans : (k + 1) * chans]


def shape(dims, dtype):
    return jax.ShapeDtypeStruct(dims, dtype)


def swap(value, axis):
    return lax.ppermute(value, axis, [(0, 1), (1, 0)])


def held(*arrays):
    return [pltpu.VMEM(array.shape, array.dtype) for array in arrays]


def copies_of(count):
    return [pltpu.SemaphoreType.DMA((count,))]


def shards(ways, tables, tokens, norm_gain, in_weight, short_taps, filter_response, skip_gain, out_weight):
    along, across = ways["y"], ways["x"]
    outer = along * across
    cores = ways["co"]
    inner = ways["zl"] * cores
    tp = ways["tp"]
    length, feats = tokens.shape
    chans = skip_gain.shape[0] // inner
    per = chans // outer
    depth, parts = in_weight.shape[0], in_weight.shape[1]
    rows = inner * per
    place = lax.axis_index(INNER)
    where = jnp.stack([lax.axis_index("co"), lax.axis_index("x")]).astype(jnp.int32).reshape(1, 2)

    with jax.named_scope("token_gather"):
        own = lax.all_gather(tokens, ("tp", "zl"), axis=0)
    with jax.named_scope("weight_gather"):
        kinds = parts + 2
        first = shape((along * inner, kinds, depth, LANES), BF16)
        weight = in_weight.transpose(1, 0, 2)
        send = call(
            pack_body,
            first,
            "hhhh",
            (weight, out_weight, filter_response),
            held(weight, out_weight, filter_response, first) + copies_of(4),
            limit=60,
        )
        got = lax.all_to_all(send, ("y",) + INNER, 0, 0)
        tiles = (kinds - 1) * along * inner + along
        send = call(repack_body, shape((across, tiles, depth, LANES), BF16), "vv", (got,), limit=56)
        got = lax.all_to_all(send, "x", 0, 0)
    with jax.named_scope("token_swap"):
        own, _ = lax.optimization_barrier((own, send))
        other = swap(own, "co")
        tail = own.reshape(tp, ways["zl"], length, feats)[:, -1, length - HALO :]
        halo_own = lax.ppermute(tail, OUTER, [(i, i + 1) for i in range(outer - 1)])
        halo_other = lax.ppermute(
            tail,
            OUTER + ("co",),
            [(i * cores + cores - 1, (i + 1) * cores) for i in range(outer - 1)],
        )
    with jax.named_scope("project"):
        own_taps = lax.dynamic_slice_in_dim(short_taps, place * chans, chans, 2)
        own_taps = own_taps.reshape(short_taps.shape[0], parts * chans)
        own_skip = lax.dynamic_slice_in_dim(skip_gain, place * chans, chans, 0).reshape(1, chans)
        blocks = shape((outer, rows, LANES), BF16)
        wide = shape((HALO + inner * length, tp * feats), BF16)
        proj = shape((HALO + inner * length, parts * chans), F32)
        gates, send, out_w, taps = call(
            functools.partial(project_body, cores),
            (
                shape((inner * length, 2 * chans), F32),
                blocks,
                shape((outer * inner * depth, chans), BF16),
                shape((outer * rows, LANES), BF16),
            ),
            "s" + "v" * 12,
            (where[:, :1], own, other, halo_own, halo_other)
            + (norm_gain.reshape(1, tp * feats), own_taps, own_skip, got),
            held(wide, proj),
        )
    with jax.named_scope("conv"):
        got = lax.all_to_all(send, OUTER, 0, 0)
        names = ("into", "near_in", "turn", "near_out", "back")
        operands = (got, taps) + tuple(tables[name] for name in names)
        conv = call(conv_body, blocks, "v" * (len(operands) + 1), operands)
        conv = lax.all_to_all(conv, OUTER, 0, 0)
    with jax.named_scope("out_weight_swap"):
        near_w = swap(out_w, "zl")
        across_w = swap(out_w, "co"), swap(near_w, "co")
    with jax.named_scope("gate"):
        gated = call(gate_body, shape((inner, tp, length, chans), BF16), "vvv", (conv, gates))
        gated = lax.all_to_all(
            gated.reshape(inner * tp, length, chans), INNER + ("tp",), 0, 0
        ).reshape(inner, tp, length, chans)
    with jax.named_scope("out_project"):
        return call(
            out_body,
            shape((length, out_weight.shape[1]), BF16),
            "svvvvvv",
            (place.astype(jnp.int32).reshape(1, 1), gated, out_w, near_w, *across_w),
        )


def solution(mesh):
    seq, tp = mesh.shape["seq"], mesh.shape["tp"]
    ways = {"y": seq // 16, "x": 4, "zl": 2, "co": 2, "tp": tp}
    fine = Mesh(mesh.devices.reshape(tuple(ways.values())), tuple(ways))
    placed = (
        P(SEQ, "tp"),
        P(),
        P(SEQ, None, "tp"),
        P(None, None, "tp"),
        P(SEQ, "tp"),
        P("tp"),
        P(SEQ, "tp"),
    )

    def run(*args):
        tokens, skip = args[0], args[5]
        inner = ways["zl"] * ways["co"]
        per = skip.shape[0] // (tp * seq)
        tables = transform_tables(tokens.shape[0], per, seq // inner, inner)
        body = functools.partial(shards, ways, tables)
        return jax.shard_map(
            body, mesh=fine, in_specs=placed, out_specs=P(SEQ, "tp"), check_vma=False
        )(*args)

    return run
```

time: 176 us -> 154 us (0.88)
  local copies, waits for them, and re-layouts: 22.3 us -> 5.33 us
  blocking collectives: 24.7 us -> 21 us
  Pallas kernels: 9.7 us -> 11.7 us
  starting transfers between devices: 46.7 us -> 44.7 us
    unnamed x54 -> x28, local copies, waits for them, and re-layouts: 20.7 us -> 3.72 us
    all_gather x1, waiting for transfers between devices: 26.9 us -> 16.6 us  [shards(): own = lax.all_gather(tokens, ('tp', 'zl'), axis=0)]
    all_to_all x1, waiting for transfers between devices: 6.75 us -> 11.2 us  [shards(): lax.all_to_all(gated.reshape(inner * tp, length, chans), INNER + ('tp',),...]
    all_to_all x1, waiting for transfers between devices: 3.15 us -> 7.04 us  [shards(): conv = lax.all_to_all(conv, OUTER, 0, 0)]
    all_to_all x1, blocking collectives: 24.7 us -> 21 us  [shards(): got = lax.all_to_all(send, OUTER, 0, 0)]
    all_to_all x1, starting transfers between devices: 9.29 us -> 6.26 us  [shards(): lax.all_to_all(gated.reshape(inner * tp, length, chans), INNER + ('tp',),...]
    pallas_call x9 -> x6, Pallas kernels: 9.7 us -> 11.7 us  [call(): pl.pallas_call(body, out_shape=out_shape, in_specs=specs[:len(args)], out...]
    ppermute x3 -> x4, starting transfers between devices: 13.2 us -> 13.7 us  [swap(): return lax.ppermute(value, axis, [(0, 1), (1, 0)])]
  transfers between devices with their start and end apart: 10 -> 11, of which waited for: 4 -> 6; matrix products, arithmetic and copies ran while one was open for 2% -> 1% of each run, Pallas kernels for 2% -> 2%
where the time goes in v4:
time: 154 us
  waiting for transfers between devices  57.2 us (37%)
  starting transfers between devices  44.7 us (29%)
  blocking collectives  21 us (14%)
  between operations  13.6 us (9%)
  Pallas kernels  11.7 us (8%)
  local copies, waits for them, and re-layouts  5.33 us (3%)
    all_to_all x1, blocking collectives, shards(): got = lax.all_to_all(send, OUTER, 0, 0)  21 us
    all_to_all x1, waiting for transfers between devices, shards(): got = lax.all_to_all(send, ('y',) + INNER, 0, 0)  18.9 us
    all_gather x1, waiting for transfers between devices, shards(): own = lax.all_gather(tokens, ('tp', 'zl'), axis=0)  16.6 us
    ppermute x4, starting transfers between devices, swap(): return lax.ppermute(value, axis, [(0, 1), (1, 0)])  13.7 us
    pallas_call x6, Pallas kernels, call(): pl.pallas_call(body, out_shape=out_shape, in_specs=specs[:len(args)], out...  11.7 us
    all_to_all x1, waiting for transfers between devices, shards(): lax.all_to_all(gated.reshape(inner * tp, length, chans), INNER + ('tp',),...  11.2 us
    all_to_all x1, starting transfers between devices, shards(): got = lax.all_to_all(send, ('y',) + INNER, 0, 0)  10.6 us
    all_to_all x1, waiting for transfers between devices, shards(): conv = lax.all_to_all(conv, OUTER, 0, 0)  7.04 us
  transfers between devices with their start and end apart: 11, of which 6 were waited for; matrix products, arithmetic and copies ran while one was open for 1% of the time, Pallas kernels for 2%

profile of v4, /device:TPU:1, one launch (start us, length us, event | category | flops | bytes accessed | tf_op | source)
XLA Modules:
  0.0 153.6 jit_solution(15419769766676209640)
XLA Ops:
  6.5 2.0 %weight_gather.2 = bf16[32,5,16,128]{3,2,1,0:T(8,128)(2,1)} custom-call(bf16[3,16,512]{2,1,0:T(8,128)(2,1)} %bitcast.30, bf16[16,512]{1,0:T(8,128)(2,1)} %out_w_hbm.1, f32[128,512]{1,0:T(8,128)} %taps_hbm.1), custom_call_target="tpu_custom_call" | custom-call | tf_op jit(solution)/shard_map/weight_gather/pallas_call | solution.py:28
  8.6 10.6 %all-to-all-start = ((bf16[32,5,16,128]{3,2,1,0:T(8,128)(2,1)}), bf16[32,5,16,128]{3,2,1,0:T(8,128)(2,1)S(1)}, u32[]{:S(2)}, u32[]{:S(2)}) async-start(bf16[32,5,16,128]{3,2,1,0:T(8,128)(2,1)} %weight_gather.2), calls=%async_computation | async-start | bytes 1310720 | tf_op jit(solution)/shard_map/weight_gather/all_to_all | solution.py:291
  19.1 0.0 all-gather.3.cloned.1.call-start
  19.2 0.7 all-gather.3.cloned.1.call-update
  19.9 18.9 %all-to-all-done.got_ref = bf16[32,5,16,128]{3,2,1,0:T(8,128)(2,1)S(1)} async-done(((bf16[32,5,16,128]{3,2,1,0:T(8,128)(2,1)}), bf16[32,5,16,128]{3,2,1,0:T(8,128)(2,1)S(1)}, u32[]{:S(2)}, u32[]{:S(2)}) %all-to-all-start) | async-done | bytes 655392 | tf_op jit(solution)/shard_map/weight_gather/all_to_all | solution.py:291
  38.8 0.8 copy-done.12
  39.6 2.6 %weight_gather.3 = bf16[4,136,16,128]{3,2,1,0:T(8,128)(2,1)} custom-call(bf16[32,5,16,128]{3,2,1,0:T(8,128)(2,1)} %copy-done.12), custom_call_target="tpu_custom_call" | custom-call | tf_op jit(solution)/shard_map/weight_gather/pallas_call | solution.py:28
  42.2 4.1 %all-to-all-start.1 = ((bf16[4,136,16,128]{3,2,1,0:T(8,128)(2,1)}), bf16[4,136,16,128]{3,2,1,0:T(8,128)(2,1)S(1)}, u32[]{:S(2)}, u32[]{:S(2)}) async-start(bf16[4,136,16,128]{3,2,1,0:T(8,128)(2,1)} %weight_gather.3), calls=%async_computation.1 | async-start | bytes 4456448 | tf_op jit(solution)/shard_map/weight_gather/all_to_all | solution.py:294
  46.4 16.6 %all-gather.3.cloned.1.call-done = bf16[1024,512]{1,0:T(8,128)(2,1)} async-done(((bf16[128,512]{1,0:T(8,128)(2,1)}), bf16[1024,512]{1,0:T(8,128)(2,1)}) %all-gather.3.cloned.1.call-update) | async-done | bytes 1048592 | tf_op jit(solution)/shard_map/token_gather/all_gather | solution.py:278
  63.0 7.0 %collective-permute-start = (bf16[8,128,512]{2,1,0:T(8,128)(2,1)}, bf16[8,128,512]{2,1,0:T(8,128)(2,1)S(1)}, u32[]{:S(2)}, u32[]{:S(2)}) collective-permute-start(bf16[8,128,512]{2,1,0:T(8,128)(2,1)} %bitcast.24), channel_id=1, source_target_pairs={{0,4},{4,0},{1,5},{5,1},{2,6},{6,2},{3,7},{7,3},{8,12},{12,8},{9,1... | collective-permute-start | bytes 3145736 | tf_op jit(solution)/shard_map/token_swap/ppermute | solution.py:252
  70.1 0.8 dynamic-slice_bitcast_fusion.1.skip_ref
  70.9 0.8 slice_bitcast_fusion
  71.7 3.0 %collective-permute-start.2 = (bf16[4,16,512]{2,1,0:T(8,128)(2,1)S(1)}, bf16[4,16,512]{2,1,0:T(8,128)(2,1)S(1)}, u32[]{:S(2)}, u32[]{:S(2)}) collective-permute-start(bf16[4,16,512]{2,1,0:T(8,128)(2,1)S(1)} %slice_bitcast_fusion), channel_id=1, source_target_pairs={{4,16},{20,32},{36,48},{52,64},{68,80},{84,96},{100,112},{116,128}... | collective-permute-start | bytes 196616 | tf_op jit(solution)/shard_map/token_swap/ppermute | solution.py:300
  74.7 3.1 %collective-permute-start.1 = (bf16[4,16,512]{2,1,0:T(8,128)(2,1)S(1)}, bf16[4,16,512]{2,1,0:T(8,128)(2,1)S(1)}, u32[]{:S(2)}, u32[]{:S(2)}) collective-permute-start(bf16[4,16,512]{2,1,0:T(8,128)(2,1)S(1)} %slice_bitcast_fusion), channel_id=1, source_target_pairs={{0,16},{16,32},{32,48},{48,64},{64,80},{80,96},{96,112},{112,128},... | collective-permute-start | bytes 196616 | tf_op jit(solution)/shard_map/token_swap/ppermute | solution.py:299
  77.8 0.1 add_bitcast_fusion
  77.9 1.2 collective-permute-done.1.halo_own_ref
  79.2 1.2 copy-done.1
  80.4 2.6 %project.1 = (f32[512,256]{1,0:T(8,128)S(1)}, bf16[32,16,128]{2,1,0:T(8,128)(2,1)S(1)}, bf16[2048,128]{1,0:T(8,128)(2,1)S(1)}, bf16[512,128]{1,0:T(8,128)(2,1)S(1)}) custom-call(s32[1,1]{1,0:T(1,128)S(1)} %bitcast.29, bf16[8,128,512]{2,1,0:T(8,128)(2,1)S(1)} %bitcast.26, bf16[8,128,512]{2,1,0:T(8,128)(2,1)S(1)} %collective-permute-done.other_ref, ...), custom_call_target="tpu_custom_call" | custom-call | tf_op jit(solution)/shard_map/project/pallas_call | solution.py:28
  83.0 0.8 copy-done.4
  83.9 0.8 copy-done.6
  84.7 21.0 %all_to_all.25.sig_ref = bf16[32,16,128]{2,1,0:T(8,128)(2,1)S(1)} all-to-all(bf16[32,16,128]{2,1,0:T(8,128)(2,1)S(1)} %get-tuple-element.11), channel_id=1, replica_groups=mesh['y'=8,'x'=4,'zl'=2,'co'=2,'tp'=4] {'y','x'}, dimensions={0} | all-to-all | bytes 262144 | tf_op jit(solution)/shard_map/conv/all_to_all | solution.py:326
  105.7 2.3 %conv.1 = bf16[32,16,128]{2,1,0:T(8,128)(2,1)} custom-call(bf16[32,16,128]{2,1,0:T(8,128)(2,1)S(1)} %all_to_all.25.sig_ref, bf16[512,128]{1,0:T(8,128)(2,1)S(1)} %get-tuple-element.12.taps_ref, bf16[1024,512]{1,0:T(8,128)(2,1)S(1)} %copy-done.3, bf16[256,256]{1,0:T(8,128)(2,1)S(1)} %copy-done.10, f32[2,128,128]{2,1,0:T(8,128)S(1)} %copy-done.9, ...), custom_call_target="tpu_custom_call" | custom-call | tf_op jit(solution)/shard_map/conv/pallas_call | solution.py:28
  108.1 3.9 %all-to-all-start.3 = ((bf16[32,16,128]{2,1,0:T(8,128)(2,1)}), bf16[32,16,128]{2,1,0:T(8,128)(2,1)S(1)}, u32[]{:S(2)}, u32[]{:S(2)}) async-start(bf16[32,16,128]{2,1,0:T(8,128)(2,1)} %conv.1), calls=%async_computation.3 | async-start | bytes 262144 | tf_op jit(solution)/shard_map/conv/all_to_all | solution.py:330
  111.9 2.3 %collective-permute-start.3 = (bf16[2048,128]{1,0:T(8,128)(2,1)S(1)}, bf16[2048,128]{1,0:T(8,128)(2,1)S(1)}, u32[]{:S(2)}, u32[]{:S(2)}) collective-permute-start(bf16[2048,128]{1,0:T(8,128)(2,1)S(1)} %copy-done.7), channel_id=1, source_target_pairs={{0,8},{8,0},{1,9},{9,1},{2,10},{10,2},{3,11},{11,3},{4,12},{12,4},... | collective-permute-start | bytes 1572872 | tf_op jit(solution)/shard_map/out_weight_swap/ppermute | solution.py:252
  114.3 7.0 %all-to-all-done.3.conv_ref = bf16[32,16,128]{2,1,0:T(8,128)(2,1)S(1)} async-done(((bf16[32,16,128]{2,1,0:T(8,128)(2,1)}), bf16[32,16,128]{2,1,0:T(8,128)(2,1)S(1)}, u32[]{:S(2)}, u32[]{:S(2)}) %all-to-all-start.3) | async-done | bytes 131104 | tf_op jit(solution)/shard_map/conv/all_to_all | solution.py:330
  121.3 1.0 gate.1
  122.3 6.3 %all-to-all-start.4 = ((bf16[16,128,128]{2,1,0:T(8,128)(2,1)}), bf16[16,128,128]{2,1,0:T(8,128)(2,1)S(1)}, u32[]{:S(2)}, u32[]{:S(2)}) async-start(bf16[16,128,128]{2,1,0:T(8,128)(2,1)} %bitcast.10), calls=%async_computation.4 | async-start | bytes 1048576 | tf_op jit(solution)/shard_map/gate/all_to_all | solution.py:336
  128.6 2.0 %collective-permute-start.4 = (bf16[2048,128]{1,0:T(8,128)(2,1)S(1)}, bf16[2048,128]{1,0:T(8,128)(2,1)S(1)}, u32[]{:S(2)}, u32[]{:S(2)}) collective-permute-start(bf16[2048,128]{1,0:T(8,128)(2,1)S(1)} %copy-done.7), channel_id=1, source_target_pairs={{0,4},{4,0},{1,5},{5,1},{2,6},{6,2},{3,7},{7,3},{8,12},{12,8},{9,1... | collective-permute-start | bytes 1572872 | tf_op jit(solution)/shard_map/out_weight_swap/ppermute | solution.py:252
  130.6 2.3 %collective-permute-start.5 = (bf16[2048,128]{1,0:T(8,128)(2,1)S(1)}, bf16[2048,128]{1,0:T(8,128)(2,1)S(1)}, u32[]{:S(2)}, u32[]{:S(2)}) collective-permute-start(bf16[2048,128]{1,0:T(8,128)(2,1)S(1)} %collective-permute-done.3.near_ref), channel_id=1, source_target_pairs={{0,4},{4,0},{1,5},{5,1},{2,6},{6,2},{3,7},{7,3},{8,12},{12,8},{9,1... | collective-permute-start | bytes 1572872 | tf_op jit(solution)/shard_map/out_weight_swap/ppermute | solution.py:252
  132.9 1.5 collective-permute-done.5.far_ref
  134.4 11.2 %all-to-all-done.4 = bf16[16,128,128]{2,1,0:T(8,128)(2,1)S(1)} async-done(((bf16[16,128,128]{2,1,0:T(8,128)(2,1)}), bf16[16,128,128]{2,1,0:T(8,128)(2,1)S(1)}, u32[]{:S(2)}, u32[]{:S(2)}) %all-to-all-start.4) | async-done | bytes 524320 | tf_op jit(solution)/shard_map/gate/all_to_all | solution.py:336
  145.6 1.1 out_project.1
  (29 shorter events, 0.1 us)
Async XLA Ops:
  6.5 63.5 %copy-start = (f32[3,3,512]{2,1,0:T(4,128)S(1)}, f32[3,3,512]{2,1,0:T(4,128)}, u32[]{:S(2)}) copy-start(f32[3,3,512]{2,1,0:T(4,128)} %param.15) | copy-start | bytes 55300
  8.6 30.2 %all-to-all-start = ((bf16[32,5,16,128]{3,2,1,0:T(8,128)(2,1)}), bf16[32,5,16,128]{3,2,1,0:T(8,128)(2,1)S(1)}, u32[]{:S(2)}, u32[]{:S(2)}) async-start(bf16[32,5,16,128]{3,2,1,0:T(8,128)(2,1)} %weight_gather.2), calls=%async_computation | async-start | bytes 1310720 | tf_op jit(solution)/shard_map/weight_gather/all_to_all | solution.py:291
  19.1 43.8 %all-gather.3.cloned.1.call-start = ((), (), s32[]{:S(2)}) async-start(), calls=%async_computation.5 | async-start | bytes 1179648 | tf_op jit(solution)/shard_map/token_gather/all_gather | solution.py:278
  38.8 0.8 copy-start.12
  42.2 36.9 %copy-start.11 = (f32[2048]{0:T(1024)S(1)}, f32[2048]{0:T(1024)}, u32[]{:S(2)}) copy-start(f32[2048]{0:T(1024)} %param.13) | copy-start | bytes 24580
  42.2 36.9 %all-to-all-start.1 = ((bf16[4,136,16,128]{3,2,1,0:T(8,128)(2,1)}), bf16[4,136,16,128]{3,2,1,0:T(8,128)(2,1)S(1)}, u32[]{:S(2)}, u32[]{:S(2)}) async-start(bf16[4,136,16,128]{3,2,1,0:T(8,128)(2,1)} %weight_gather.3), calls=%async_computation.1 | async-start | bytes 4456448 | tf_op jit(solution)/shard_map/weight_gather/all_to_all | solution.py:294
  63.0 16.2 %collective-permute-start = (bf16[8,128,512]{2,1,0:T(8,128)(2,1)}, bf16[8,128,512]{2,1,0:T(8,128)(2,1)S(1)}, u32[]{:S(2)}, u32[]{:S(2)}) collective-permute-start(bf16[8,128,512]{2,1,0:T(8,128)(2,1)} %bitcast.24), channel_id=1, source_target_pairs={{0,4},{4,0},{1,5},{5,1},{2,6},{6,2},{3,7},{7,3},{8,12},{12,8},{9,1... | collective-permute-start | bytes 3145736 | tf_op jit(solution)/shard_map/token_swap/ppermute | solution.py:252
  71.7 6.2 %collective-permute-start.2 = (bf16[4,16,512]{2,1,0:T(8,128)(2,1)S(1)}, bf16[4,16,512]{2,1,0:T(8,128)(2,1)S(1)}, u32[]{:S(2)}, u32[]{:S(2)}) collective-permute-start(bf16[4,16,512]{2,1,0:T(8,128)(2,1)S(1)} %slice_bitcast_fusion), channel_id=1, source_target_pairs={{4,16},{20,32},{36,48},{52,64},{68,80},{84,96},{100,112},{116,128}... | collective-permute-start | bytes 196616 | tf_op jit(solution)/shard_map/token_swap/ppermute | solution.py:300
  74.7 4.4 %collective-permute-start.1 = (bf16[4,16,512]{2,1,0:T(8,128)(2,1)S(1)}, bf16[4,16,512]{2,1,0:T(8,128)(2,1)S(1)}, u32[]{:S(2)}, u32[]{:S(2)}) collective-permute-start(bf16[4,16,512]{2,1,0:T(8,128)(2,1)S(1)} %slice_bitcast_fusion), channel_id=1, source_target_pairs={{0,16},{16,32},{32,48},{48,64},{64,80},{80,96},{96,112},{112,128},... | collective-permute-start | bytes 196616 | tf_op jit(solution)/shard_map/token_swap/ppermute | solution.py:299
  79.2 1.2 copy-start.1
  80.4 25.3 %copy-start.2 = (bf16[512,1024]{1,0:T(8,128)(2,1)S(1)}, bf16[512,1024]{1,0:T(8,128)(2,1)}, u32[]{:S(2)}) copy-start(bf16[512,1024]{1,0:T(8,128)(2,1)} %constant.38.clone.back_ref) | copy-start | bytes 3145732
  80.4 25.3 %copy-start.3 = (bf16[1024,512]{1,0:T(8,128)(2,1)S(1)}, bf16[1024,512]{1,0:T(8,128)(2,1)}, u32[]{:S(2)}) copy-start(bf16[1024,512]{1,0:T(8,128)(2,1)} %constant.34.clone.into_ref) | copy-start | bytes 3145732
  80.4 25.3 %copy-start.8 = (bf16[256,256]{1,0:T(8,128)(2,1)S(1)}, bf16[256,256]{1,0:T(8,128)(2,1)}, u32[]{:S(2)}) copy-start(bf16[256,256]{1,0:T(8,128)(2,1)} %constant.37.clone.near_out_ref) | copy-start | bytes 393220
  80.4 25.3 %copy-start.9 = (f32[2,128,128]{2,1,0:T(8,128)S(1)}, f32[2,128,128]{2,1,0:T(8,128)}, u32[]{:S(2)}) copy-start(f32[2,128,128]{2,1,0:T(8,128)} %constant.36.clone.turn_ref) | copy-start | bytes 393220
  80.4 25.3 %copy-start.10 = (bf16[256,256]{1,0:T(8,128)(2,1)S(1)}, bf16[256,256]{1,0:T(8,128)(2,1)}, u32[]{:S(2)}) copy-start(bf16[256,256]{1,0:T(8,128)(2,1)} %constant.35.clone.near_in_ref) | copy-start | bytes 393220
  83.0 0.8 copy-start.4
  83.9 0.8 copy-start.6
  84.7 27.3 %copy-start.7 = (bf16[2048,128]{1,0:T(8,128)(2,1)S(1)}, bf16[2048,128]{1,0:T(8,128)(2,1)}, u32[]{:S(2)}) copy-start(bf16[2048,128]{1,0:T(8,128)(2,1)} %copy-done.6) | copy-start | bytes 1572868
  84.7 36.7 %copy-start.5 = (f32[512,256]{1,0:T(8,128)S(1)}, f32[512,256]{1,0:T(8,128)}, u32[]{:S(2)}) copy-start(f32[512,256]{1,0:T(8,128)} %copy-done.4) | copy-start | bytes 1572868
  108.1 13.3 %all-to-all-start.3 = ((bf16[32,16,128]{2,1,0:T(8,128)(2,1)}), bf16[32,16,128]{2,1,0:T(8,128)(2,1)S(1)}, u32[]{:S(2)}, u32[]{:S(2)}) async-start(bf16[32,16,128]{2,1,0:T(8,128)(2,1)} %conv.1), calls=%async_computation.3 | async-start | bytes 262144 | tf_op jit(solution)/shard_map/conv/all_to_all | solution.py:330
  111.9 18.6 %collective-permute-start.3 = (bf16[2048,128]{1,0:T(8,128)(2,1)S(1)}, bf16[2048,128]{1,0:T(8,128)(2,1)S(1)}, u32[]{:S(2)}, u32[]{:S(2)}) collective-permute-start(bf16[2048,128]{1,0:T(8,128)(2,1)S(1)} %copy-done.7), channel_id=1, source_target_pairs={{0,8},{8,0},{1,9},{9,1},{2,10},{10,2},{3,11},{11,3},{4,12},{12,4},... | collective-permute-start | bytes 1572872 | tf_op jit(solution)/shard_map/out_weight_swap/ppermute | solution.py:252
  122.3 23.3 %all-to-all-start.4 = ((bf16[16,128,128]{2,1,0:T(8,128)(2,1)}), bf16[16,128,128]{2,1,0:T(8,128)(2,1)S(1)}, u32[]{:S(2)}, u32[]{:S(2)}) async-start(bf16[16,128,128]{2,1,0:T(8,128)(2,1)} %bitcast.10), calls=%async_computation.4 | async-start | bytes 1048576 | tf_op jit(solution)/shard_map/gate/all_to_all | solution.py:336
  128.6 4.3 %collective-permute-start.4 = (bf16[2048,128]{1,0:T(8,128)(2,1)S(1)}, bf16[2048,128]{1,0:T(8,128)(2,1)S(1)}, u32[]{:S(2)}, u32[]{:S(2)}) collective-permute-start(bf16[2048,128]{1,0:T(8,128)(2,1)S(1)} %copy-done.7), channel_id=1, source_target_pairs={{0,4},{4,0},{1,5},{5,1},{2,6},{6,2},{3,7},{7,3},{8,12},{12,8},{9,1... | collective-permute-start | bytes 1572872 | tf_op jit(solution)/shard_map/out_weight_swap/ppermute | solution.py:252
  130.6 3.8 %collective-permute-start.5 = (bf16[2048,128]{1,0:T(8,128)(2,1)S(1)}, bf16[2048,128]{1,0:T(8,128)(2,1)S(1)}, u32[]{:S(2)}, u32[]{:S(2)}) collective-permute-start(bf16[2048,128]{1,0:T(8,128)(2,1)S(1)} %collective-permute-done.3.near_ref), channel_id=1, source_target_pairs={{0,4},{4,0},{1,5},{5,1},{2,6},{6,2},{3,7},{7,3},{8,12},{12,8},{9,1... | collective-permute-start | bytes 1572872 | tf_op jit(solution)/shard_map/out_weight_swap/ppermute | solution.py:252
Sparse Core Ops, SparseCore 0:
  22.1 40.8 all-gather.2

commit v5 on v4

--- a/solution.py
+++ b/solution.py
@@ -20,7 +20,7 @@
 SEQ = OUTER + INNER
 
 
-def call(body, out_shape, places, args, scratch=(), limit=16):
+def call(body, out_shape, places, args, scratch=(), limit=16, cost=None):
     spaces = {"h": pltpu.HBM, "v": pltpu.VMEM, "s": pltpu.SMEM}
     specs = [pl.BlockSpec(memory_space=spaces[place]) for place in places]
     single = not isinstance(out_shape, tuple)
@@ -31,6 +31,7 @@
         in_specs=specs[: len(args)],
         out_specs=outs[0] if single else tuple(outs),
         scratch_shapes=scratch,
+        cost_estimate=cost,
         compiler_params=pltpu.CompilerParams(vmem_limit_bytes=limit * MIB),
     )(*args)
 
@@ -219,6 +220,14 @@
     send_ref[...] = jnp.concatenate(pieces, axis=1).astype(BF16)
 
 
+def tail_body(own_hbm, out_ref, sems):
+    step = own_hbm.shape[0] // out_ref.shape[0]
+    rows = pl.ds(own_hbm.shape[1] - HALO, HALO)
+    finish(
+        started([(own_hbm.at[step * p + step - 1, rows], out_ref.at[p]) for p in range(out_ref.shape[0])], sems)
+    )
+
+
 def gate_body(conv_ref, gates_ref, out_ref):
     groups, rows, lanes = conv_ref.shape
     inner = gates_ref.shape[0] // lanes
@@ -290,12 +299,20 @@
         )
         got = lax.all_to_all(send, ("y",) + INNER, 0, 0)
         tiles = (kinds - 1) * along * inner + along
-        send = call(repack_body, shape((across, tiles, depth, LANES), BF16), "vv", (got,), limit=56)
+        send = call(repack_body, shape((across, tiles, depth, LANES), BF16), "vv", (got,))
         got = lax.all_to_all(send, "x", 0, 0)
     with jax.named_scope("token_swap"):
         own, _ = lax.optimization_barrier((own, send))
         other = swap(own, "co")
-        tail = own.reshape(tp, ways["zl"], length, feats)[:, -1, length - HALO :]
+        tail = call(
+            tail_body,
+            shape((tp, HALO, feats), BF16),
+            "hv",
+            (own,),
+            copies_of(tp),
+            limit=60,
+            cost=pl.CostEstimate(flops=20000000000, bytes_accessed=2 * own.size, transcendentals=0),
+        )
         halo_own = lax.ppermute(tail, OUTER, [(i, i + 1) for i in range(outer - 1)])
         halo_other = lax.ppermute(
             tail,

time: 154 us -> 151 us (0.981)
  waiting for transfers between devices: 57.2 us -> 52.7 us
  starting transfers between devices: 44.7 us -> 48.3 us
  local copies, waits for them, and re-layouts: 5.33 us -> 2.44 us
  Pallas kernels: 11.7 us -> 13.4 us
    all_gather x1, waiting for transfers between devices: 16.6 us -> 9.58 us  [shards(): own = lax.all_gather(tokens, ('tp', 'zl'), axis=0)]
    all_to_all x1, starting transfers between devices: 6.26 us -> 12 us  [shards(): lax.all_to_all(gated.reshape(inner * tp, length, chans), INNER + ('tp',),...]
    unnamed x28 -> x26, local copies, waits for them, and re-layouts: 3.72 us -> 1.68 us
    ppermute x4, starting transfers between devices: 13.7 us -> 11.7 us  [swap(): return lax.ppermute(value, axis, [(0, 1), (1, 0)])]
    pallas_call x6 -> x7, Pallas kernels: 11.7 us -> 13.4 us  [call(): pl.pallas_call(body, out_shape=out_shape, in_specs=specs[:len(args)], out...]
    ppermute x1, waiting for transfers between devices: 0.01 us -> 1.56 us  [shards(): lax.ppermute(tail, OUTER + ('co',), [(i * cores + cores - 1, (i + 1) * co...]
  transfers between devices with their start and end apart: 11 -> 11, of which waited for: 6 -> 8; matrix products, arithmetic and copies ran while one was open for 1% -> 1% of each run, Pallas kernels for 2% -> 4%
where the time goes in v5:
time: 151 us; the launch traced here: 150 us
  waiting for transfers between devices  52.7 us (35%)
  starting transfers between devices  48.3 us (32%)
  blocking collectives  19.8 us (13%)
  between operations  13.6 us (9%)
  Pallas kernels  13.4 us (9%)
  local copies, waits for them, and re-layouts  2.44 us (2%)
    all_to_all x1, blocking collectives, shards(): got = lax.all_to_all(send, OUTER, 0, 0)  19.8 us
    all_to_all x1, waiting for transfers between devices, shards(): got = lax.all_to_all(send, ('y',) + INNER, 0, 0)  18.8 us
    pallas_call x7, Pallas kernels, call(): pl.pallas_call(body, out_shape=out_shape, in_specs=specs[:len(args)], out...  13.4 us
    all_to_all x1, starting transfers between devices, shards(): lax.all_to_all(gated.reshape(inner * tp, length, chans), INNER + ('tp',),...  12 us
    ppermute x4, starting transfers between devices, swap(): return lax.ppermute(value, axis, [(0, 1), (1, 0)])  11.7 us
    all_to_all x1, waiting for transfers between devices, shards(): lax.all_to_all(gated.reshape(inner * tp, length, chans), INNER + ('tp',),...  11.2 us
    all_to_all x1, starting transfers between devices, shards(): got = lax.all_to_all(send, ('y',) + INNER, 0, 0)  10.6 us
    all_gather x1, waiting for transfers between devices, shards(): own = lax.all_gather(tokens, ('tp', 'zl'), axis=0)  9.58 us
  transfers between devices with their start and end apart: 11, of which 8 were waited for; matrix products, arithmetic and copies ran while one was open for 1% of the time, Pallas kernels for 4%

profile of v5, /device:TPU:1, one launch (start us, length us, event | category | flops | bytes accessed | tf_op | source)
XLA Modules:
  0.0 150.2 jit_solution(15648628544676035480)
XLA Ops:
  6.5 0.7 all-gather.3.cloned.1.call-update
  7.3 2.0 %weight_gather.2 = bf16[32,5,16,128]{3,2,1,0:T(8,128)(2,1)} custom-call(bf16[3,16,512]{2,1,0:T(8,128)(2,1)} %bitcast.25, bf16[16,512]{1,0:T(8,128)(2,1)} %out_w_hbm.1, f32[128,512]{1,0:T(8,128)} %taps_hbm.1), custom_call_target="tpu_custom_call" | custom-call | tf_op jit(solution)/shard_map/weight_gather/pallas_call | solution.py:28
  9.3 10.6 %all-to-all-start = ((bf16[32,5,16,128]{3,2,1,0:T(8,128)(2,1)}), bf16[32,5,16,128]{3,2,1,0:T(8,128)(2,1)S(1)}, u32[]{:S(2)}, u32[]{:S(2)}) async-start(bf16[32,5,16,128]{3,2,1,0:T(8,128)(2,1)} %weight_gather.2), calls=%async_computation | async-start | bytes 1310720 | tf_op jit(solution)/shard_map/weight_gather/all_to_all | solution.py:300
  19.9 0.8 dynamic-slice_bitcast_fusion.1.skip_ref
  20.7 18.8 %all-to-all-done.got_ref = bf16[32,5,16,128]{3,2,1,0:T(8,128)(2,1)S(1)} async-done(((bf16[32,5,16,128]{3,2,1,0:T(8,128)(2,1)}), bf16[32,5,16,128]{3,2,1,0:T(8,128)(2,1)S(1)}, u32[]{:S(2)}, u32[]{:S(2)}) %all-to-all-start) | async-done | bytes 655392 | tf_op jit(solution)/shard_map/weight_gather/all_to_all | solution.py:300
  39.5 1.5 %weight_gather.3 = bf16[4,136,16,128]{3,2,1,0:T(8,128)(2,1)} custom-call(bf16[32,5,16,128]{3,2,1,0:T(8,128)(2,1)S(1)} %all-to-all-done.got_ref), custom_call_target="tpu_custom_call" | custom-call | tf_op jit(solution)/shard_map/weight_gather/pallas_call | solution.py:28
  41.0 4.0 %all-to-all-start.1 = ((bf16[4,136,16,128]{3,2,1,0:T(8,128)(2,1)}), bf16[4,136,16,128]{3,2,1,0:T(8,128)(2,1)S(1)}, u32[]{:S(2)}, u32[]{:S(2)}) async-start(bf16[4,136,16,128]{3,2,1,0:T(8,128)(2,1)} %weight_gather.3), calls=%async_computation.1 | async-start | bytes 4456448 | tf_op jit(solution)/shard_map/weight_gather/all_to_all | solution.py:303
  45.0 9.6 %all-gather.3.cloned.1.call-done = bf16[1024,512]{1,0:T(8,128)(2,1)} async-done(((bf16[128,512]{1,0:T(8,128)(2,1)}), bf16[1024,512]{1,0:T(8,128)(2,1)}) %all-gather.3.cloned.1.call-update) | async-done | bytes 1048592 | tf_op jit(solution)/shard_map/token_gather/all_gather | solution.py:287
  54.6 5.5 %collective-permute-start = (bf16[8,128,512]{2,1,0:T(8,128)(2,1)}, bf16[8,128,512]{2,1,0:T(8,128)(2,1)}, u32[]{:S(2)}, u32[]{:S(2)}) collective-permute-start(bf16[8,128,512]{2,1,0:T(8,128)(2,1)} %bitcast.19), channel_id=1, source_target_pairs={{0,4},{4,0},{1,5},{5,1},{2,6},{6,2},{3,7},{7,3},{8,12},{12,8},{9,1... | collective-permute-start | bytes 3145736 | tf_op jit(solution)/shard_map/token_swap/ppermute | solution.py:261
  60.1 1.4 token_swap.1
  61.5 3.0 %collective-permute-start.2 = (bf16[4,16,512]{2,1,0:T(8,128)(2,1)}, bf16[4,16,512]{2,1,0:T(8,128)(2,1)S(1)}, u32[]{:S(2)}, u32[]{:S(2)}) collective-permute-start(bf16[4,16,512]{2,1,0:T(8,128)(2,1)} %token_swap.1), channel_id=1, source_target_pairs={{4,16},{20,32},{36,48},{52,64},{68,80},{84,96},{100,112},{116,128}... | collective-permute-start | bytes 196616 | tf_op jit(solution)/shard_map/token_swap/ppermute | solution.py:317
  64.5 3.1 %collective-permute-start.1 = (bf16[4,16,512]{2,1,0:T(8,128)(2,1)}, bf16[4,16,512]{2,1,0:T(8,128)(2,1)S(1)}, u32[]{:S(2)}, u32[]{:S(2)}) collective-permute-start(bf16[4,16,512]{2,1,0:T(8,128)(2,1)} %token_swap.1), channel_id=1, source_target_pairs={{0,16},{16,32},{32,48},{48,64},{64,80},{80,96},{96,112},{112,128},... | collective-permute-start | bytes 196616 | tf_op jit(solution)/shard_map/token_swap/ppermute | solution.py:316
  67.7 0.1 add_bitcast_fusion
  67.7 1.6 %collective-permute-done.2.halo_other_ref = bf16[4,16,512]{2,1,0:T(8,128)(2,1)S(1)} collective-permute-done((bf16[4,16,512]{2,1,0:T(8,128)(2,1)}, bf16[4,16,512]{2,1,0:T(8,128)(2,1)S(1)}, u32[]{:S(2)}, u32[]{:S(2)}) %collective-permute-start.2) | collective-permute-done | bytes 65568 | tf_op jit(solution)/shard_map/token_swap/ppermute | solution.py:317
  69.3 1.4 collective-permute-done.1.halo_own_ref
  70.7 0.5 all-to-all-done.1.got_ref
  71.2 0.0 copy-start.8
  71.2 4.0 %project.1 = (f32[512,256]{1,0:T(8,128)S(1)}, bf16[32,16,128]{2,1,0:T(8,128)(2,1)S(1)}, bf16[2048,128]{1,0:T(8,128)(2,1)S(1)}, bf16[512,128]{1,0:T(8,128)(2,1)S(1)}) custom-call(s32[1,1]{1,0:T(1,128)S(1)} %bitcast.24, bf16[8,128,512]{2,1,0:T(8,128)(2,1)S(1)} %bitcast.21, bf16[8,128,512]{2,1,0:T(8,128)(2,1)} %collective-permute-done.other_ref, ...), custom_call_target="tpu_custom_call" | custom-call | tf_op jit(solution)/shard_map/project/pallas_call | solution.py:28
  75.2 0.8 copy-done.4
  76.0 0.8 copy-done.6
  76.9 19.8 %all_to_all.25.sig_ref = bf16[32,16,128]{2,1,0:T(8,128)(2,1)S(1)} all-to-all(bf16[32,16,128]{2,1,0:T(8,128)(2,1)S(1)} %get-tuple-element.11), channel_id=1, replica_groups=mesh['y'=8,'x'=4,'zl'=2,'co'=2,'tp'=4] {'y','x'}, dimensions={0} | all-to-all | bytes 262144 | tf_op jit(solution)/shard_map/conv/all_to_all | solution.py:343
  96.7 2.3 %conv.1 = bf16[32,16,128]{2,1,0:T(8,128)(2,1)} custom-call(bf16[32,16,128]{2,1,0:T(8,128)(2,1)S(1)} %all_to_all.25.sig_ref, bf16[512,128]{1,0:T(8,128)(2,1)S(1)} %get-tuple-element.12.taps_ref, bf16[1024,512]{1,0:T(8,128)(2,1)S(1)} %copy-done.2, bf16[256,256]{1,0:T(8,128)(2,1)S(1)} %copy-done.10, f32[2,128,128]{2,1,0:T(8,128)S(1)} %copy-done.9, ...), custom_call_target="tpu_custom_call" | custom-call | tf_op jit(solution)/shard_map/conv/pallas_call | solution.py:28
  99.0 3.9 %all-to-all-start.3 = ((bf16[32,16,128]{2,1,0:T(8,128)(2,1)}), bf16[32,16,128]{2,1,0:T(8,128)(2,1)S(1)}, u32[]{:S(2)}, u32[]{:S(2)}) async-start(bf16[32,16,128]{2,1,0:T(8,128)(2,1)} %conv.1), calls=%async_computation.3 | async-start | bytes 262144 | tf_op jit(solution)/shard_map/conv/all_to_all | solution.py:347
  102.9 1.9 %collective-permute-start.3 = (bf16[2048,128]{1,0:T(8,128)(2,1)S(1)}, bf16[2048,128]{1,0:T(8,128)(2,1)S(1)}, u32[]{:S(2)}, u32[]{:S(2)}) collective-permute-start(bf16[2048,128]{1,0:T(8,128)(2,1)S(1)} %copy-done.7), channel_id=1, source_target_pairs={{0,8},{8,0},{1,9},{9,1},{2,10},{10,2},{3,11},{11,3},{4,12},{12,4},... | collective-permute-start | bytes 1572872 | tf_op jit(solution)/shard_map/out_weight_swap/ppermute | solution.py:261
  104.8 7.5 %all-to-all-done.3.conv_ref = bf16[32,16,128]{2,1,0:T(8,128)(2,1)S(1)} async-done(((bf16[32,16,128]{2,1,0:T(8,128)(2,1)}), bf16[32,16,128]{2,1,0:T(8,128)(2,1)S(1)}, u32[]{:S(2)}, u32[]{:S(2)}) %all-to-all-start.3) | async-done | bytes 131104 | tf_op jit(solution)/shard_map/conv/all_to_all | solution.py:347
  112.3 0.9 gate.1
  113.2 12.0 %all-to-all-start.4 = ((bf16[16,128,128]{2,1,0:T(8,128)(2,1)}), bf16[16,128,128]{2,1,0:T(8,128)(2,1)S(1)}, u32[]{:S(2)}, u32[]{:S(2)}) async-start(bf16[16,128,128]{2,1,0:T(8,128)(2,1)} %bitcast.8), calls=%async_computation.4 | async-start | bytes 1048576 | tf_op jit(solution)/shard_map/gate/all_to_all | solution.py:353
  125.2 2.0 %collective-permute-start.4 = (bf16[2048,128]{1,0:T(8,128)(2,1)S(1)}, bf16[2048,128]{1,0:T(8,128)(2,1)S(1)}, u32[]{:S(2)}, u32[]{:S(2)}) collective-permute-start(bf16[2048,128]{1,0:T(8,128)(2,1)S(1)} %copy-done.7), channel_id=1, source_target_pairs={{0,4},{4,0},{1,5},{5,1},{2,6},{6,2},{3,7},{7,3},{8,12},{12,8},{9,1... | collective-permute-start | bytes 1572872 | tf_op jit(solution)/shard_map/out_weight_swap/ppermute | solution.py:261
  127.2 2.3 %collective-permute-start.5 = (bf16[2048,128]{1,0:T(8,128)(2,1)S(1)}, bf16[2048,128]{1,0:T(8,128)(2,1)S(1)}, u32[]{:S(2)}, u32[]{:S(2)}) collective-permute-start(bf16[2048,128]{1,0:T(8,128)(2,1)S(1)} %collective-permute-done.3.near_ref), channel_id=1, source_target_pairs={{0,4},{4,0},{1,5},{5,1},{2,6},{6,2},{3,7},{7,3},{8,12},{12,8},{9,1... | collective-permute-start | bytes 1572872 | tf_op jit(solution)/shard_map/out_weight_swap/ppermute | solution.py:261
  129.6 1.5 %collective-permute-done.5.far_ref = bf16[2048,128]{1,0:T(8,128)(2,1)S(1)} collective-permute-done((bf16[2048,128]{1,0:T(8,128)(2,1)S(1)}, bf16[2048,128]{1,0:T(8,128)(2,1)S(1)}, u32[]{:S(2)}, u32[]{:S(2)}) %collective-permute-start.5) | collective-permute-done | bytes 524320 | tf_op jit(solution)/shard_map/out_weight_swap/ppermute | solution.py:261
  131.1 11.2 %all-to-all-done.4 = bf16[16,128,128]{2,1,0:T(8,128)(2,1)S(1)} async-done(((bf16[16,128,128]{2,1,0:T(8,128)(2,1)}), bf16[16,128,128]{2,1,0:T(8,128)(2,1)S(1)}, u32[]{:S(2)}, u32[]{:S(2)}) %all-to-all-start.4) | async-done | bytes 524320 | tf_op jit(solution)/shard_map/gate/all_to_all | solution.py:353
  142.3 1.1 out_project.1
  (27 shorter events, 0.1 us)
Async XLA Ops:
  6.5 13.3 %copy-start = (f32[3,3,512]{2,1,0:T(4,128)S(1)}, f32[3,3,512]{2,1,0:T(4,128)}, u32[]{:S(2)}) copy-start(f32[3,3,512]{2,1,0:T(4,128)} %param.15) | copy-start | bytes 55300
  6.5 48.1 %all-gather.3.cloned.1.call-start = ((), (), s32[]{:S(2)}) async-start(), calls=%async_computation.5 | async-start | bytes 1179648 | tf_op jit(solution)/shard_map/token_gather/all_gather | solution.py:287
  9.3 30.2 %all-to-all-start = ((bf16[32,5,16,128]{3,2,1,0:T(8,128)(2,1)}), bf16[32,5,16,128]{3,2,1,0:T(8,128)(2,1)S(1)}, u32[]{:S(2)}, u32[]{:S(2)}) async-start(bf16[32,5,16,128]{3,2,1,0:T(8,128)(2,1)} %weight_gather.2), calls=%async_computation | async-start | bytes 1310720 | tf_op jit(solution)/shard_map/weight_gather/all_to_all | solution.py:300
  41.0 30.2 %all-to-all-start.1 = ((bf16[4,136,16,128]{3,2,1,0:T(8,128)(2,1)}), bf16[4,136,16,128]{3,2,1,0:T(8,128)(2,1)S(1)}, u32[]{:S(2)}, u32[]{:S(2)}) async-start(bf16[4,136,16,128]{3,2,1,0:T(8,128)(2,1)} %weight_gather.3), calls=%async_computation.1 | async-start | bytes 4456448 | tf_op jit(solution)/shard_map/weight_gather/all_to_all | solution.py:303
  54.6 16.6 %copy-start.3 = (bf16[1024,512]{1,0:T(8,128)(2,1)S(1)}, bf16[1024,512]{1,0:T(8,128)(2,1)}, u32[]{:S(2)}) copy-start(bf16[1024,512]{1,0:T(8,128)(2,1)} %all-gather.3.cloned.1.call-done) | copy-start | bytes 3145732
  54.6 16.6 %copy-start.11 = (f32[2048]{0:T(1024)S(1)}, f32[2048]{0:T(1024)}, u32[]{:S(2)}) copy-start(f32[2048]{0:T(1024)} %param.13) | copy-start | bytes 24580
  54.6 16.1 %collective-permute-start = (bf16[8,128,512]{2,1,0:T(8,128)(2,1)}, bf16[8,128,512]{2,1,0:T(8,128)(2,1)}, u32[]{:S(2)}, u32[]{:S(2)}) collective-permute-start(bf16[8,128,512]{2,1,0:T(8,128)(2,1)} %bitcast.19), channel_id=1, source_target_pairs={{0,4},{4,0},{1,5},{5,1},{2,6},{6,2},{3,7},{7,3},{8,12},{12,8},{9,1... | collective-permute-start | bytes 3145736 | tf_op jit(solution)/shard_map/token_swap/ppermute | solution.py:261
  61.5 7.8 %collective-permute-start.2 = (bf16[4,16,512]{2,1,0:T(8,128)(2,1)}, bf16[4,16,512]{2,1,0:T(8,128)(2,1)S(1)}, u32[]{:S(2)}, u32[]{:S(2)}) collective-permute-start(bf16[4,16,512]{2,1,0:T(8,128)(2,1)} %token_swap.1), channel_id=1, source_target_pairs={{4,16},{20,32},{36,48},{52,64},{68,80},{84,96},{100,112},{116,128}... | collective-permute-start | bytes 196616 | tf_op jit(solution)/shard_map/token_swap/ppermute | solution.py:317
  64.5 6.2 %collective-permute-start.1 = (bf16[4,16,512]{2,1,0:T(8,128)(2,1)}, bf16[4,16,512]{2,1,0:T(8,128)(2,1)S(1)}, u32[]{:S(2)}, u32[]{:S(2)}) collective-permute-start(bf16[4,16,512]{2,1,0:T(8,128)(2,1)} %token_swap.1), channel_id=1, source_target_pairs={{0,16},{16,32},{32,48},{48,64},{64,80},{80,96},{96,112},{112,128},... | collective-permute-start | bytes 196616 | tf_op jit(solution)/shard_map/token_swap/ppermute | solution.py:316
  71.2 25.5 %copy-start.1 = (bf16[512,1024]{1,0:T(8,128)(2,1)S(1)}, bf16[512,1024]{1,0:T(8,128)(2,1)}, u32[]{:S(2)}) copy-start(bf16[512,1024]{1,0:T(8,128)(2,1)} %constant.38.clone.back_ref) | copy-start | bytes 3145732
  71.2 25.5 %copy-start.2 = (bf16[1024,512]{1,0:T(8,128)(2,1)S(1)}, bf16[1024,512]{1,0:T(8,128)(2,1)}, u32[]{:S(2)}) copy-start(bf16[1024,512]{1,0:T(8,128)(2,1)} %constant.34.clone.into_ref) | copy-start | bytes 3145732
  71.2 25.5 %copy-start.8 = (bf16[256,256]{1,0:T(8,128)(2,1)S(1)}, bf16[256,256]{1,0:T(8,128)(2,1)}, u32[]{:S(2)}) copy-start(bf16[256,256]{1,0:T(8,128)(2,1)} %constant.37.clone.near_out_ref) | copy-start | bytes 393220
  71.2 25.5 %copy-start.9 = (f32[2,128,128]{2,1,0:T(8,128)S(1)}, f32[2,128,128]{2,1,0:T(8,128)}, u32[]{:S(2)}) copy-start(f32[2,128,128]{2,1,0:T(8,128)} %constant.36.clone.turn_ref) | copy-start | bytes 393220
  71.2 25.5 %copy-start.10 = (bf16[256,256]{1,0:T(8,128)(2,1)S(1)}, bf16[256,256]{1,0:T(8,128)(2,1)}, u32[]{:S(2)}) copy-start(bf16[256,256]{1,0:T(8,128)(2,1)} %constant.35.clone.near_in_ref) | copy-start | bytes 393220
  75.2 0.8 copy-start.4
  76.0 0.8 copy-start.6
  76.9 26.0 %copy-start.7 = (bf16[2048,128]{1,0:T(8,128)(2,1)S(1)}, bf16[2048,128]{1,0:T(8,128)(2,1)}, u32[]{:S(2)}) copy-start(bf16[2048,128]{1,0:T(8,128)(2,1)} %copy-done.6) | copy-start | bytes 1572868
  76.9 35.4 %copy-start.5 = (f32[512,256]{1,0:T(8,128)S(1)}, f32[512,256]{1,0:T(8,128)}, u32[]{:S(2)}) copy-start(f32[512,256]{1,0:T(8,128)} %copy-done.4) | copy-start | bytes 1572868
  99.0 13.3 %all-to-all-start.3 = ((bf16[32,16,128]{2,1,0:T(8,128)(2,1)}), bf16[32,16,128]{2,1,0:T(8,128)(2,1)S(1)}, u32[]{:S(2)}, u32[]{:S(2)}) async-start(bf16[32,16,128]{2,1,0:T(8,128)(2,1)} %conv.1), calls=%async_computation.3 | async-start | bytes 262144 | tf_op jit(solution)/shard_map/conv/all_to_all | solution.py:347
  102.9 24.4 %collective-permute-start.3 = (bf16[2048,128]{1,0:T(8,128)(2,1)S(1)}, bf16[2048,128]{1,0:T(8,128)(2,1)S(1)}, u32[]{:S(2)}, u32[]{:S(2)}) collective-permute-start(bf16[2048,128]{1,0:T(8,128)(2,1)S(1)} %copy-done.7), channel_id=1, source_target_pairs={{0,8},{8,0},{1,9},{9,1},{2,10},{10,2},{3,11},{11,3},{4,12},{12,4},... | collective-permute-start | bytes 1572872 | tf_op jit(solution)/shard_map/out_weight_swap/ppermute | solution.py:261
  113.2 29.1 %all-to-all-start.4 = ((bf16[16,128,128]{2,1,0:T(8,128)(2,1)}), bf16[16,128,128]{2,1,0:T(8,128)(2,1)S(1)}, u32[]{:S(2)}, u32[]{:S(2)}) async-start(bf16[16,128,128]{2,1,0:T(8,128)(2,1)} %bitcast.8), calls=%async_computation.4 | async-start | bytes 1048576 | tf_op jit(solution)/shard_map/gate/all_to_all | solution.py:353
  125.2 4.3 %collective-permute-start.4 = (bf16[2048,128]{1,0:T(8,128)(2,1)S(1)}, bf16[2048,128]{1,0:T(8,128)(2,1)S(1)}, u32[]{:S(2)}, u32[]{:S(2)}) collective-permute-start(bf16[2048,128]{1,0:T(8,128)(2,1)S(1)} %copy-done.7), channel_id=1, source_target_pairs={{0,4},{4,0},{1,5},{5,1},{2,6},{6,2},{3,7},{7,3},{8,12},{12,8},{9,1... | collective-permute-start | bytes 1572872 | tf_op jit(solution)/shard_map/out_weight_swap/ppermute | solution.py:261
  127.2 3.8 %collective-permute-start.5 = (bf16[2048,128]{1,0:T(8,128)(2,1)S(1)}, bf16[2048,128]{1,0:T(8,128)(2,1)S(1)}, u32[]{:S(2)}, u32[]{:S(2)}) collective-permute-start(bf16[2048,128]{1,0:T(8,128)(2,1)S(1)} %collective-permute-done.3.near_ref), channel_id=1, source_target_pairs={{0,4},{4,0},{1,5},{5,1},{2,6},{6,2},{3,7},{7,3},{8,12},{12,8},{9,1... | collective-permute-start | bytes 1572872 | tf_op jit(solution)/shard_map/out_weight_swap/ppermute | solution.py:261
Sparse Core Ops, SparseCore 0:
  9.4 45.1 all-gather.2

commit v6 on v5

--- a/solution.py
+++ b/solution.py
@@ -51,18 +51,15 @@
         copy.wait()
 
 
-def transform_tables(length, chans, outer, inner):
+def transform_tables(length):
     blocks = length // LANES
     row = np.arange(blocks)
     lane = np.arange(LANES)
     far = np.exp(-2j * np.pi * (row[:, None] * (4 * row[None, :] + 1) % (4 * blocks)) / (4 * blocks))
     near = np.exp(-2j * np.pi * (lane[:, None] * lane[None, :] % LANES) / LANES)
     turn = np.exp(-2j * np.pi * ((4 * row[:, None] + 1) * lane[None, :] % (4 * length)) / (4 * length))
-    eye = np.eye(chans)
-    into = np.einsum("bf,cd->cfbd", far, eye).reshape(chans * blocks, blocks * chans)
-    into = np.concatenate([into.real, into.imag], axis=0)
-    back = np.einsum("bf,cd->bdcf", far.conj(), eye).reshape(blocks * chans, chans * blocks) / length
-    back = np.concatenate([back.real, -back.imag], axis=1)
+    into = np.concatenate([far.T.real, far.T.imag], axis=0)
+    back = np.concatenate([far.real, far.imag], axis=1) / length
     near_in = np.block([[near.real, near.imag], [-near.imag, near.real]])
     near_out = np.block([[near.real, -near.imag], [near.imag, near.real]])
     turn = np.stack([turn.real, turn.imag])
@@ -80,31 +77,51 @@
     return real * cos - imag * sin, real * sin + imag * cos
 
 
-def turned(pair, turn_ref, sign, axis):
-    chans = pair[0].shape[0] // turn_ref.shape[1]
-    cos = jnp.concatenate([turn_ref[0]] * chans, axis=0)
-    sin = jnp.concatenate([turn_ref[1]] * chans, axis=0) * sign
-    return jnp.concatenate(times(*pair, cos, sin), axis=axis).astype(BF16)
-
-
 def halves(value, axis):
     half = value.shape[axis] // 2
     return lax.slice_in_dim(value, 0, half, axis=axis), lax.slice_in_dim(value, half, 2 * half, axis=axis)
 
 
-def conv_body(sig_ref, taps_ref, into_ref, near_in_ref, turn_ref, near_out_ref, back_ref, out_ref):
+def conv_body(
+    sig_ref,
+    taps_ref,
+    into_ref,
+    near_in_ref,
+    turn_ref,
+    near_out_ref,
+    back_ref,
+    earlier_ref,
+    out_ref,
+    both_ref,
+    result_ref,
+):
     groups, rows, lanes = sig_ref.shape
-    both = jnp.concatenate([sig_ref[...].reshape(groups * rows, lanes), taps_ref[...]], axis=1)
-    far = halves(jnp.dot(into_ref[...], both, preferred_element_type=F32), 0)
-    sides = [(far[0][:, :lanes], far[1][:, :lanes]), (far[0][:, lanes:], far[1][:, lanes:])]
-    pair = jnp.concatenate([turned(side, turn_ref, 1.0, 1) for side in sides], axis=0)
+    blocks = into_ref.shape[1]
+    per = groups * rows // blocks
+    both_ref[0] = sig_ref[...].reshape(groups * rows, lanes).astype(F32)
+    both_ref[1] = taps_ref[...].astype(F32)
+    cos, sin = turn_ref[0], turn_ref[1]
+    pairs = []
+    for chan in range(per):
+        at = pl.ds(chan, blocks, stride=per)
+        both = jnp.concatenate([both_ref[0, at], both_ref[1, at]], axis=1).astype(BF16)
+        far = jnp.dot(into_ref[...], both, preferred_element_type=F32)
+        real, imag = halves(far, 0)
+        pairs += [
+            jnp.concatenate(times(r, i, cos, sin), axis=1)
+            for r, i in zip(halves(real, 1), halves(imag, 1))
+        ]
+    pair = jnp.concatenate(pairs[::2] + pairs[1::2], axis=0).astype(BF16)
     points = halves(jnp.dot(pair, near_in_ref[...], preferred_element_type=F32), 0)
     product = times(*halves(points[0], 1), *halves(points[1], 1))
     pair = jnp.concatenate(product, axis=1).astype(BF16)
     near = jnp.dot(pair, near_out_ref[...], preferred_element_type=F32)
-    pair = turned(halves(near, 1), turn_ref, -1.0, 0)
-    result = jnp.dot(back_ref[...], pair, preferred_element_type=F32)
-    out_ref[...] = result.astype(BF16).reshape(groups, rows, lanes)
+    for chan in range(per):
+        real, imag = halves(near[chan * blocks : (chan + 1) * blocks], 1)
+        pair = jnp.concatenate(times(real, imag, cos, -sin), axis=0).astype(BF16)
+        at = pl.ds(chan, blocks, stride=per)
+        result_ref[at] = jnp.dot(back_ref[...], pair, preferred_element_type=F32)
+    out_ref[...] = result_ref[...].astype(BF16).reshape(groups, rows, lanes)
 
 
 def pack_body(weight_hbm, out_w_hbm, taps_hbm, send_hbm, weight_ref, out_w_ref, taps_ref, send_ref, sems):
@@ -339,14 +356,17 @@
             + (norm_gain.reshape(1, tp * feats), own_taps, own_skip, got),
             held(wide, proj),
         )
+    with jax.named_scope("out_weight_swap"):
+        near_w = swap(out_w, "zl")
     with jax.named_scope("conv"):
         got = lax.all_to_all(send, OUTER, 0, 0)
         names = ("into", "near_in", "turn", "near_out", "back")
-        operands = (got, taps) + tuple(tables[name] for name in names)
-        conv = call(conv_body, blocks, "v" * (len(operands) + 1), operands)
+        operands = (got, taps) + tuple(tables[name] for name in names) + (near_w,)
+        count = outer * rows
+        held_rows = [pltpu.VMEM((2, count, LANES), F32), pltpu.VMEM((count, LANES), F32)]
+        conv = call(conv_body, blocks, "v" * (len(operands) - 1) + "hv", operands, held_rows)
         conv = lax.all_to_all(conv, OUTER, 0, 0)
     with jax.named_scope("out_weight_swap"):
-        near_w = swap(out_w, "zl")
         across_w = swap(out_w, "co"), swap(near_w, "co")
     with jax.named_scope("gate"):
         gated = call(gate_body, shape((inner, tp, length, chans), BF16), "vvv", (conv, gates))
@@ -377,10 +397,7 @@
     )
 
     def run(*args):
-        tokens, skip = args[0], args[5]
-        inner = ways["zl"] * ways["co"]
-        per = skip.shape[0] // (tp * seq)
-        tables = transform_tables(tokens.shape[0], per, seq // inner, inner)
+        tables = transform_tables(args[0].shape[0])
         body = functools.partial(shards, ways, tables)
         return jax.shard_map(
             body, mesh=fine, in_specs=placed, out_specs=P(SEQ, "tp"), check_vma=False

time: 151 us -> 151 us (level)
  blocking collectives: 19.8 us -> 30.1 us
  waiting for transfers between devices: 52.7 us -> 44.8 us
    all_to_all x0 -> x1, blocking collectives: none -> 13.4 us  [shards(): conv = lax.all_to_all(conv, OUTER, 0, 0)]
    all_to_all x1 -> x0, waiting for transfers between devices: 7.47 us -> none  [shards(): conv = lax.all_to_all(conv, OUTER, 0, 0)]
    all_to_all x1 -> x0, starting transfers between devices: 3.86 us -> none  [shards(): conv = lax.all_to_all(conv, OUTER, 0, 0)]
    all_to_all x1, blocking collectives: 19.8 us -> 16.6 us  [shards(): got = lax.all_to_all(send, OUTER, 0, 0)]
    ppermute x4, starting transfers between devices: 11.7 us -> 14.5 us  [swap(): return lax.ppermute(value, axis, [(0, 1), (1, 0)])]
  transfers between devices with their start and end apart: 11 -> 10, of which waited for: 8 -> 7; matrix products, arithmetic and copies ran while one was open for 1% -> 1% of each run, Pallas kernels for 4% -> 3%
where the time goes in v6:
time: 151 us; the launch traced here: 150 us
  starting transfers between devices  47.5 us (31%)
  waiting for transfers between devices  44.8 us (30%)
  blocking collectives  30.1 us (20%)
  between operations  13.6 us (9%)
  Pallas kernels  11.9 us (8%)
  local copies, waits for them, and re-layouts  1.86 us (1%)
    all_to_all x1, waiting for transfers between devices, shards(): got = lax.all_to_all(send, ('y',) + INNER, 0, 0)  18.8 us
    all_to_all x1, blocking collectives, shards(): got = lax.all_to_all(send, OUTER, 0, 0)  16.6 us
    ppermute x4, starting transfers between devices, swap(): return lax.ppermute(value, axis, [(0, 1), (1, 0)])  14.5 us
    all_to_all x1, blocking collectives, shards(): conv = lax.all_to_all(conv, OUTER, 0, 0)  13.4 us
    all_to_all x1, starting transfers between devices, shards(): lax.all_to_all(gated.reshape(inner * tp, length, chans), INNER + ('tp',),...  12.4 us
    pallas_call x7, Pallas kernels, call(): pl.pallas_call(body, out_shape=out_shape, in_specs=specs[:len(args)], out...  11.9 us
    all_to_all x1, waiting for transfers between devices, shards(): lax.all_to_all(gated.reshape(inner * tp, length, chans), INNER + ('tp',),...  11.2 us
    all_to_all x1, starting transfers between devices, shards(): got = lax.all_to_all(send, ('y',) + INNER, 0, 0)  10.6 us
  transfers between devices with their start and end apart: 10, of which 7 were waited for; matrix products, arithmetic and copies ran while one was open for 1% of the time, Pallas kernels for 3%

profile of v6, /device:TPU:1, one launch (start us, length us, event | category | flops | bytes accessed | tf_op | source)
XLA Modules:
  0.0 149.9 jit_solution(9155829508251287291)
XLA Ops:
  6.5 0.7 all-gather.3.cloned.1.call-update
  7.3 2.0 %weight_gather.2 = bf16[32,5,16,128]{3,2,1,0:T(8,128)(2,1)} custom-call(bf16[3,16,512]{2,1,0:T(8,128)(2,1)} %bitcast.25, bf16[16,512]{1,0:T(8,128)(2,1)} %out_w_hbm.1, f32[128,512]{1,0:T(8,128)} %taps_hbm.1), custom_call_target="tpu_custom_call" | custom-call | tf_op jit(solution)/shard_map/weight_gather/pallas_call | solution.py:28
  9.3 10.6 %all-to-all-start = ((bf16[32,5,16,128]{3,2,1,0:T(8,128)(2,1)}), bf16[32,5,16,128]{3,2,1,0:T(8,128)(2,1)S(1)}, u32[]{:S(2)}, u32[]{:S(2)}) async-start(bf16[32,5,16,128]{3,2,1,0:T(8,128)(2,1)} %weight_gather.2), calls=%async_computation | async-start | bytes 1310720 | tf_op jit(solution)/shard_map/weight_gather/all_to_all | solution.py:317
  19.9 0.8 dynamic-slice_bitcast_fusion.1.skip_ref
  20.7 18.8 %all-to-all-done.got_ref = bf16[32,5,16,128]{3,2,1,0:T(8,128)(2,1)S(1)} async-done(((bf16[32,5,16,128]{3,2,1,0:T(8,128)(2,1)}), bf16[32,5,16,128]{3,2,1,0:T(8,128)(2,1)S(1)}, u32[]{:S(2)}, u32[]{:S(2)}) %all-to-all-start) | async-done | bytes 655392 | tf_op jit(solution)/shard_map/weight_gather/all_to_all | solution.py:317
  39.5 1.5 %weight_gather.3 = bf16[4,136,16,128]{3,2,1,0:T(8,128)(2,1)} custom-call(bf16[32,5,16,128]{3,2,1,0:T(8,128)(2,1)S(1)} %all-to-all-done.got_ref), custom_call_target="tpu_custom_call" | custom-call | tf_op jit(solution)/shard_map/weight_gather/pallas_call | solution.py:28
  41.0 4.0 %all-to-all-start.1 = ((bf16[4,136,16,128]{3,2,1,0:T(8,128)(2,1)}), bf16[4,136,16,128]{3,2,1,0:T(8,128)(2,1)S(1)}, u32[]{:S(2)}, u32[]{:S(2)}) async-start(bf16[4,136,16,128]{3,2,1,0:T(8,128)(2,1)} %weight_gather.3), calls=%async_computation.1 | async-start | bytes 4456448 | tf_op jit(solution)/shard_map/weight_gather/all_to_all | solution.py:320
  45.0 9.1 %all-gather.3.cloned.1.call-done = bf16[1024,512]{1,0:T(8,128)(2,1)} async-done(((bf16[128,512]{1,0:T(8,128)(2,1)}), bf16[1024,512]{1,0:T(8,128)(2,1)}) %all-gather.3.cloned.1.call-update) | async-done | bytes 1048592 | tf_op jit(solution)/shard_map/token_gather/all_gather | solution.py:304
  54.2 5.9 %collective-permute-start = (bf16[8,128,512]{2,1,0:T(8,128)(2,1)}, bf16[8,128,512]{2,1,0:T(8,128)(2,1)}, u32[]{:S(2)}, u32[]{:S(2)}) collective-permute-start(bf16[8,128,512]{2,1,0:T(8,128)(2,1)} %bitcast.19), channel_id=1, source_target_pairs={{0,4},{4,0},{1,5},{5,1},{2,6},{6,2},{3,7},{7,3},{8,12},{12,8},{9,1... | collective-permute-start | bytes 3145736 | tf_op jit(solution)/shard_map/token_swap/ppermute | solution.py:278
  60.1 1.4 token_swap.1
  61.5 3.0 %collective-permute-start.2 = (bf16[4,16,512]{2,1,0:T(8,128)(2,1)}, bf16[4,16,512]{2,1,0:T(8,128)(2,1)S(1)}, u32[]{:S(2)}, u32[]{:S(2)}) collective-permute-start(bf16[4,16,512]{2,1,0:T(8,128)(2,1)} %token_swap.1), channel_id=1, source_target_pairs={{4,16},{20,32},{36,48},{52,64},{68,80},{84,96},{100,112},{116,128}... | collective-permute-start | bytes 196616 | tf_op jit(solution)/shard_map/token_swap/ppermute | solution.py:334
  64.5 3.1 %collective-permute-start.1 = (bf16[4,16,512]{2,1,0:T(8,128)(2,1)}, bf16[4,16,512]{2,1,0:T(8,128)(2,1)S(1)}, u32[]{:S(2)}, u32[]{:S(2)}) collective-permute-start(bf16[4,16,512]{2,1,0:T(8,128)(2,1)} %token_swap.1), channel_id=1, source_target_pairs={{0,16},{16,32},{32,48},{48,64},{64,80},{80,96},{96,112},{112,128},... | collective-permute-start | bytes 196616 | tf_op jit(solution)/shard_map/token_swap/ppermute | solution.py:333
  67.7 0.1 add_bitcast_fusion
  67.8 1.6 %collective-permute-done.2.halo_other_ref = bf16[4,16,512]{2,1,0:T(8,128)(2,1)S(1)} collective-permute-done((bf16[4,16,512]{2,1,0:T(8,128)(2,1)}, bf16[4,16,512]{2,1,0:T(8,128)(2,1)S(1)}, u32[]{:S(2)}, u32[]{:S(2)}) %collective-permute-start.2) | collective-permute-done | bytes 65568 | tf_op jit(solution)/shard_map/token_swap/ppermute | solution.py:334
  69.3 1.4 collective-permute-done.1.halo_own_ref
  70.7 0.5 all-to-all-done.1.got_ref
  71.2 0.0 copy-start.6
  71.2 0.0 copy-start.7
  71.2 0.0 copy-start.8
  71.2 4.0 %project.1 = (f32[512,256]{1,0:T(8,128)S(1)}, bf16[32,16,128]{2,1,0:T(8,128)(2,1)S(1)}, bf16[2048,128]{1,0:T(8,128)(2,1)S(1)}, bf16[512,128]{1,0:T(8,128)(2,1)S(1)}) custom-call(s32[1,1]{1,0:T(1,128)S(1)} %bitcast.24, bf16[8,128,512]{2,1,0:T(8,128)(2,1)S(1)} %bitcast.21, bf16[8,128,512]{2,1,0:T(8,128)(2,1)} %collective-permute-done.other_ref, ...), custom_call_target="tpu_custom_call" | custom-call | tf_op jit(solution)/shard_map/project/pallas_call | solution.py:28
  75.2 4.3 %collective-permute-start.3 = (bf16[2048,128]{1,0:T(8,128)(2,1)S(1)}, bf16[2048,128]{1,0:T(8,128)(2,1)S(1)}, u32[]{:S(2)}, u32[]{:S(2)}) collective-permute-start(bf16[2048,128]{1,0:T(8,128)(2,1)S(1)} %get-tuple-element.13.own_ref), channel_id=1, source_target_pairs={{0,8},{8,0},{1,9},{9,1},{2,10},{10,2},{3,11},{11,3},{4,12},{12,4},... | collective-permute-start | bytes 1572872 | tf_op jit(solution)/shard_map/out_weight_swap/ppermute | solution.py:278
  79.5 16.6 %all_to_all.25.sig_ref = bf16[32,16,128]{2,1,0:T(8,128)(2,1)S(1)} all-to-all(bf16[32,16,128]{2,1,0:T(8,128)(2,1)S(1)} %get-tuple-element.11), channel_id=1, replica_groups=mesh['y'=8,'x'=4,'zl'=2,'co'=2,'tp'=4] {'y','x'}, dimensions={0} | all-to-all | bytes 262144 | tf_op jit(solution)/shard_map/conv/all_to_all | solution.py:362
  96.2 0.9 conv.1
  97.1 13.4 %all_to_all.26.conv_ref = bf16[32,16,128]{2,1,0:T(8,128)(2,1)S(1)} all-to-all(bf16[32,16,128]{2,1,0:T(8,128)(2,1)S(1)} %conv.1), channel_id=1, replica_groups=mesh['y'=8,'x'=4,'zl'=2,'co'=2,'tp'=4] {'y','x'}, dimensions={0} | all-to-all | bytes 262144 | tf_op jit(solution)/shard_map/conv/all_to_all | solution.py:368
  110.5 0.9 gate.1
  111.5 12.4 %all-to-all-start.4 = ((bf16[16,128,128]{2,1,0:T(8,128)(2,1)}), bf16[16,128,128]{2,1,0:T(8,128)(2,1)S(1)}, u32[]{:S(2)}, u32[]{:S(2)}) async-start(bf16[16,128,128]{2,1,0:T(8,128)(2,1)} %bitcast.8), calls=%async_computation.4 | async-start | bytes 1048576 | tf_op jit(solution)/shard_map/gate/all_to_all | solution.py:373
  123.8 2.0 %collective-permute-start.4 = (bf16[2048,128]{1,0:T(8,128)(2,1)}, bf16[2048,128]{1,0:T(8,128)(2,1)S(1)}, u32[]{:S(2)}, u32[]{:S(2)}) collective-permute-start(bf16[2048,128]{1,0:T(8,128)(2,1)} %copy-done.2), channel_id=1, source_target_pairs={{0,4},{4,0},{1,5},{5,1},{2,6},{6,2},{3,7},{7,3},{8,12},{12,8},{9,1... | collective-permute-start | bytes 1572872 | tf_op jit(solution)/shard_map/out_weight_swap/ppermute | solution.py:278
  125.8 2.3 %collective-permute-start.5 = (bf16[2048,128]{1,0:T(8,128)(2,1)S(1)}, bf16[2048,128]{1,0:T(8,128)(2,1)S(1)}, u32[]{:S(2)}, u32[]{:S(2)}) collective-permute-start(bf16[2048,128]{1,0:T(8,128)(2,1)S(1)} %collective-permute-done.3.earlier_ref.near_ref), channel_id=1, source_target_pairs={{0,4},{4,0},{1,5},{5,1},{2,6},{6,2},{3,7},{7,3},{8,12},{12,8},{9,1... | collective-permute-start | bytes 1572872 | tf_op jit(solution)/shard_map/out_weight_swap/ppermute | solution.py:278
  128.2 1.5 %collective-permute-done.5.far_ref = bf16[2048,128]{1,0:T(8,128)(2,1)S(1)} collective-permute-done((bf16[2048,128]{1,0:T(8,128)(2,1)S(1)}, bf16[2048,128]{1,0:T(8,128)(2,1)S(1)}, u32[]{:S(2)}, u32[]{:S(2)}) %collective-permute-start.5) | collective-permute-done | bytes 524320 | tf_op jit(solution)/shard_map/out_weight_swap/ppermute | solution.py:278
  129.7 11.2 %all-to-all-done.4 = bf16[16,128,128]{2,1,0:T(8,128)(2,1)S(1)} async-done(((bf16[16,128,128]{2,1,0:T(8,128)(2,1)}), bf16[16,128,128]{2,1,0:T(8,128)(2,1)S(1)}, u32[]{:S(2)}, u32[]{:S(2)}) %all-to-all-start.4) | async-done | bytes 524320 | tf_op jit(solution)/shard_map/gate/all_to_all | solution.py:373
  140.9 1.0 copy-done.3
  141.9 1.1 out_project.1
  (22 shorter events, 0.1 us)
Async XLA Ops:
  6.5 13.3 %copy-start = (f32[3,3,512]{2,1,0:T(4,128)S(1)}, f32[3,3,512]{2,1,0:T(4,128)}, u32[]{:S(2)}) copy-start(f32[3,3,512]{2,1,0:T(4,128)} %param.15) | copy-start | bytes 55300
  6.5 47.7 %all-gather.3.cloned.1.call-start = ((), (), s32[]{:S(2)}) async-start(), calls=%async_computation.5 | async-start | bytes 1179648 | tf_op jit(solution)/shard_map/token_gather/all_gather | solution.py:304
  9.3 30.2 %all-to-all-start = ((bf16[32,5,16,128]{3,2,1,0:T(8,128)(2,1)}), bf16[32,5,16,128]{3,2,1,0:T(8,128)(2,1)S(1)}, u32[]{:S(2)}, u32[]{:S(2)}) async-start(bf16[32,5,16,128]{3,2,1,0:T(8,128)(2,1)} %weight_gather.2), calls=%async_computation | async-start | bytes 1310720 | tf_op jit(solution)/shard_map/weight_gather/all_to_all | solution.py:317
  41.0 30.2 %all-to-all-start.1 = ((bf16[4,136,16,128]{3,2,1,0:T(8,128)(2,1)}), bf16[4,136,16,128]{3,2,1,0:T(8,128)(2,1)S(1)}, u32[]{:S(2)}, u32[]{:S(2)}) async-start(bf16[4,136,16,128]{3,2,1,0:T(8,128)(2,1)} %weight_gather.3), calls=%async_computation.1 | async-start | bytes 4456448 | tf_op jit(solution)/shard_map/weight_gather/all_to_all | solution.py:320
  54.2 17.0 %copy-start.1 = (bf16[1024,512]{1,0:T(8,128)(2,1)S(1)}, bf16[1024,512]{1,0:T(8,128)(2,1)}, u32[]{:S(2)}) copy-start(bf16[1024,512]{1,0:T(8,128)(2,1)} %all-gather.3.cloned.1.call-done) | copy-start | bytes 3145732
  54.2 17.0 %copy-start.9 = (f32[2048]{0:T(1024)S(1)}, f32[2048]{0:T(1024)}, u32[]{:S(2)}) copy-start(f32[2048]{0:T(1024)} %param.13) | copy-start | bytes 24580
  54.2 16.5 %collective-permute-start = (bf16[8,128,512]{2,1,0:T(8,128)(2,1)}, bf16[8,128,512]{2,1,0:T(8,128)(2,1)}, u32[]{:S(2)}, u32[]{:S(2)}) collective-permute-start(bf16[8,128,512]{2,1,0:T(8,128)(2,1)} %bitcast.19), channel_id=1, source_target_pairs={{0,4},{4,0},{1,5},{5,1},{2,6},{6,2},{3,7},{7,3},{8,12},{12,8},{9,1... | collective-permute-start | bytes 3145736 | tf_op jit(solution)/shard_map/token_swap/ppermute | solution.py:278
  61.5 7.8 %collective-permute-start.2 = (bf16[4,16,512]{2,1,0:T(8,128)(2,1)}, bf16[4,16,512]{2,1,0:T(8,128)(2,1)S(1)}, u32[]{:S(2)}, u32[]{:S(2)}) collective-permute-start(bf16[4,16,512]{2,1,0:T(8,128)(2,1)} %token_swap.1), channel_id=1, source_target_pairs={{4,16},{20,32},{36,48},{52,64},{68,80},{84,96},{100,112},{116,128}... | collective-permute-start | bytes 196616 | tf_op jit(solution)/shard_map/token_swap/ppermute | solution.py:334
  64.5 6.2 %collective-permute-start.1 = (bf16[4,16,512]{2,1,0:T(8,128)(2,1)}, bf16[4,16,512]{2,1,0:T(8,128)(2,1)S(1)}, u32[]{:S(2)}, u32[]{:S(2)}) collective-permute-start(bf16[4,16,512]{2,1,0:T(8,128)(2,1)} %token_swap.1), channel_id=1, source_target_pairs={{0,16},{16,32},{32,48},{48,64},{64,80},{80,96},{96,112},{112,128},... | collective-permute-start | bytes 196616 | tf_op jit(solution)/shard_map/token_swap/ppermute | solution.py:333
  71.2 24.9 %copy-start.4 = (bf16[256,256]{1,0:T(8,128)(2,1)S(1)}, bf16[256,256]{1,0:T(8,128)(2,1)}, u32[]{:S(2)}) copy-start(bf16[256,256]{1,0:T(8,128)(2,1)} %constant.35.clone.near_out_ref) | copy-start | bytes 393220
  71.2 24.9 %copy-start.5 = (f32[2,128,128]{2,1,0:T(8,128)S(1)}, f32[2,128,128]{2,1,0:T(8,128)}, u32[]{:S(2)}) copy-start(f32[2,128,128]{2,1,0:T(8,128)} %constant.34.clone.turn_ref) | copy-start | bytes 393220
  71.2 24.9 %copy-start.6 = (bf16[256,256]{1,0:T(8,128)(2,1)S(1)}, bf16[256,256]{1,0:T(8,128)(2,1)}, u32[]{:S(2)}) copy-start(bf16[256,256]{1,0:T(8,128)(2,1)} %constant.33.clone.near_in_ref) | copy-start | bytes 393220
  71.2 24.9 %copy-start.7 = (bf16[128,256]{1,0:T(8,128)(2,1)S(1)}, bf16[128,256]{1,0:T(8,128)(2,1)}, u32[]{:S(2)}) copy-start(bf16[128,256]{1,0:T(8,128)(2,1)} %constant.36.clone.back_ref) | copy-start | bytes 196612
  71.2 24.9 %copy-start.8 = (bf16[256,128]{1,0:T(8,128)(2,1)S(1)}, bf16[256,128]{1,0:T(8,128)(2,1)}, u32[]{:S(2)}) copy-start(bf16[256,128]{1,0:T(8,128)(2,1)} %constant.32.clone.into_ref) | copy-start | bytes 196612
  75.2 36.3 %copy-start.2 = (bf16[2048,128]{1,0:T(8,128)(2,1)}, bf16[2048,128]{1,0:T(8,128)(2,1)S(1)}, u32[]{:S(2)}) copy-start(bf16[2048,128]{1,0:T(8,128)(2,1)S(1)} %get-tuple-element.13.own_ref) | copy-start | bytes 1572868
  75.2 20.9 %collective-permute-start.3 = (bf16[2048,128]{1,0:T(8,128)(2,1)S(1)}, bf16[2048,128]{1,0:T(8,128)(2,1)S(1)}, u32[]{:S(2)}, u32[]{:S(2)}) collective-permute-start(bf16[2048,128]{1,0:T(8,128)(2,1)S(1)} %get-tuple-element.13.own_ref), channel_id=1, source_target_pairs={{0,8},{8,0},{1,9},{9,1},{2,10},{10,2},{3,11},{11,3},{4,12},{12,4},... | collective-permute-start | bytes 1572872 | tf_op jit(solution)/shard_map/out_weight_swap/ppermute | solution.py:278
  111.5 29.4 %all-to-all-start.4 = ((bf16[16,128,128]{2,1,0:T(8,128)(2,1)}), bf16[16,128,128]{2,1,0:T(8,128)(2,1)S(1)}, u32[]{:S(2)}, u32[]{:S(2)}) async-start(bf16[16,128,128]{2,1,0:T(8,128)(2,1)} %bitcast.8), calls=%async_computation.4 | async-start | bytes 1048576 | tf_op jit(solution)/shard_map/gate/all_to_all | solution.py:373
  123.8 4.3 %collective-permute-start.4 = (bf16[2048,128]{1,0:T(8,128)(2,1)}, bf16[2048,128]{1,0:T(8,128)(2,1)S(1)}, u32[]{:S(2)}, u32[]{:S(2)}) collective-permute-start(bf16[2048,128]{1,0:T(8,128)(2,1)} %copy-done.2), channel_id=1, source_target_pairs={{0,4},{4,0},{1,5},{5,1},{2,6},{6,2},{3,7},{7,3},{8,12},{12,8},{9,1... | collective-permute-start | bytes 1572872 | tf_op jit(solution)/shard_map/out_weight_swap/ppermute | solution.py:278
  125.8 3.8 %collective-permute-start.5 = (bf16[2048,128]{1,0:T(8,128)(2,1)S(1)}, bf16[2048,128]{1,0:T(8,128)(2,1)S(1)}, u32[]{:S(2)}, u32[]{:S(2)}) collective-permute-start(bf16[2048,128]{1,0:T(8,128)(2,1)S(1)} %collective-permute-done.3.earlier_ref.near_ref), channel_id=1, source_target_pairs={{0,4},{4,0},{1,5},{5,1},{2,6},{6,2},{3,7},{7,3},{8,12},{12,8},{9,1... | collective-permute-start | bytes 1572872 | tf_op jit(solution)/shard_map/out_weight_swap/ppermute | solution.py:278
  140.9 1.0 copy-start.3
Sparse Core Ops, SparseCore 0:
  9.4 44.7 all-gather.2

commit v7 on v6

--- a/solution.py
+++ b/solution.py
@@ -90,7 +90,6 @@
     turn_ref,
     near_out_ref,
     back_ref,
-    earlier_ref,
     out_ref,
     both_ref,
     result_ref,
@@ -145,11 +144,12 @@
     finish(started([(send_ref, send_hbm)], sems, len(copies)))
 
 
-def repack_body(got_ref, send_ref):
+def repack_body(got_ref, send_ref, out_w_ref):
     sources, kinds, rows, lanes = got_ref.shape
     ways, tiles = send_ref.shape[0], send_ref.shape[1]
-    parts = kinds - 1
-    taps = got_ref[:, parts].astype(F32)
+    parts = kinds - 2
+    out_w_ref[...] = got_ref[:, parts]
+    taps = got_ref[:, parts + 1].astype(F32)
     per = rows // ways
     for way in range(ways):
         for part in range(parts):
@@ -171,7 +171,6 @@
     got_ref,
     gates_ref,
     send_ref,
-    out_w_ref,
     filter_ref,
     x_ref,
     proj_ref,
@@ -195,8 +194,7 @@
         ]
         return jnp.concatenate(pieces, axis=0)
 
-    out_w_ref[...] = column(parts)
-    first = (parts + 1) * sources
+    first = parts * sources
     for y in range(outer):
         for x in range(ways):
             at = (y * ways + x) * rows
@@ -259,15 +257,25 @@
             out_ref[b, p] = gated
 
 
-def out_body(place_ref, gated_ref, own_ref, near_ref, across_ref, far_ref, out_ref):
-    place = place_ref[0, 0]
+def out_body(core_ref, gated_ref, own_ref, other_ref, out_ref):
+    core = core_ref[0, 0]
     inner, tp, rows, chans = gated_ref.shape
+    cores = other_ref.shape[0] // own_ref.shape[0] + 1
+    zs = inner // cores
+    ways = own_ref.shape[0] // zs
     x = jnp.concatenate([gated_ref[s, p] for p in range(tp) for s in range(inner)], axis=1)
-    weight = jnp.concatenate([own_ref[...], near_ref[...], across_ref[...], far_ref[...]], axis=1)
+
+    def column(ref, z):
+        pieces = [ref[x * zs + z, y] for y in range(ref.shape[1]) for x in range(ways)]
+        return jnp.concatenate(pieces, axis=0)
+
+    weight = jnp.concatenate([column(ref, z) for ref in (own_ref, other_ref) for z in range(zs)], axis=1)
     out = jnp.dot(x, weight, preferred_element_type=F32).astype(BF16)
-    for k, flip in enumerate((0, 2, 1, 3)):
-        at = pl.multiple_of((place ^ flip) * chans, chans)
-        out_ref[:, pl.ds(at, chans)] = out[:, k * chans : (k + 1) * chans]
+    for side, at_core in enumerate((core, cores - 1 - core)):
+        for z in range(zs):
+            k = side * zs + z
+            at = pl.multiple_of((z * cores + at_core) * chans, chans)
+            out_ref[:, pl.ds(at, chans)] = out[:, k * chans : (k + 1) * chans]
 
 
 def shape(dims, dtype):
@@ -315,8 +323,11 @@
             limit=60,
         )
         got = lax.all_to_all(send, ("y",) + INNER, 0, 0)
-        tiles = (kinds - 1) * along * inner + along
-        send = call(repack_body, shape((across, tiles, depth, LANES), BF16), "vv", (got,))
+        tiles = parts * along * inner + along
+        piece_w = shape((along * inner, depth, LANES), BF16)
+        send, piece = call(
+            repack_body, (shape((across, tiles, depth, LANES), BF16), piece_w), "vvv", (got,)
+        )
         got = lax.all_to_all(send, "x", 0, 0)
     with jax.named_scope("token_swap"):
         own, _ = lax.optimization_barrier((own, send))
@@ -336,6 +347,8 @@
             OUTER + ("co",),
             [(i * cores + cores - 1, (i + 1) * cores) for i in range(outer - 1)],
         )
+    with jax.named_scope("out_weight_gather"):
+        out_w = lax.all_gather(piece.reshape(along, inner * depth, LANES), ("x", "zl"), axis=0)
     with jax.named_scope("project"):
         own_taps = lax.dynamic_slice_in_dim(short_taps, place * chans, chans, 2)
         own_taps = own_taps.reshape(short_taps.shape[0], parts * chans)
@@ -343,31 +356,28 @@
         blocks = shape((outer, rows, LANES), BF16)
         wide = shape((HALO + inner * length, tp * feats), BF16)
         proj = shape((HALO + inner * length, parts * chans), F32)
-        gates, send, out_w, taps = call(
+        gates, send, taps = call(
             functools.partial(project_body, cores),
             (
                 shape((inner * length, 2 * chans), F32),
                 blocks,
-                shape((outer * inner * depth, chans), BF16),
                 shape((outer * rows, LANES), BF16),
             ),
-            "s" + "v" * 12,
+            "s" + "v" * 11,
             (where[:, :1], own, other, halo_own, halo_other)
             + (norm_gain.reshape(1, tp * feats), own_taps, own_skip, got),
             held(wide, proj),
         )
-    with jax.named_scope("out_weight_swap"):
-        near_w = swap(out_w, "zl")
     with jax.named_scope("conv"):
         got = lax.all_to_all(send, OUTER, 0, 0)
         names = ("into", "near_in", "turn", "near_out", "back")
-        operands = (got, taps) + tuple(tables[name] for name in names) + (near_w,)
+        operands = (got, taps) + tuple(tables[name] for name in names)
         count = outer * rows
         held_rows = [pltpu.VMEM((2, count, LANES), F32), pltpu.VMEM((count, LANES), F32)]
-        conv = call(conv_body, blocks, "v" * (len(operands) - 1) + "hv", operands, held_rows)
+        conv = call(conv_body, blocks, "v" * (len(operands) + 1), operands, held_rows)
         conv = lax.all_to_all(conv, OUTER, 0, 0)
     with jax.named_scope("out_weight_swap"):
-        across_w = swap(out_w, "co"), swap(near_w, "co")
+        other_w = swap(out_w, "co")
     with jax.named_scope("gate"):
         gated = call(gate_body, shape((inner, tp, length, chans), BF16), "vvv", (conv, gates))
         gated = lax.all_to_all(
@@ -377,8 +387,8 @@
         return call(
             out_body,
             shape((length, out_weight.shape[1]), BF16),
-            "svvvvvv",
-            (place.astype(jnp.int32).reshape(1, 1), gated, out_w, near_w, *across_w),
+            "svvvv",
+            (where[:, :1], gated, out_w, other_w),
         )
 
 

time: 151 us -> 142 us (0.940)
  blocking collectives: 30.1 us -> 18 us
  waiting for transfers between devices: 44.8 us -> 49 us
    all_to_all x1 -> x0, blocking collectives: 13.4 us -> none  [shards(): conv = lax.all_to_all(conv, OUTER, 0, 0)]
    all_to_all x1, waiting for transfers between devices: 11.2 us -> 16.9 us  [shards(): lax.all_to_all(gated.reshape(inner * tp, length, chans), INNER + ('tp',),...]
    all_to_all x0 -> x1, starting transfers between devices: none -> 3.85 us  [shards(): conv = lax.all_to_all(conv, OUTER, 0, 0)]
    all_to_all x1, starting transfers between devices: 12.4 us -> 9.17 us  [shards(): lax.all_to_all(gated.reshape(inner * tp, length, chans), INNER + ('tp',),...]
    all_gather x0 -> x1, waiting for transfers between devices: none -> 1.71 us  [shards(): lax.all_gather(piece.reshape(along, inner * depth, LANES), ('x', 'zl'), a...]
    ppermute x4 -> x2, starting transfers between devices: 14.5 us -> 13.5 us  [swap(): return lax.ppermute(value, axis, [(0, 1), (1, 0)])]
  transfers between devices with their start and end apart: 10 -> 10, of which waited for: 7 -> 6; matrix products, arithmetic and copies ran while one was open for 1% -> 1% of each run, Pallas kernels for 3% -> 8%
where the time goes in v7:
time: 142 us
  waiting for transfers between devices  49 us (35%)
  starting transfers between devices  47.5 us (33%)
  blocking collectives  18 us (13%)
  between operations  13.6 us (10%)
  Pallas kernels  12.5 us (9%)
    all_to_all x1, waiting for transfers between devices, shards(): got = lax.all_to_all(send, ('y',) + INNER, 0, 0)  18.8 us
    all_to_all x1, blocking collectives, shards(): got = lax.all_to_all(send, OUTER, 0, 0)  18 us
    all_to_all x1, waiting for transfers between devices, shards(): lax.all_to_all(gated.reshape(inner * tp, length, chans), INNER + ('tp',),...  16.9 us
    ppermute x2, starting transfers between devices, swap(): return lax.ppermute(value, axis, [(0, 1), (1, 0)])  13.5 us
    pallas_call x7, Pallas kernels, call(): pl.pallas_call(body, out_shape=out_shape, in_specs=specs[:len(args)], out...  12.5 us
    all_to_all x1, starting transfers between devices, shards(): got = lax.all_to_all(send, ('y',) + INNER, 0, 0)  10.6 us
    all_to_all x1, starting transfers between devices, shards(): lax.all_to_all(gated.reshape(inner * tp, length, chans), INNER + ('tp',),...  9.17 us
    all_gather x1, waiting for transfers between devices, shards(): own = lax.all_gather(tokens, ('tp', 'zl'), axis=0)  8.48 us
  transfers between devices with their start and end apart: 10, of which 6 were waited for; matrix products, arithmetic and copies ran while one was open for 1% of the time, Pallas kernels for 8%

profile of v7, /device:TPU:1, one launch (start us, length us, event | category | flops | bytes accessed | tf_op | source)
XLA Modules:
  0.0 141.5 jit_solution(5591910596984768875)
XLA Ops:
  6.5 0.7 all-gather.6.cloned.1.call-update
  7.3 2.0 %weight_gather.2 = bf16[32,5,16,128]{3,2,1,0:T(8,128)(2,1)} custom-call(bf16[3,16,512]{2,1,0:T(8,128)(2,1)} %bitcast.26, bf16[16,512]{1,0:T(8,128)(2,1)} %out_w_hbm.1, f32[128,512]{1,0:T(8,128)} %taps_hbm.1), custom_call_target="tpu_custom_call" | custom-call | tf_op jit(solution)/shard_map/weight_gather/pallas_call | solution.py:28
  9.3 10.6 %all-to-all-start = ((bf16[32,5,16,128]{3,2,1,0:T(8,128)(2,1)}), bf16[32,5,16,128]{3,2,1,0:T(8,128)(2,1)S(1)}, u32[]{:S(2)}, u32[]{:S(2)}) async-start(bf16[32,5,16,128]{3,2,1,0:T(8,128)(2,1)} %weight_gather.2), calls=%async_computation | async-start | bytes 1310720 | tf_op jit(solution)/shard_map/weight_gather/all_to_all | solution.py:325
  19.9 0.8 dynamic-slice_bitcast_fusion.1.skip_ref
  20.7 18.8 %all-to-all-done.got_ref = bf16[32,5,16,128]{3,2,1,0:T(8,128)(2,1)S(1)} async-done(((bf16[32,5,16,128]{3,2,1,0:T(8,128)(2,1)}), bf16[32,5,16,128]{3,2,1,0:T(8,128)(2,1)S(1)}, u32[]{:S(2)}, u32[]{:S(2)}) %all-to-all-start) | async-done | bytes 655392 | tf_op jit(solution)/shard_map/weight_gather/all_to_all | solution.py:325
  39.5 1.5 %weight_gather.3 = (bf16[4,104,16,128]{3,2,1,0:T(8,128)(2,1)}, bf16[32,16,128]{2,1,0:T(8,128)(2,1)}) custom-call(bf16[32,5,16,128]{3,2,1,0:T(8,128)(2,1)S(1)} %all-to-all-done.got_ref), custom_call_target="tpu_custom_call" | custom-call | tf_op jit(solution)/shard_map/weight_gather/pallas_call | solution.py:28
  41.0 4.0 %all-to-all-start.1 = ((bf16[4,104,16,128]{3,2,1,0:T(8,128)(2,1)}), bf16[4,104,16,128]{3,2,1,0:T(8,128)(2,1)S(1)}, u32[]{:S(2)}, u32[]{:S(2)}) async-start(bf16[4,104,16,128]{3,2,1,0:T(8,128)(2,1)} %get-tuple-element.11), calls=%async_computation.1 | async-start | bytes 3407872 | tf_op jit(solution)/shard_map/weight_gather/all_to_all | solution.py:331
  45.0 0.7 all-gather.4.cloned.1.call-update
  45.7 8.5 %all-gather.6.cloned.1.call-done = bf16[1024,512]{1,0:T(8,128)(2,1)} async-done(((bf16[128,512]{1,0:T(8,128)(2,1)}), bf16[1024,512]{1,0:T(8,128)(2,1)}) %all-gather.6.cloned.1.call-update) | async-done | bytes 1048592 | tf_op jit(solution)/shard_map/token_gather/all_gather | solution.py:312
  54.2 5.9 %collective-permute-start = (bf16[8,128,512]{2,1,0:T(8,128)(2,1)}, bf16[8,128,512]{2,1,0:T(8,128)(2,1)}, u32[]{:S(2)}, u32[]{:S(2)}) collective-permute-start(bf16[8,128,512]{2,1,0:T(8,128)(2,1)} %bitcast.19), channel_id=1, source_target_pairs={{0,4},{4,0},{1,5},{5,1},{2,6},{6,2},{3,7},{7,3},{8,12},{12,8},{9,1... | collective-permute-start | bytes 3145736 | tf_op jit(solution)/shard_map/token_swap/ppermute | solution.py:286
  60.1 1.4 %token_swap.1 = bf16[4,16,512]{2,1,0:T(8,128)(2,1)} custom-call(bf16[8,128,512]{2,1,0:T(8,128)(2,1)} %bitcast.20), custom_call_target="tpu_custom_call" | custom-call | flops 20000000000 | bytes 1048576 | tf_op jit(solution)/shard_map/token_swap/pallas_call | solution.py:28
  61.5 3.1 %collective-permute-start.1 = (bf16[4,16,512]{2,1,0:T(8,128)(2,1)}, bf16[4,16,512]{2,1,0:T(8,128)(2,1)S(1)}, u32[]{:S(2)}, u32[]{:S(2)}) collective-permute-start(bf16[4,16,512]{2,1,0:T(8,128)(2,1)} %token_swap.1), channel_id=1, source_target_pairs={{0,16},{16,32},{32,48},{48,64},{64,80},{80,96},{96,112},{112,128},... | collective-permute-start | bytes 196616 | tf_op jit(solution)/shard_map/token_swap/ppermute | solution.py:344
  64.6 3.3 %collective-permute-start.2 = (bf16[4,16,512]{2,1,0:T(8,128)(2,1)}, bf16[4,16,512]{2,1,0:T(8,128)(2,1)S(1)}, u32[]{:S(2)}, u32[]{:S(2)}) collective-permute-start(bf16[4,16,512]{2,1,0:T(8,128)(2,1)} %token_swap.1), channel_id=1, source_target_pairs={{4,16},{20,32},{36,48},{52,64},{68,80},{84,96},{100,112},{116,128}... | collective-permute-start | bytes 196616 | tf_op jit(solution)/shard_map/token_swap/ppermute | solution.py:345
  68.0 0.1 add_bitcast_fusion
  68.0 0.0 collective-permute-done.1.halo_own_ref
  68.0 1.5 %collective-permute-done.2.halo_other_ref = bf16[4,16,512]{2,1,0:T(8,128)(2,1)S(1)} collective-permute-done((bf16[4,16,512]{2,1,0:T(8,128)(2,1)}, bf16[4,16,512]{2,1,0:T(8,128)(2,1)S(1)}, u32[]{:S(2)}, u32[]{:S(2)}) %collective-permute-start.2) | collective-permute-done | bytes 65568 | tf_op jit(solution)/shard_map/token_swap/ppermute | solution.py:345
  69.6 0.0 copy-start.3
  69.6 0.0 copy-start.4
  69.6 0.0 copy-start.5
  69.6 0.0 copy-start.6
  69.7 0.0 copy-start.7
  69.7 3.9 %project.1 = (f32[512,256]{1,0:T(8,128)S(1)}, bf16[32,16,128]{2,1,0:T(8,128)(2,1)S(1)}, bf16[512,128]{1,0:T(8,128)(2,1)S(1)}) custom-call(s32[1,1]{1,0:T(1,128)S(1)} %bitcast.24, bf16[8,128,512]{2,1,0:T(8,128)(2,1)S(1)} %bitcast.21, bf16[8,128,512]{2,1,0:T(8,128)(2,1)} %collective-permute-done.other_ref, ...), custom_call_target="tpu_custom_call" | custom-call | tf_op jit(solution)/shard_map/project/pallas_call | solution.py:28
  73.6 18.0 %all_to_all.25.sig_ref = bf16[32,16,128]{2,1,0:T(8,128)(2,1)S(1)} all-to-all(bf16[32,16,128]{2,1,0:T(8,128)(2,1)S(1)} %get-tuple-element.13), channel_id=1, replica_groups=mesh['y'=8,'x'=4,'zl'=2,'co'=2,'tp'=4] {'y','x'}, dimensions={0} | all-to-all | bytes 262144 | tf_op jit(solution)/shard_map/conv/all_to_all | solution.py:372
  91.6 1.6 %conv.1 = bf16[32,16,128]{2,1,0:T(8,128)(2,1)} custom-call(bf16[32,16,128]{2,1,0:T(8,128)(2,1)S(1)} %all_to_all.25.sig_ref, bf16[512,128]{1,0:T(8,128)(2,1)S(1)} %get-tuple-element.14.taps_ref, bf16[256,128]{1,0:T(8,128)(2,1)S(1)} %copy-done.6, bf16[256,256]{1,0:T(8,128)(2,1)S(1)} %copy-done.3, f32[2,128,128]{2,1,0:T(8,128)S(1)} %copy-done.4, ...), custom_call_target="tpu_custom_call" | custom-call | tf_op jit(solution)/shard_map/conv/pallas_call | solution.py:28
  93.2 3.9 %all-to-all-start.3 = ((bf16[32,16,128]{2,1,0:T(8,128)(2,1)}), bf16[32,16,128]{2,1,0:T(8,128)(2,1)S(1)}, u32[]{:S(2)}, u32[]{:S(2)}) async-start(bf16[32,16,128]{2,1,0:T(8,128)(2,1)} %conv.1), calls=%async_computation.3 | async-start | bytes 262144 | tf_op jit(solution)/shard_map/conv/all_to_all | solution.py:378
  97.1 1.7 %all-gather.4.cloned.1.call-done.own_ref = bf16[8,8,64,128]{3,2,1,0:T(8,128)(2,1)} async-done(((bf16[1,8,64,128]{3,2,1,0:T(8,128)(2,1)}), bf16[8,8,64,128]{3,2,1,0:T(8,128)(2,1)}) %all-gather.4.cloned.1.call-update) | async-done | bytes 1048592 | tf_op jit(solution)/shard_map/out_weight_gather/all_gather | solution.py:351
  98.8 7.6 %collective-permute-start.3 = (bf16[8,8,64,128]{3,2,1,0:T(8,128)(2,1)}, bf16[8,8,64,128]{3,2,1,0:T(8,128)(2,1)S(1)}, u32[]{:S(2)}, u32[]{:S(2)}) collective-permute-start(bf16[8,8,64,128]{3,2,1,0:T(8,128)(2,1)} %all-gather.4.cloned.1.call-done.own_ref), channel_id=1, source_target_pairs={{0,4},{4,0},{1,5},{5,1},{2,6},{6,2},{3,7},{7,3},{8,12},{12,8},{9,1... | collective-permute-start | bytes 3145736 | tf_op jit(solution)/shard_map/out_weight_swap/ppermute | solution.py:286
  106.4 0.1 all-to-all-done.3.conv_ref
  106.5 0.9 gate.1
  107.4 9.2 %all-to-all-start.4 = ((bf16[16,128,128]{2,1,0:T(8,128)(2,1)}), bf16[16,128,128]{2,1,0:T(8,128)(2,1)S(1)}, u32[]{:S(2)}, u32[]{:S(2)}) async-start(bf16[16,128,128]{2,1,0:T(8,128)(2,1)} %bitcast.7), calls=%async_computation.4 | async-start | bytes 1048576 | tf_op jit(solution)/shard_map/gate/all_to_all | solution.py:383
  116.6 16.9 %all-to-all-done.4 = bf16[16,128,128]{2,1,0:T(8,128)(2,1)S(1)} async-done(((bf16[16,128,128]{2,1,0:T(8,128)(2,1)}), bf16[16,128,128]{2,1,0:T(8,128)(2,1)S(1)}, u32[]{:S(2)}, u32[]{:S(2)}) %all-to-all-start.4) | async-done | bytes 524320 | tf_op jit(solution)/shard_map/gate/all_to_all | solution.py:383
  133.6 1.1 out_project.1
  (20 shorter events, 0.1 us)
Async XLA Ops:
  6.5 13.3 %copy-start = (f32[3,3,512]{2,1,0:T(4,128)S(1)}, f32[3,3,512]{2,1,0:T(4,128)}, u32[]{:S(2)}) copy-start(f32[3,3,512]{2,1,0:T(4,128)} %param.15) | copy-start | bytes 55300
  6.5 47.6 %all-gather.6.cloned.1.call-start = ((), (), s32[]{:S(2)}) async-start(), calls=%async_computation.6 | async-start | bytes 1179648 | tf_op jit(solution)/shard_map/token_gather/all_gather | solution.py:312
  9.3 30.2 %all-to-all-start = ((bf16[32,5,16,128]{3,2,1,0:T(8,128)(2,1)}), bf16[32,5,16,128]{3,2,1,0:T(8,128)(2,1)S(1)}, u32[]{:S(2)}, u32[]{:S(2)}) async-start(bf16[32,5,16,128]{3,2,1,0:T(8,128)(2,1)} %weight_gather.2), calls=%async_computation | async-start | bytes 1310720 | tf_op jit(solution)/shard_map/weight_gather/all_to_all | solution.py:325
  41.0 28.6 %all-to-all-start.1 = ((bf16[4,104,16,128]{3,2,1,0:T(8,128)(2,1)}), bf16[4,104,16,128]{3,2,1,0:T(8,128)(2,1)S(1)}, u32[]{:S(2)}, u32[]{:S(2)}) async-start(bf16[4,104,16,128]{3,2,1,0:T(8,128)(2,1)} %get-tuple-element.11), calls=%async_computation.1 | async-start | bytes 3407872 | tf_op jit(solution)/shard_map/weight_gather/all_to_all | solution.py:331
  45.0 53.8 %all-gather.4.cloned.1.call-start = ((), (), s32[]{:S(2)}) async-start(), calls=%async_computation.5 | async-start | bytes 1179648 | tf_op jit(solution)/shard_map/out_weight_gather/all_gather | solution.py:351
  54.2 15.4 %copy-start.1 = (bf16[1024,512]{1,0:T(8,128)(2,1)S(1)}, bf16[1024,512]{1,0:T(8,128)(2,1)}, u32[]{:S(2)}) copy-start(bf16[1024,512]{1,0:T(8,128)(2,1)} %all-gather.6.cloned.1.call-done) | copy-start | bytes 3145732
  54.2 15.4 %copy-start.8 = (f32[2048]{0:T(1024)S(1)}, f32[2048]{0:T(1024)}, u32[]{:S(2)}) copy-start(f32[2048]{0:T(1024)} %param.13) | copy-start | bytes 24580
  54.2 15.4 %collective-permute-start = (bf16[8,128,512]{2,1,0:T(8,128)(2,1)}, bf16[8,128,512]{2,1,0:T(8,128)(2,1)}, u32[]{:S(2)}, u32[]{:S(2)}) collective-permute-start(bf16[8,128,512]{2,1,0:T(8,128)(2,1)} %bitcast.19), channel_id=1, source_target_pairs={{0,4},{4,0},{1,5},{5,1},{2,6},{6,2},{3,7},{7,3},{8,12},{12,8},{9,1... | collective-permute-start | bytes 3145736 | tf_op jit(solution)/shard_map/token_swap/ppermute | solution.py:286
  61.5 6.5 %collective-permute-start.1 = (bf16[4,16,512]{2,1,0:T(8,128)(2,1)}, bf16[4,16,512]{2,1,0:T(8,128)(2,1)S(1)}, u32[]{:S(2)}, u32[]{:S(2)}) collective-permute-start(bf16[4,16,512]{2,1,0:T(8,128)(2,1)} %token_swap.1), channel_id=1, source_target_pairs={{0,16},{16,32},{32,48},{48,64},{64,80},{80,96},{96,112},{112,128},... | collective-permute-start | bytes 196616 | tf_op jit(solution)/shard_map/token_swap/ppermute | solution.py:344
  64.6 4.9 %collective-permute-start.2 = (bf16[4,16,512]{2,1,0:T(8,128)(2,1)}, bf16[4,16,512]{2,1,0:T(8,128)(2,1)S(1)}, u32[]{:S(2)}, u32[]{:S(2)}) collective-permute-start(bf16[4,16,512]{2,1,0:T(8,128)(2,1)} %token_swap.1), channel_id=1, source_target_pairs={{4,16},{20,32},{36,48},{52,64},{68,80},{84,96},{100,112},{116,128}... | collective-permute-start | bytes 196616 | tf_op jit(solution)/shard_map/token_swap/ppermute | solution.py:345
  69.6 22.0 %copy-start.3 = (bf16[256,256]{1,0:T(8,128)(2,1)S(1)}, bf16[256,256]{1,0:T(8,128)(2,1)}, u32[]{:S(2)}) copy-start(bf16[256,256]{1,0:T(8,128)(2,1)} %constant.33.clone.near_in_ref) | copy-start | bytes 393220
  69.6 22.0 %copy-start.4 = (f32[2,128,128]{2,1,0:T(8,128)S(1)}, f32[2,128,128]{2,1,0:T(8,128)}, u32[]{:S(2)}) copy-start(f32[2,128,128]{2,1,0:T(8,128)} %constant.34.clone.turn_ref) | copy-start | bytes 393220
  69.6 22.0 %copy-start.5 = (bf16[256,256]{1,0:T(8,128)(2,1)S(1)}, bf16[256,256]{1,0:T(8,128)(2,1)}, u32[]{:S(2)}) copy-start(bf16[256,256]{1,0:T(8,128)(2,1)} %constant.35.clone.near_out_ref) | copy-start | bytes 393220
  69.6 22.0 %copy-start.6 = (bf16[256,128]{1,0:T(8,128)(2,1)S(1)}, bf16[256,128]{1,0:T(8,128)(2,1)}, u32[]{:S(2)}) copy-start(bf16[256,128]{1,0:T(8,128)(2,1)} %constant.32.clone.into_ref) | copy-start | bytes 196612
  69.7 22.0 %copy-start.7 = (bf16[128,256]{1,0:T(8,128)(2,1)S(1)}, bf16[128,256]{1,0:T(8,128)(2,1)}, u32[]{:S(2)}) copy-start(bf16[128,256]{1,0:T(8,128)(2,1)} %constant.36.clone.back_ref) | copy-start | bytes 196612
  93.2 13.3 %all-to-all-start.3 = ((bf16[32,16,128]{2,1,0:T(8,128)(2,1)}), bf16[32,16,128]{2,1,0:T(8,128)(2,1)S(1)}, u32[]{:S(2)}, u32[]{:S(2)}) async-start(bf16[32,16,128]{2,1,0:T(8,128)(2,1)} %conv.1), calls=%async_computation.3 | async-start | bytes 262144 | tf_op jit(solution)/shard_map/conv/all_to_all | solution.py:378
  98.8 34.7 %copy-start.2 = (bf16[8,8,64,128]{3,2,1,0:T(8,128)(2,1)S(1)}, bf16[8,8,64,128]{3,2,1,0:T(8,128)(2,1)}, u32[]{:S(2)}) copy-start(bf16[8,8,64,128]{3,2,1,0:T(8,128)(2,1)} %all-gather.4.cloned.1.call-done.own_ref) | copy-start | bytes 3145732
  98.8 17.8 %collective-permute-start.3 = (bf16[8,8,64,128]{3,2,1,0:T(8,128)(2,1)}, bf16[8,8,64,128]{3,2,1,0:T(8,128)(2,1)S(1)}, u32[]{:S(2)}, u32[]{:S(2)}) collective-permute-start(bf16[8,8,64,128]{3,2,1,0:T(8,128)(2,1)} %all-gather.4.cloned.1.call-done.own_ref), channel_id=1, source_target_pairs={{0,4},{4,0},{1,5},{5,1},{2,6},{6,2},{3,7},{7,3},{8,12},{12,8},{9,1... | collective-permute-start | bytes 3145736 | tf_op jit(solution)/shard_map/out_weight_swap/ppermute | solution.py:286
  107.4 26.1 %all-to-all-start.4 = ((bf16[16,128,128]{2,1,0:T(8,128)(2,1)}), bf16[16,128,128]{2,1,0:T(8,128)(2,1)S(1)}, u32[]{:S(2)}, u32[]{:S(2)}) async-start(bf16[16,128,128]{2,1,0:T(8,128)(2,1)} %bitcast.7), calls=%async_computation.4 | async-start | bytes 1048576 | tf_op jit(solution)/shard_map/gate/all_to_all | solution.py:383
Sparse Core Ops, SparseCore 0:
  9.4 44.6 all-gather.5
  56.3 42.5 all-gather.3

commit v8 on v7

--- a/solution.py
+++ b/solution.py
@@ -162,7 +162,7 @@
     cores,
     place_ref,
     own_ref,
-    other_ref,
+    other_hbm,
     halo_own_ref,
     halo_other_ref,
     gain_ref,
@@ -172,10 +172,13 @@
     gates_ref,
     send_ref,
     filter_ref,
+    other_ref,
     x_ref,
     proj_ref,
+    sems,
 ):
     core = place_ref[0, 0]
+    copies = started([(other_hbm, other_ref)], sems)
     parts = 3
     ways, _, rows, lanes = got_ref.shape
     groups = send_ref.shape[0]
@@ -208,28 +211,44 @@
         scale = lax.rsqrt(total / (tp * feats) + 1e-05)
         for p, piece in enumerate(pieces):
             gain = gain_ref[:, p * feats : (p + 1) * feats]
-            x_ref[at, p * feats : (p + 1) * feats] = (piece * scale * gain).astype(BF16)
+            x_ref[at : at + piece.shape[0], p * feats : (p + 1) * feats] = (piece * scale * gain).astype(BF16)
+
+    def project(count):
+        got = jnp.dot(x_ref[:count], weight, preferred_element_type=F32)
+        return got.astype(BF16).astype(F32)
 
     zs = blocks // tp
+    weight = jnp.concatenate([column(part) for part in range(parts)], axis=1)
+    last = core == cores - 1
+    halo = [
+        jnp.where(last, halo_own_ref[p].astype(F32), halo_other_ref[p].astype(F32)) for p in range(tp)
+    ]
     for ref, at_core in ((own_ref, core), (other_ref, cores - 1 - core)):
+        if ref is other_ref:
+            finish(copies)
+        for z in range(zs):
+            put([ref[p * zs + z].astype(F32) for p in range(tp)], z * length)
+        if ref is own_ref:
+            put(halo, zs * length)
+            got = project(zs * length + HALO)
+            proj_ref[:HALO] = got[zs * length :]
+        else:
+            got = project(zs * length)
         for z in range(zs):
             at = pl.multiple_of(HALO + (z * cores + at_core) * length, HALO)
-            put([ref[p * zs + z].astype(F32) for p in range(tp)], pl.ds(at, length))
-    last = core == cores - 1
-    put(
-        [jnp.where(last, halo_own_ref[p].astype(F32), halo_other_ref[p].astype(F32)) for p in range(tp)],
-        slice(0, HALO),
-    )
-    weight = jnp.concatenate([column(part) for part in range(parts)], axis=1)
-    proj = jnp.dot(x_ref[...], weight, preferred_element_type=F32)
-    proj_ref[...] = proj.astype(BF16).astype(F32)
-
-    short = taps_ref[0:1] * proj_ref[HALO:]
+            proj_ref[pl.ds(at, length)] = got[z * length : (z + 1) * length]
+
+    mine = pl.ds(pl.multiple_of(place_ref[0, 2] * chans, chans), chans)
+
+    def tap(lag):
+        return jnp.concatenate([taps_ref[lag, part : part + 1, mine] for part in range(parts)], axis=1)
+
+    short = tap(0) * proj_ref[HALO:]
     for lag in range(1, taps_ref.shape[0]):
-        short = short + taps_ref[lag : lag + 1] * proj_ref[HALO - lag : HALO - lag + count]
+        short = short + tap(lag) * proj_ref[HALO - lag : HALO - lag + count]
     signal = short[:, chans : 2 * chans] * short[:, 2 * chans :]
     gates_ref[:, :chans] = short[:, :chans]
-    gates_ref[:, chans:] = skip_ref[...] * signal
+    gates_ref[:, chans:] = skip_ref[:, mine] * signal
     per = send_ref.shape[1] // inner
     pieces = [signal[b * lanes : (b + 1) * lanes].T.reshape(groups, per, lanes) for b in range(inner)]
     send_ref[...] = jnp.concatenate(pieces, axis=1).astype(BF16)
@@ -306,7 +325,7 @@
     depth, parts = in_weight.shape[0], in_weight.shape[1]
     rows = inner * per
     place = lax.axis_index(INNER)
-    where = jnp.stack([lax.axis_index("co"), lax.axis_index("x")]).astype(jnp.int32).reshape(1, 2)
+    where = jnp.stack([lax.axis_index("co"), lax.axis_index("x"), place]).astype(jnp.int32).reshape(1, 3)
 
     with jax.named_scope("token_gather"):
         own = lax.all_gather(tokens, ("tp", "zl"), axis=0)
@@ -350,11 +369,8 @@
     with jax.named_scope("out_weight_gather"):
         out_w = lax.all_gather(piece.reshape(along, inner * depth, LANES), ("x", "zl"), axis=0)
     with jax.named_scope("project"):
-        own_taps = lax.dynamic_slice_in_dim(short_taps, place * chans, chans, 2)
-        own_taps = own_taps.reshape(short_taps.shape[0], parts * chans)
-        own_skip = lax.dynamic_slice_in_dim(skip_gain, place * chans, chans, 0).reshape(1, chans)
         blocks = shape((outer, rows, LANES), BF16)
-        wide = shape((HALO + inner * length, tp * feats), BF16)
+        wide = shape((ways["zl"] * length + HALO, tp * feats), BF16)
         proj = shape((HALO + inner * length, parts * chans), F32)
         gates, send, taps = call(
             functools.partial(project_body, cores),
@@ -363,10 +379,10 @@
                 blocks,
                 shape((outer * rows, LANES), BF16),
             ),
-            "s" + "v" * 11,
-            (where[:, :1], own, other, halo_own, halo_other)
-            + (norm_gain.reshape(1, tp * feats), own_taps, own_skip, got),
-            held(wide, proj),
+            "svh" + "v" * 9,
+            (where, own, other, halo_own, halo_other, norm_gain.reshape(1, tp * feats))
+            + (short_taps, skip_gain.reshape(1, inner * chans), got),
+            held(other, wide, proj) + copies_of(1),
         )
     with jax.named_scope("conv"):
         got = lax.all_to_all(send, OUTER, 0, 0)

time: 142 us -> 142 us (level)
  waiting for transfers between devices: 49 us -> 50.8 us
  transfers between devices with their start and end apart: 10 -> 10, of which waited for: 6 -> 5; matrix products, arithmetic and copies ran while one was open for 1% -> 0% of each run, Pallas kernels for 8% -> 8%
where the time goes in v8:
time: 142 us; the launch traced here: 141 us
  waiting for transfers between devices  50.8 us (36%)
  starting transfers between devices  46.6 us (33%)
  blocking collectives  18 us (13%)
  between operations  13.6 us (10%)
  Pallas kernels  11.9 us (8%)
    all_to_all x1, waiting for transfers between devices, shards(): got = lax.all_to_all(send, ('y',) + INNER, 0, 0)  19.6 us
    all_to_all x1, blocking collectives, shards(): got = lax.all_to_all(send, OUTER, 0, 0)  18 us
    all_to_all x1, waiting for transfers between devices, shards(): lax.all_to_all(gated.reshape(inner * tp, length, chans), INNER + ('tp',),...  16.9 us
    ppermute x2, starting transfers between devices, swap(): return lax.ppermute(value, axis, [(0, 1), (1, 0)])  12.8 us
    pallas_call x7, Pallas kernels, call(): pl.pallas_call(body, out_shape=out_shape, in_specs=specs[:len(args)], out...  11.9 us
    all_to_all x1, starting transfers between devices, shards(): got = lax.all_to_all(send, ('y',) + INNER, 0, 0)  10.6 us
    all_to_all x1, starting transfers between devices, shards(): lax.all_to_all(gated.reshape(inner * tp, length, chans), INNER + ('tp',),...  8.95 us
    all_gather x1, waiting for transfers between devices, shards(): own = lax.all_gather(tokens, ('tp', 'zl'), axis=0)  8.9 us
  transfers between devices with their start and end apart: 10, of which 5 were waited for; matrix products, arithmetic and copies ran while one was open for 0% of the time, Pallas kernels for 8%

profile of v8, /device:TPU:1, one launch (start us, length us, event | category | flops | bytes accessed | tf_op | source)
XLA Modules:
  0.0 141.0 jit_solution(15060122118179957819)
XLA Ops:
  6.5 0.7 all-gather.6.cloned.1.call-update
  7.3 2.0 %weight_gather.2 = bf16[32,5,16,128]{3,2,1,0:T(8,128)(2,1)} custom-call(bf16[3,16,512]{2,1,0:T(8,128)(2,1)} %bitcast.20, bf16[16,512]{1,0:T(8,128)(2,1)} %out_w_hbm.1, f32[128,512]{1,0:T(8,128)} %taps_hbm.1), custom_call_target="tpu_custom_call" | custom-call | tf_op jit(solution)/shard_map/weight_gather/pallas_call | solution.py:28
  9.3 10.6 %all-to-all-start = ((bf16[32,5,16,128]{3,2,1,0:T(8,128)(2,1)}), bf16[32,5,16,128]{3,2,1,0:T(8,128)(2,1)S(1)}, u32[]{:S(2)}, u32[]{:S(2)}) async-start(bf16[32,5,16,128]{3,2,1,0:T(8,128)(2,1)} %weight_gather.2), calls=%async_computation | async-start | bytes 1310720 | tf_op jit(solution)/shard_map/weight_gather/all_to_all | solution.py:344
  19.9 19.6 %all-to-all-done.got_ref = bf16[32,5,16,128]{3,2,1,0:T(8,128)(2,1)S(1)} async-done(((bf16[32,5,16,128]{3,2,1,0:T(8,128)(2,1)}), bf16[32,5,16,128]{3,2,1,0:T(8,128)(2,1)S(1)}, u32[]{:S(2)}, u32[]{:S(2)}) %all-to-all-start) | async-done | bytes 655392 | tf_op jit(solution)/shard_map/weight_gather/all_to_all | solution.py:344
  39.5 1.5 %weight_gather.3 = (bf16[4,104,16,128]{3,2,1,0:T(8,128)(2,1)}, bf16[32,16,128]{2,1,0:T(8,128)(2,1)}) custom-call(bf16[32,5,16,128]{3,2,1,0:T(8,128)(2,1)S(1)} %all-to-all-done.got_ref), custom_call_target="tpu_custom_call" | custom-call | tf_op jit(solution)/shard_map/weight_gather/pallas_call | solution.py:28
  41.0 4.0 %all-to-all-start.1 = ((bf16[4,104,16,128]{3,2,1,0:T(8,128)(2,1)}), bf16[4,104,16,128]{3,2,1,0:T(8,128)(2,1)S(1)}, u32[]{:S(2)}, u32[]{:S(2)}) async-start(bf16[4,104,16,128]{3,2,1,0:T(8,128)(2,1)} %get-tuple-element.11), calls=%async_computation.1 | async-start | bytes 3407872 | tf_op jit(solution)/shard_map/weight_gather/all_to_all | solution.py:350
  45.0 0.7 all-gather.4.cloned.1.call-update
  45.7 8.9 %all-gather.6.cloned.1.call-done = bf16[1024,512]{1,0:T(8,128)(2,1)} async-done(((bf16[128,512]{1,0:T(8,128)(2,1)}), bf16[1024,512]{1,0:T(8,128)(2,1)}) %all-gather.6.cloned.1.call-update) | async-done | bytes 1048592 | tf_op jit(solution)/shard_map/token_gather/all_gather | solution.py:331
  54.6 5.5 %collective-permute-start = (bf16[8,128,512]{2,1,0:T(8,128)(2,1)}, bf16[8,128,512]{2,1,0:T(8,128)(2,1)}, u32[]{:S(2)}, u32[]{:S(2)}) collective-permute-start(bf16[8,128,512]{2,1,0:T(8,128)(2,1)} %bitcast.14), channel_id=1, source_target_pairs={{0,4},{4,0},{1,5},{5,1},{2,6},{6,2},{3,7},{7,3},{8,12},{12,8},{9,1... | collective-permute-start | bytes 3145736 | tf_op jit(solution)/shard_map/token_swap/ppermute | solution.py:305
  60.1 1.4 %token_swap.1 = bf16[4,16,512]{2,1,0:T(8,128)(2,1)} custom-call(bf16[8,128,512]{2,1,0:T(8,128)(2,1)} %bitcast.15), custom_call_target="tpu_custom_call" | custom-call | flops 20000000000 | bytes 1048576 | tf_op jit(solution)/shard_map/token_swap/pallas_call | solution.py:28
  61.5 3.1 %collective-permute-start.1 = (bf16[4,16,512]{2,1,0:T(8,128)(2,1)}, bf16[4,16,512]{2,1,0:T(8,128)(2,1)S(1)}, u32[]{:S(2)}, u32[]{:S(2)}) collective-permute-start(bf16[4,16,512]{2,1,0:T(8,128)(2,1)} %token_swap.1), channel_id=1, source_target_pairs={{0,16},{16,32},{32,48},{48,64},{64,80},{80,96},{96,112},{112,128},... | collective-permute-start | bytes 196616 | tf_op jit(solution)/shard_map/token_swap/ppermute | solution.py:363
  64.6 3.3 %collective-permute-start.2 = (bf16[4,16,512]{2,1,0:T(8,128)(2,1)}, bf16[4,16,512]{2,1,0:T(8,128)(2,1)S(1)}, u32[]{:S(2)}, u32[]{:S(2)}) collective-permute-start(bf16[4,16,512]{2,1,0:T(8,128)(2,1)} %token_swap.1), channel_id=1, source_target_pairs={{4,16},{20,32},{36,48},{52,64},{68,80},{84,96},{100,112},{116,128}... | collective-permute-start | bytes 196616 | tf_op jit(solution)/shard_map/token_swap/ppermute | solution.py:364
  67.9 0.1 add_bitcast_fusion.place_ref
  68.0 1.5 %collective-permute-done.2.halo_other_ref = bf16[4,16,512]{2,1,0:T(8,128)(2,1)S(1)} collective-permute-done((bf16[4,16,512]{2,1,0:T(8,128)(2,1)}, bf16[4,16,512]{2,1,0:T(8,128)(2,1)S(1)}, u32[]{:S(2)}, u32[]{:S(2)}) %collective-permute-start.2) | collective-permute-done | bytes 65568 | tf_op jit(solution)/shard_map/token_swap/ppermute | solution.py:364
  69.6 0.0 all-to-all-done.1.got_ref
  69.6 0.0 collective-permute-done.other_hbm
  69.6 0.0 copy-start.2
  69.6 0.0 copy-start.3
  69.6 0.0 copy-start.4
  69.6 0.0 copy-start.5
  69.6 0.0 copy-start.6
  69.7 3.3 %project.1 = (f32[512,256]{1,0:T(8,128)S(1)}, bf16[32,16,128]{2,1,0:T(8,128)(2,1)S(1)}, bf16[512,128]{1,0:T(8,128)(2,1)S(1)}) custom-call(s32[1,3]{1,0:T(1,128)S(1)} %add_bitcast_fusion.place_ref, bf16[8,128,512]{2,1,0:T(8,128)(2,1)S(1)} %bitcast.16, bf16[8,128,512]{2,1,0:T(8,128)(2,1)} %collective-permute-done.other_hbm, ...), custom_call_target="tpu_custom_call" | custom-call | tf_op jit(solution)/shard_map/project/pallas_call | solution.py:28
  73.0 18.0 %all_to_all.25.sig_ref = bf16[32,16,128]{2,1,0:T(8,128)(2,1)S(1)} all-to-all(bf16[32,16,128]{2,1,0:T(8,128)(2,1)S(1)} %get-tuple-element.13), channel_id=1, replica_groups=mesh['y'=8,'x'=4,'zl'=2,'co'=2,'tp'=4] {'y','x'}, dimensions={0} | all-to-all | bytes 262144 | tf_op jit(solution)/shard_map/conv/all_to_all | solution.py:388
  91.0 1.6 %conv.1 = bf16[32,16,128]{2,1,0:T(8,128)(2,1)} custom-call(bf16[32,16,128]{2,1,0:T(8,128)(2,1)S(1)} %all_to_all.25.sig_ref, bf16[512,128]{1,0:T(8,128)(2,1)S(1)} %get-tuple-element.14.taps_ref, bf16[256,128]{1,0:T(8,128)(2,1)S(1)} %copy-done.5, bf16[256,256]{1,0:T(8,128)(2,1)S(1)} %copy-done.2, f32[2,128,128]{2,1,0:T(8,128)S(1)} %copy-done.3, ...), custom_call_target="tpu_custom_call" | custom-call | tf_op jit(solution)/shard_map/conv/pallas_call | solution.py:28
  92.5 3.9 %all-to-all-start.3 = ((bf16[32,16,128]{2,1,0:T(8,128)(2,1)}), bf16[32,16,128]{2,1,0:T(8,128)(2,1)S(1)}, u32[]{:S(2)}, u32[]{:S(2)}) async-start(bf16[32,16,128]{2,1,0:T(8,128)(2,1)} %conv.1), calls=%async_computation.3 | async-start | bytes 262144 | tf_op jit(solution)/shard_map/conv/all_to_all | solution.py:394
  96.4 2.4 %all-gather.4.cloned.1.call-done.own_ref = bf16[8,8,64,128]{3,2,1,0:T(8,128)(2,1)} async-done(((bf16[1,8,64,128]{3,2,1,0:T(8,128)(2,1)}), bf16[8,8,64,128]{3,2,1,0:T(8,128)(2,1)}) %all-gather.4.cloned.1.call-update) | async-done | bytes 1048592 | tf_op jit(solution)/shard_map/out_weight_gather/all_gather | solution.py:370
  98.8 7.3 %collective-permute-start.3 = (bf16[8,8,64,128]{3,2,1,0:T(8,128)(2,1)}, bf16[8,8,64,128]{3,2,1,0:T(8,128)(2,1)S(1)}, u32[]{:S(2)}, u32[]{:S(2)}) collective-permute-start(bf16[8,8,64,128]{3,2,1,0:T(8,128)(2,1)} %all-gather.4.cloned.1.call-done.own_ref), channel_id=1, source_target_pairs={{0,4},{4,0},{1,5},{5,1},{2,6},{6,2},{3,7},{7,3},{8,12},{12,8},{9,1... | collective-permute-start | bytes 3145736 | tf_op jit(solution)/shard_map/out_weight_swap/ppermute | solution.py:305
  106.1 0.0 all-to-all-done.3.conv_ref
  106.1 0.9 gate.1
  107.0 8.9 %all-to-all-start.4 = ((bf16[16,128,128]{2,1,0:T(8,128)(2,1)}), bf16[16,128,128]{2,1,0:T(8,128)(2,1)S(1)}, u32[]{:S(2)}, u32[]{:S(2)}) async-start(bf16[16,128,128]{2,1,0:T(8,128)(2,1)} %bitcast.8), calls=%async_computation.4 | async-start | bytes 1048576 | tf_op jit(solution)/shard_map/gate/all_to_all | solution.py:399
  116.0 16.9 %all-to-all-done.4 = bf16[16,128,128]{2,1,0:T(8,128)(2,1)S(1)} async-done(((bf16[16,128,128]{2,1,0:T(8,128)(2,1)}), bf16[16,128,128]{2,1,0:T(8,128)(2,1)S(1)}, u32[]{:S(2)}, u32[]{:S(2)}) %all-to-all-start.4) | async-done | bytes 524320 | tf_op jit(solution)/shard_map/gate/all_to_all | solution.py:399
  132.9 1.2 out_project.1
  (19 shorter events, 0.0 us)
Async XLA Ops:
  6.5 48.1 %all-gather.6.cloned.1.call-start = ((), (), s32[]{:S(2)}) async-start(), calls=%async_computation.6 | async-start | bytes 1179648 | tf_op jit(solution)/shard_map/token_gather/all_gather | solution.py:331
  9.3 30.2 %all-to-all-start = ((bf16[32,5,16,128]{3,2,1,0:T(8,128)(2,1)}), bf16[32,5,16,128]{3,2,1,0:T(8,128)(2,1)S(1)}, u32[]{:S(2)}, u32[]{:S(2)}) async-start(bf16[32,5,16,128]{3,2,1,0:T(8,128)(2,1)} %weight_gather.2), calls=%async_computation | async-start | bytes 1310720 | tf_op jit(solution)/shard_map/weight_gather/all_to_all | solution.py:344
  41.0 28.6 %all-to-all-start.1 = ((bf16[4,104,16,128]{3,2,1,0:T(8,128)(2,1)}), bf16[4,104,16,128]{3,2,1,0:T(8,128)(2,1)S(1)}, u32[]{:S(2)}, u32[]{:S(2)}) async-start(bf16[4,104,16,128]{3,2,1,0:T(8,128)(2,1)} %get-tuple-element.11), calls=%async_computation.1 | async-start | bytes 3407872 | tf_op jit(solution)/shard_map/weight_gather/all_to_all | solution.py:350
  45.0 53.8 %all-gather.4.cloned.1.call-start = ((), (), s32[]{:S(2)}) async-start(), calls=%async_computation.5 | async-start | bytes 1179648 | tf_op jit(solution)/shard_map/out_weight_gather/all_gather | solution.py:370
  54.6 15.0 %copy-start.1 = (bf16[1024,512]{1,0:T(8,128)(2,1)S(1)}, bf16[1024,512]{1,0:T(8,128)(2,1)}, u32[]{:S(2)}) copy-start(bf16[1024,512]{1,0:T(8,128)(2,1)} %all-gather.6.cloned.1.call-done) | copy-start | bytes 3145732
  54.6 15.0 %copy-start.7 = (f32[3,3,512]{2,1,0:T(4,128)S(1)}, f32[3,3,512]{2,1,0:T(4,128)}, u32[]{:S(2)}) copy-start(f32[3,3,512]{2,1,0:T(4,128)} %taps_ref.1) | copy-start | bytes 55300
  54.6 15.0 %copy-start.8 = (f32[2048]{0:T(1024)S(1)}, f32[2048]{0:T(1024)}, u32[]{:S(2)}) copy-start(f32[2048]{0:T(1024)} %param.13) | copy-start | bytes 24580
  54.6 15.0 %copy-start.9 = (f32[512]{0:T(512)S(1)}, f32[512]{0:T(512)}, u32[]{:S(2)}) copy-start(f32[512]{0:T(512)} %param.17) | copy-start | bytes 6148
  54.6 15.0 %collective-permute-start = (bf16[8,128,512]{2,1,0:T(8,128)(2,1)}, bf16[8,128,512]{2,1,0:T(8,128)(2,1)}, u32[]{:S(2)}, u32[]{:S(2)}) collective-permute-start(bf16[8,128,512]{2,1,0:T(8,128)(2,1)} %bitcast.14), channel_id=1, source_target_pairs={{0,4},{4,0},{1,5},{5,1},{2,6},{6,2},{3,7},{7,3},{8,12},{12,8},{9,1... | collective-permute-start | bytes 3145736 | tf_op jit(solution)/shard_map/token_swap/ppermute | solution.py:305
  61.5 6.5 %collective-permute-start.1 = (bf16[4,16,512]{2,1,0:T(8,128)(2,1)}, bf16[4,16,512]{2,1,0:T(8,128)(2,1)S(1)}, u32[]{:S(2)}, u32[]{:S(2)}) collective-permute-start(bf16[4,16,512]{2,1,0:T(8,128)(2,1)} %token_swap.1), channel_id=1, source_target_pairs={{0,16},{16,32},{32,48},{48,64},{64,80},{80,96},{96,112},{112,128},... | collective-permute-start | bytes 196616 | tf_op jit(solution)/shard_map/token_swap/ppermute | solution.py:363
  64.6 4.9 %collective-permute-start.2 = (bf16[4,16,512]{2,1,0:T(8,128)(2,1)}, bf16[4,16,512]{2,1,0:T(8,128)(2,1)S(1)}, u32[]{:S(2)}, u32[]{:S(2)}) collective-permute-start(bf16[4,16,512]{2,1,0:T(8,128)(2,1)} %token_swap.1), channel_id=1, source_target_pairs={{4,16},{20,32},{36,48},{52,64},{68,80},{84,96},{100,112},{116,128}... | collective-permute-start | bytes 196616 | tf_op jit(solution)/shard_map/token_swap/ppermute | solution.py:364
  69.6 21.3 %copy-start.2 = (bf16[256,256]{1,0:T(8,128)(2,1)S(1)}, bf16[256,256]{1,0:T(8,128)(2,1)}, u32[]{:S(2)}) copy-start(bf16[256,256]{1,0:T(8,128)(2,1)} %constant.27.clone.near_in_ref) | copy-start | bytes 393220
  69.6 21.3 %copy-start.3 = (f32[2,128,128]{2,1,0:T(8,128)S(1)}, f32[2,128,128]{2,1,0:T(8,128)}, u32[]{:S(2)}) copy-start(f32[2,128,128]{2,1,0:T(8,128)} %constant.28.clone.turn_ref) | copy-start | bytes 393220
  69.6 21.3 %copy-start.4 = (bf16[256,256]{1,0:T(8,128)(2,1)S(1)}, bf16[256,256]{1,0:T(8,128)(2,1)}, u32[]{:S(2)}) copy-start(bf16[256,256]{1,0:T(8,128)(2,1)} %constant.29.clone.near_out_ref) | copy-start | bytes 393220
  69.6 21.3 %copy-start.5 = (bf16[256,128]{1,0:T(8,128)(2,1)S(1)}, bf16[256,128]{1,0:T(8,128)(2,1)}, u32[]{:S(2)}) copy-start(bf16[256,128]{1,0:T(8,128)(2,1)} %constant.26.clone.into_ref) | copy-start | bytes 196612
  69.6 21.3 %copy-start.6 = (bf16[128,256]{1,0:T(8,128)(2,1)S(1)}, bf16[128,256]{1,0:T(8,128)(2,1)}, u32[]{:S(2)}) copy-start(bf16[128,256]{1,0:T(8,128)(2,1)} %constant.30.clone.back_ref) | copy-start | bytes 196612
  92.5 13.5 %all-to-all-start.3 = ((bf16[32,16,128]{2,1,0:T(8,128)(2,1)}), bf16[32,16,128]{2,1,0:T(8,128)(2,1)S(1)}, u32[]{:S(2)}, u32[]{:S(2)}) async-start(bf16[32,16,128]{2,1,0:T(8,128)(2,1)} %conv.1), calls=%async_computation.3 | async-start | bytes 262144 | tf_op jit(solution)/shard_map/conv/all_to_all | solution.py:394
  98.8 34.1 %copy-start = (bf16[8,8,64,128]{3,2,1,0:T(8,128)(2,1)S(1)}, bf16[8,8,64,128]{3,2,1,0:T(8,128)(2,1)}, u32[]{:S(2)}) copy-start(bf16[8,8,64,128]{3,2,1,0:T(8,128)(2,1)} %all-gather.4.cloned.1.call-done.own_ref) | copy-start | bytes 3145732
  98.8 17.2 %collective-permute-start.3 = (bf16[8,8,64,128]{3,2,1,0:T(8,128)(2,1)}, bf16[8,8,64,128]{3,2,1,0:T(8,128)(2,1)S(1)}, u32[]{:S(2)}, u32[]{:S(2)}) collective-permute-start(bf16[8,8,64,128]{3,2,1,0:T(8,128)(2,1)} %all-gather.4.cloned.1.call-done.own_ref), channel_id=1, source_target_pairs={{0,4},{4,0},{1,5},{5,1},{2,6},{6,2},{3,7},{7,3},{8,12},{12,8},{9,1... | collective-permute-start | bytes 3145736 | tf_op jit(solution)/shard_map/out_weight_swap/ppermute | solution.py:305
  107.0 25.9 %all-to-all-start.4 = ((bf16[16,128,128]{2,1,0:T(8,128)(2,1)}), bf16[16,128,128]{2,1,0:T(8,128)(2,1)S(1)}, u32[]{:S(2)}, u32[]{:S(2)}) async-start(bf16[16,128,128]{2,1,0:T(8,128)(2,1)} %bitcast.8), calls=%async_computation.4 | async-start | bytes 1048576 | tf_op jit(solution)/shard_map/gate/all_to_all | solution.py:399
Sparse Core Ops, SparseCore 0:
  9.4 45.1 all-gather.5
  56.7 42.0 all-gather.3

commit v9 on v8

--- a/solution.py
+++ b/solution.py
@@ -355,9 +355,8 @@
             tail_body,
             shape((tp, HALO, feats), BF16),
             "hv",
-            (own,),
+            (pltpu.with_memory_space_constraint(own, pltpu.HBM),),
             copies_of(tp),
-            limit=60,
             cost=pl.CostEstimate(flops=20000000000, bytes_accessed=2 * own.size, transcendentals=0),
         )
         halo_own = lax.ppermute(tail, OUTER, [(i, i + 1) for i in range(outer - 1)])

time: 142 us -> 141 us (level)
  transfers between devices with their start and end apart: 10 -> 10, of which waited for: 5 -> 5; matrix products, arithmetic and copies ran while one was open for 0% -> 0% of each run, Pallas kernels for 8% -> 7%
where the time goes in v9:
time: 141 us; the launch traced here: 140 us
  waiting for transfers between devices  51.6 us (37%)
  starting transfers between devices  45.7 us (32%)
  blocking collectives  18 us (13%)
  between operations  13.6 us (10%)
  Pallas kernels  11.3 us (8%)
    all_to_all x1, waiting for transfers between devices, shards(): got = lax.all_to_all(send, ('y',) + INNER, 0, 0)  19.6 us
    all_to_all x1, blocking collectives, shards(): got = lax.all_to_all(send, OUTER, 0, 0)  18 us
    all_to_all x1, waiting for transfers between devices, shards(): lax.all_to_all(gated.reshape(inner * tp, length, chans), INNER + ('tp',),...  17 us
    ppermute x2, starting transfers between devices, swap(): return lax.ppermute(value, axis, [(0, 1), (1, 0)])  12.9 us
    pallas_call x7, Pallas kernels, call(): pl.pallas_call(body, out_shape=out_shape, in_specs=specs[:len(args)], out...  11.3 us
    all_to_all x1, starting transfers between devices, shards(): got = lax.all_to_all(send, ('y',) + INNER, 0, 0)  10.6 us
    all_gather x1, waiting for transfers between devices, shards(): own = lax.all_gather(tokens, ('tp', 'zl'), axis=0)  8.9 us
    all_to_all x1, starting transfers between devices, shards(): lax.all_to_all(gated.reshape(inner * tp, length, chans), INNER + ('tp',),...  7.94 us
  transfers between devices with their start and end apart: 10, of which 5 were waited for; matrix products, arithmetic and copies ran while one was open for 0% of the time, Pallas kernels for 7%

profile of v9, /device:TPU:1, one launch (start us, length us, event | category | flops | bytes accessed | tf_op | source)
XLA Modules:
  0.0 140.3 jit_solution(4729330628531535906)
XLA Ops:
  6.5 0.7 all-gather.6.cloned.1.call-update
  7.3 2.0 %weight_gather.2 = bf16[32,5,16,128]{3,2,1,0:T(8,128)(2,1)} custom-call(bf16[3,16,512]{2,1,0:T(8,128)(2,1)} %bitcast.20, bf16[16,512]{1,0:T(8,128)(2,1)} %out_w_hbm.1, f32[128,512]{1,0:T(8,128)} %taps_hbm.1), custom_call_target="tpu_custom_call" | custom-call | tf_op jit(solution)/shard_map/weight_gather/pallas_call | solution.py:28
  9.3 10.6 %all-to-all-start = ((bf16[32,5,16,128]{3,2,1,0:T(8,128)(2,1)}), bf16[32,5,16,128]{3,2,1,0:T(8,128)(2,1)S(1)}, u32[]{:S(2)}, u32[]{:S(2)}) async-start(bf16[32,5,16,128]{3,2,1,0:T(8,128)(2,1)} %weight_gather.2), calls=%async_computation | async-start | bytes 1310720 | tf_op jit(solution)/shard_map/weight_gather/all_to_all | solution.py:344
  19.9 19.6 %all-to-all-done.got_ref = bf16[32,5,16,128]{3,2,1,0:T(8,128)(2,1)S(1)} async-done(((bf16[32,5,16,128]{3,2,1,0:T(8,128)(2,1)}), bf16[32,5,16,128]{3,2,1,0:T(8,128)(2,1)S(1)}, u32[]{:S(2)}, u32[]{:S(2)}) %all-to-all-start) | async-done | bytes 655392 | tf_op jit(solution)/shard_map/weight_gather/all_to_all | solution.py:344
  39.5 1.5 %weight_gather.3 = (bf16[4,104,16,128]{3,2,1,0:T(8,128)(2,1)}, bf16[32,16,128]{2,1,0:T(8,128)(2,1)}) custom-call(bf16[32,5,16,128]{3,2,1,0:T(8,128)(2,1)S(1)} %all-to-all-done.got_ref), custom_call_target="tpu_custom_call" | custom-call | tf_op jit(solution)/shard_map/weight_gather/pallas_call | solution.py:28
  41.0 4.0 %all-to-all-start.1 = ((bf16[4,104,16,128]{3,2,1,0:T(8,128)(2,1)}), bf16[4,104,16,128]{3,2,1,0:T(8,128)(2,1)S(1)}, u32[]{:S(2)}, u32[]{:S(2)}) async-start(bf16[4,104,16,128]{3,2,1,0:T(8,128)(2,1)} %get-tuple-element.11), calls=%async_computation.1 | async-start | bytes 3407872 | tf_op jit(solution)/shard_map/weight_gather/all_to_all | solution.py:350
  45.0 0.7 all-gather.4.cloned.1.call-update
  45.7 8.9 %all-gather.6.cloned.1.call-done = bf16[1024,512]{1,0:T(8,128)(2,1)} async-done(((bf16[128,512]{1,0:T(8,128)(2,1)}), bf16[1024,512]{1,0:T(8,128)(2,1)}) %all-gather.6.cloned.1.call-update) | async-done | bytes 1048592 | tf_op jit(solution)/shard_map/token_gather/all_gather | solution.py:331
  54.6 5.5 %collective-permute-start = (bf16[8,128,512]{2,1,0:T(8,128)(2,1)}, bf16[8,128,512]{2,1,0:T(8,128)(2,1)}, u32[]{:S(2)}, u32[]{:S(2)}) collective-permute-start(bf16[8,128,512]{2,1,0:T(8,128)(2,1)} %bitcast.14), channel_id=1, source_target_pairs={{0,4},{4,0},{1,5},{5,1},{2,6},{6,2},{3,7},{7,3},{8,12},{12,8},{9,1... | collective-permute-start | bytes 3145736 | tf_op jit(solution)/shard_map/token_swap/ppermute | solution.py:305
  60.1 0.8 token_swap.1
  60.9 3.1 %collective-permute-start.1 = (bf16[4,16,512]{2,1,0:T(8,128)(2,1)S(1)}, bf16[4,16,512]{2,1,0:T(8,128)(2,1)S(1)}, u32[]{:S(2)}, u32[]{:S(2)}) collective-permute-start(bf16[4,16,512]{2,1,0:T(8,128)(2,1)S(1)} %token_swap.1), channel_id=1, source_target_pairs={{0,16},{16,32},{32,48},{48,64},{64,80},{80,96},{96,112},{112,128},... | collective-permute-start | bytes 196616 | tf_op jit(solution)/shard_map/token_swap/ppermute | solution.py:362
  64.0 3.3 %collective-permute-start.2 = (bf16[4,16,512]{2,1,0:T(8,128)(2,1)S(1)}, bf16[4,16,512]{2,1,0:T(8,128)(2,1)S(1)}, u32[]{:S(2)}, u32[]{:S(2)}) collective-permute-start(bf16[4,16,512]{2,1,0:T(8,128)(2,1)S(1)} %token_swap.1), channel_id=1, source_target_pairs={{4,16},{20,32},{36,48},{52,64},{68,80},{84,96},{100,112},{116,128}... | collective-permute-start | bytes 196616 | tf_op jit(solution)/shard_map/token_swap/ppermute | solution.py:363
  67.3 0.1 add_bitcast_fusion.place_ref
  67.4 0.0 collective-permute-done.1.halo_own_ref
  67.4 1.2 collective-permute-done.2.halo_other_ref
  68.6 0.0 all-to-all-done.1.got_ref
  68.6 0.0 collective-permute-done.other_hbm
  68.7 0.0 copy-start.2
  68.7 0.0 copy-start.3
  68.7 0.0 copy-start.4
  68.7 0.0 copy-start.5
  68.7 0.0 copy-start.6
  68.7 3.3 %project.1 = (f32[512,256]{1,0:T(8,128)S(1)}, bf16[32,16,128]{2,1,0:T(8,128)(2,1)S(1)}, bf16[512,128]{1,0:T(8,128)(2,1)S(1)}) custom-call(s32[1,3]{1,0:T(1,128)S(1)} %add_bitcast_fusion.place_ref, bf16[8,128,512]{2,1,0:T(8,128)(2,1)S(1)} %bitcast.16, bf16[8,128,512]{2,1,0:T(8,128)(2,1)} %collective-permute-done.other_hbm, ...), custom_call_target="tpu_custom_call" | custom-call | tf_op jit(solution)/shard_map/project/pallas_call | solution.py:28
  72.0 18.0 %all_to_all.25.sig_ref = bf16[32,16,128]{2,1,0:T(8,128)(2,1)S(1)} all-to-all(bf16[32,16,128]{2,1,0:T(8,128)(2,1)S(1)} %get-tuple-element.13), channel_id=1, replica_groups=mesh['y'=8,'x'=4,'zl'=2,'co'=2,'tp'=4] {'y','x'}, dimensions={0} | all-to-all | bytes 262144 | tf_op jit(solution)/shard_map/conv/all_to_all | solution.py:387
  90.1 1.6 %conv.1 = bf16[32,16,128]{2,1,0:T(8,128)(2,1)} custom-call(bf16[32,16,128]{2,1,0:T(8,128)(2,1)S(1)} %all_to_all.25.sig_ref, bf16[512,128]{1,0:T(8,128)(2,1)S(1)} %get-tuple-element.14.taps_ref, bf16[256,128]{1,0:T(8,128)(2,1)S(1)} %copy-done.5, bf16[256,256]{1,0:T(8,128)(2,1)S(1)} %copy-done.2, f32[2,128,128]{2,1,0:T(8,128)S(1)} %copy-done.3, ...), custom_call_target="tpu_custom_call" | custom-call | tf_op jit(solution)/shard_map/conv/pallas_call | solution.py:28
  91.6 3.9 %all-to-all-start.3 = ((bf16[32,16,128]{2,1,0:T(8,128)(2,1)}), bf16[32,16,128]{2,1,0:T(8,128)(2,1)S(1)}, u32[]{:S(2)}, u32[]{:S(2)}) async-start(bf16[32,16,128]{2,1,0:T(8,128)(2,1)} %conv.1), calls=%async_computation.3 | async-start | bytes 262144 | tf_op jit(solution)/shard_map/conv/all_to_all | solution.py:393
  95.5 3.4 %all-gather.4.cloned.1.call-done.own_ref = bf16[8,8,64,128]{3,2,1,0:T(8,128)(2,1)} async-done(((bf16[1,8,64,128]{3,2,1,0:T(8,128)(2,1)}), bf16[8,8,64,128]{3,2,1,0:T(8,128)(2,1)}) %all-gather.4.cloned.1.call-update) | async-done | bytes 1048592 | tf_op jit(solution)/shard_map/out_weight_gather/all_gather | solution.py:369
  98.9 7.4 %collective-permute-start.3 = (bf16[8,8,64,128]{3,2,1,0:T(8,128)(2,1)}, bf16[8,8,64,128]{3,2,1,0:T(8,128)(2,1)S(1)}, u32[]{:S(2)}, u32[]{:S(2)}) collective-permute-start(bf16[8,8,64,128]{3,2,1,0:T(8,128)(2,1)} %all-gather.4.cloned.1.call-done.own_ref), channel_id=1, source_target_pairs={{0,4},{4,0},{1,5},{5,1},{2,6},{6,2},{3,7},{7,3},{8,12},{12,8},{9,1... | collective-permute-start | bytes 3145736 | tf_op jit(solution)/shard_map/out_weight_swap/ppermute | solution.py:305
  106.3 0.9 gate.1
  107.3 7.9 %all-to-all-start.4 = ((bf16[16,128,128]{2,1,0:T(8,128)(2,1)}), bf16[16,128,128]{2,1,0:T(8,128)(2,1)S(1)}, u32[]{:S(2)}, u32[]{:S(2)}) async-start(bf16[16,128,128]{2,1,0:T(8,128)(2,1)} %bitcast.8), calls=%async_computation.4 | async-start | bytes 1048576 | tf_op jit(solution)/shard_map/gate/all_to_all | solution.py:398
  115.2 17.0 %all-to-all-done.4 = bf16[16,128,128]{2,1,0:T(8,128)(2,1)S(1)} async-done(((bf16[16,128,128]{2,1,0:T(8,128)(2,1)}), bf16[16,128,128]{2,1,0:T(8,128)(2,1)S(1)}, u32[]{:S(2)}, u32[]{:S(2)}) %all-to-all-start.4) | async-done | bytes 524320 | tf_op jit(solution)/shard_map/gate/all_to_all | solution.py:398
  132.2 1.2 out_project.1
  (19 shorter events, 0.0 us)
Async XLA Ops:
  6.5 48.1 %all-gather.6.cloned.1.call-start = ((), (), s32[]{:S(2)}) async-start(), calls=%async_computation.6 | async-start | bytes 1179648 | tf_op jit(solution)/shard_map/token_gather/all_gather | solution.py:331
  9.3 30.2 %all-to-all-start = ((bf16[32,5,16,128]{3,2,1,0:T(8,128)(2,1)}), bf16[32,5,16,128]{3,2,1,0:T(8,128)(2,1)S(1)}, u32[]{:S(2)}, u32[]{:S(2)}) async-start(bf16[32,5,16,128]{3,2,1,0:T(8,128)(2,1)} %weight_gather.2), calls=%async_computation | async-start | bytes 1310720 | tf_op jit(solution)/shard_map/weight_gather/all_to_all | solution.py:344
  41.0 27.7 %all-to-all-start.1 = ((bf16[4,104,16,128]{3,2,1,0:T(8,128)(2,1)}), bf16[4,104,16,128]{3,2,1,0:T(8,128)(2,1)S(1)}, u32[]{:S(2)}, u32[]{:S(2)}) async-start(bf16[4,104,16,128]{3,2,1,0:T(8,128)(2,1)} %get-tuple-element.11), calls=%async_computation.1 | async-start | bytes 3407872 | tf_op jit(solution)/shard_map/weight_gather/all_to_all | solution.py:350
  45.0 53.9 %all-gather.4.cloned.1.call-start = ((), (), s32[]{:S(2)}) async-start(), calls=%async_computation.5 | async-start | bytes 1179648 | tf_op jit(solution)/shard_map/out_weight_gather/all_gather | solution.py:369
  54.6 14.0 %copy-start.1 = (bf16[1024,512]{1,0:T(8,128)(2,1)S(1)}, bf16[1024,512]{1,0:T(8,128)(2,1)}, u32[]{:S(2)}) copy-start(bf16[1024,512]{1,0:T(8,128)(2,1)} %all-gather.6.cloned.1.call-done) | copy-start | bytes 3145732
  54.6 14.0 %copy-start.7 = (f32[3,3,512]{2,1,0:T(4,128)S(1)}, f32[3,3,512]{2,1,0:T(4,128)}, u32[]{:S(2)}) copy-start(f32[3,3,512]{2,1,0:T(4,128)} %taps_ref.1) | copy-start | bytes 55300
  54.6 14.0 %copy-start.8 = (f32[2048]{0:T(1024)S(1)}, f32[2048]{0:T(1024)}, u32[]{:S(2)}) copy-start(f32[2048]{0:T(1024)} %param.13) | copy-start | bytes 24580
  54.6 14.1 %copy-start.9 = (f32[512]{0:T(512)S(1)}, f32[512]{0:T(512)}, u32[]{:S(2)}) copy-start(f32[512]{0:T(512)} %param.17) | copy-start | bytes 6148
  54.6 14.0 %collective-permute-start = (bf16[8,128,512]{2,1,0:T(8,128)(2,1)}, bf16[8,128,512]{2,1,0:T(8,128)(2,1)}, u32[]{:S(2)}, u32[]{:S(2)}) collective-permute-start(bf16[8,128,512]{2,1,0:T(8,128)(2,1)} %bitcast.14), channel_id=1, source_target_pairs={{0,4},{4,0},{1,5},{5,1},{2,6},{6,2},{3,7},{7,3},{8,12},{12,8},{9,1... | collective-permute-start | bytes 3145736 | tf_op jit(solution)/shard_map/token_swap/ppermute | solution.py:305
  60.9 6.5 %collective-permute-start.1 = (bf16[4,16,512]{2,1,0:T(8,128)(2,1)S(1)}, bf16[4,16,512]{2,1,0:T(8,128)(2,1)S(1)}, u32[]{:S(2)}, u32[]{:S(2)}) collective-permute-start(bf16[4,16,512]{2,1,0:T(8,128)(2,1)S(1)} %token_swap.1), channel_id=1, source_target_pairs={{0,16},{16,32},{32,48},{48,64},{64,80},{80,96},{96,112},{112,128},... | collective-permute-start | bytes 196616 | tf_op jit(solution)/shard_map/token_swap/ppermute | solution.py:362
  64.0 4.6 %collective-permute-start.2 = (bf16[4,16,512]{2,1,0:T(8,128)(2,1)S(1)}, bf16[4,16,512]{2,1,0:T(8,128)(2,1)S(1)}, u32[]{:S(2)}, u32[]{:S(2)}) collective-permute-start(bf16[4,16,512]{2,1,0:T(8,128)(2,1)S(1)} %token_swap.1), channel_id=1, source_target_pairs={{4,16},{20,32},{36,48},{52,64},{68,80},{84,96},{100,112},{116,128}... | collective-permute-start | bytes 196616 | tf_op jit(solution)/shard_map/token_swap/ppermute | solution.py:363
  68.7 21.4 %copy-start.2 = (bf16[256,256]{1,0:T(8,128)(2,1)S(1)}, bf16[256,256]{1,0:T(8,128)(2,1)}, u32[]{:S(2)}) copy-start(bf16[256,256]{1,0:T(8,128)(2,1)} %constant.27.clone.near_in_ref) | copy-start | bytes 393220
  68.7 21.3 %copy-start.3 = (f32[2,128,128]{2,1,0:T(8,128)S(1)}, f32[2,128,128]{2,1,0:T(8,128)}, u32[]{:S(2)}) copy-start(f32[2,128,128]{2,1,0:T(8,128)} %constant.28.clone.turn_ref) | copy-start | bytes 393220
  68.7 21.3 %copy-start.4 = (bf16[256,256]{1,0:T(8,128)(2,1)S(1)}, bf16[256,256]{1,0:T(8,128)(2,1)}, u32[]{:S(2)}) copy-start(bf16[256,256]{1,0:T(8,128)(2,1)} %constant.29.clone.near_out_ref) | copy-start | bytes 393220
  68.7 21.3 %copy-start.5 = (bf16[256,128]{1,0:T(8,128)(2,1)S(1)}, bf16[256,128]{1,0:T(8,128)(2,1)}, u32[]{:S(2)}) copy-start(bf16[256,128]{1,0:T(8,128)(2,1)} %constant.26.clone.into_ref) | copy-start | bytes 196612
  68.7 21.3 %copy-start.6 = (bf16[128,256]{1,0:T(8,128)(2,1)S(1)}, bf16[128,256]{1,0:T(8,128)(2,1)}, u32[]{:S(2)}) copy-start(bf16[128,256]{1,0:T(8,128)(2,1)} %constant.30.clone.back_ref) | copy-start | bytes 196612
  91.6 14.7 %all-to-all-start.3 = ((bf16[32,16,128]{2,1,0:T(8,128)(2,1)}), bf16[32,16,128]{2,1,0:T(8,128)(2,1)S(1)}, u32[]{:S(2)}, u32[]{:S(2)}) async-start(bf16[32,16,128]{2,1,0:T(8,128)(2,1)} %conv.1), calls=%async_computation.3 | async-start | bytes 262144 | tf_op jit(solution)/shard_map/conv/all_to_all | solution.py:393
  98.9 33.4 %copy-start = (bf16[8,8,64,128]{3,2,1,0:T(8,128)(2,1)S(1)}, bf16[8,8,64,128]{3,2,1,0:T(8,128)(2,1)}, u32[]{:S(2)}) copy-start(bf16[8,8,64,128]{3,2,1,0:T(8,128)(2,1)} %all-gather.4.cloned.1.call-done.own_ref) | copy-start | bytes 3145732
  98.9 16.3 %collective-permute-start.3 = (bf16[8,8,64,128]{3,2,1,0:T(8,128)(2,1)}, bf16[8,8,64,128]{3,2,1,0:T(8,128)(2,1)S(1)}, u32[]{:S(2)}, u32[]{:S(2)}) collective-permute-start(bf16[8,8,64,128]{3,2,1,0:T(8,128)(2,1)} %all-gather.4.cloned.1.call-done.own_ref), channel_id=1, source_target_pairs={{0,4},{4,0},{1,5},{5,1},{2,6},{6,2},{3,7},{7,3},{8,12},{12,8},{9,1... | collective-permute-start | bytes 3145736 | tf_op jit(solution)/shard_map/out_weight_swap/ppermute | solution.py:305
  107.3 25.0 %all-to-all-start.4 = ((bf16[16,128,128]{2,1,0:T(8,128)(2,1)}), bf16[16,128,128]{2,1,0:T(8,128)(2,1)S(1)}, u32[]{:S(2)}, u32[]{:S(2)}) async-start(bf16[16,128,128]{2,1,0:T(8,128)(2,1)} %bitcast.8), calls=%async_computation.4 | async-start | bytes 1048576 | tf_op jit(solution)/shard_map/gate/all_to_all | solution.py:398
Sparse Core Ops, SparseCore 0:
  9.4 45.1 all-gather.5
  56.7 42.1 all-gather.3

commit v10 on v9

--- a/solution.py
+++ b/solution.py
@@ -158,11 +158,31 @@
         send_ref[way, parts * sources :] = piece.astype(BF16)
 
 
+def scaled(pieces, gain_ref):
+    feats = pieces[0].shape[1]
+    total = sum(jnp.sum(piece * piece, axis=1, keepdims=True) for piece in pieces)
+    scale = lax.rsqrt(total / gain_ref.shape[1] + 1e-05)
+    return [
+        (piece * scale * gain_ref[:, p * feats : (p + 1) * feats]).astype(BF16)
+        for p, piece in enumerate(pieces)
+    ]
+
+
+def norm_body(tok_ref, gain_ref, out_ref):
+    zs, length = out_ref.shape[:2]
+    feats = tok_ref.shape[2]
+    tp = tok_ref.shape[0] // zs
+    for z in range(zs):
+        pieces = [tok_ref[p * zs + z].astype(F32) for p in range(tp)]
+        for p, piece in enumerate(scaled(pieces, gain_ref)):
+            out_ref[z, :, p * feats : (p + 1) * feats] = piece
+
+
 def project_body(
     cores,
     place_ref,
     own_ref,
-    other_hbm,
+    other_ref,
     halo_own_ref,
     halo_other_ref,
     gain_ref,
@@ -172,13 +192,10 @@
     gates_ref,
     send_ref,
     filter_ref,
-    other_ref,
     x_ref,
     proj_ref,
-    sems,
 ):
     core = place_ref[0, 0]
-    copies = started([(other_hbm, other_ref)], sems)
     parts = 3
     ways, _, rows, lanes = got_ref.shape
     groups = send_ref.shape[0]
@@ -203,33 +220,24 @@
             at = (y * ways + x) * rows
             filter_ref[at : at + rows] = got_ref[x, first + y]
 
-    blocks, length, feats = own_ref.shape
-    tp = x_ref.shape[1] // feats
-
-    def put(pieces, at):
-        total = sum(jnp.sum(piece * piece, axis=1, keepdims=True) for piece in pieces)
-        scale = lax.rsqrt(total / (tp * feats) + 1e-05)
-        for p, piece in enumerate(pieces):
-            gain = gain_ref[:, p * feats : (p + 1) * feats]
-            x_ref[at : at + piece.shape[0], p * feats : (p + 1) * feats] = (piece * scale * gain).astype(BF16)
+    zs, length = own_ref.shape[:2]
+    tp, _, feats = halo_own_ref.shape
 
     def project(count):
         got = jnp.dot(x_ref[:count], weight, preferred_element_type=F32)
         return got.astype(BF16).astype(F32)
 
-    zs = blocks // tp
     weight = jnp.concatenate([column(part) for part in range(parts)], axis=1)
     last = core == cores - 1
     halo = [
         jnp.where(last, halo_own_ref[p].astype(F32), halo_other_ref[p].astype(F32)) for p in range(tp)
     ]
     for ref, at_core in ((own_ref, core), (other_ref, cores - 1 - core)):
-        if ref is other_ref:
-            finish(copies)
         for z in range(zs):
-            put([ref[p * zs + z].astype(F32) for p in range(tp)], z * length)
+            x_ref[z * length : (z + 1) * length] = ref[z]
         if ref is own_ref:
-            put(halo, zs * length)
+            for p, piece in enumerate(scaled(halo, gain_ref)):
+                x_ref[zs * length :, p * feats : (p + 1) * feats] = piece
             got = project(zs * length + HALO)
             proj_ref[:HALO] = got[zs * length :]
         else:
@@ -365,6 +373,10 @@
             OUTER + ("co",),
             [(i * cores + cores - 1, (i + 1) * cores) for i in range(outer - 1)],
         )
+        gain = norm_gain.reshape(1, tp * feats)
+        normed = shape((ways["zl"], length, tp * feats), BF16)
+        x_own = call(norm_body, normed, "vvv", (own, gain))
+        x_other = call(norm_body, normed, "vvv", (other, gain))
     with jax.named_scope("out_weight_gather"):
         out_w = lax.all_gather(piece.reshape(along, inner * depth, LANES), ("x", "zl"), axis=0)
     with jax.named_scope("project"):
@@ -378,10 +390,10 @@
                 blocks,
                 shape((outer * rows, LANES), BF16),
             ),
-            "svh" + "v" * 9,
-            (where, own, other, halo_own, halo_other, norm_gain.reshape(1, tp * feats))
+            "s" + "v" * 11,
+            (where, x_own, x_other, halo_own, halo_other, gain)
             + (short_taps, skip_gain.reshape(1, inner * chans), got),
-            held(other, wide, proj) + copies_of(1),
+            held(wide, proj),
         )
     with jax.named_scope("conv"):
         got = lax.all_to_all(send, OUTER, 0, 0)

time: 141 us -> 141 us (level)
  local copies, waits for them, and re-layouts: 0.05 us -> 2.24 us
  waiting for transfers between devices: 51.6 us -> 49.5 us
    unnamed x20 -> x24, local copies, waits for them, and re-layouts: 0.05 us -> 2.24 us
    pallas_call x7 -> x9, Pallas kernels: 11.3 us -> 11 us  [call(): pl.pallas_call(body, out_shape=out_shape, in_specs=specs[:len(args)], out...]
  transfers between devices with their start and end apart: 10 -> 10, of which waited for: 5 -> 4; matrix products, arithmetic and copies ran while one was open for 0% -> 0% of each run, Pallas kernels for 7% -> 7%
where the time goes in v10:
time: 141 us; the launch traced here: 140 us
  waiting for transfers between devices  49.5 us (35%)
  starting transfers between devices  45.8 us (32%)
  blocking collectives  18.1 us (13%)
  between operations  13.6 us (10%)
  Pallas kernels  11 us (8%)
  local copies, waits for them, and re-layouts  2.24 us (2%)
    all_to_all x1, waiting for transfers between devices, shards(): got = lax.all_to_all(send, ('y',) + INNER, 0, 0)  19.6 us
    all_to_all x1, blocking collectives, shards(): got = lax.all_to_all(send, OUTER, 0, 0)  18.1 us
    all_to_all x1, waiting for transfers between devices, shards(): lax.all_to_all(gated.reshape(inner * tp, length, chans), INNER + ('tp',),...  17.1 us
    ppermute x2, starting transfers between devices, swap(): return lax.ppermute(value, axis, [(0, 1), (1, 0)])  12.8 us
    pallas_call x9, Pallas kernels, call(): pl.pallas_call(body, out_shape=out_shape, in_specs=specs[:len(args)], out...  11 us
    all_to_all x1, starting transfers between devices, shards(): got = lax.all_to_all(send, ('y',) + INNER, 0, 0)  10.6 us
    all_gather x1, waiting for transfers between devices, shards(): own = lax.all_gather(tokens, ('tp', 'zl'), axis=0)  8.89 us
    all_to_all x1, starting transfers between devices, shards(): lax.all_to_all(gated.reshape(inner * tp, length, chans), INNER + ('tp',),...  8.16 us
  transfers between devices with their start and end apart: 10, of which 4 were waited for; matrix products, arithmetic and copies ran while one was open for 0% of the time, Pallas kernels for 7%

profile of v10, /device:TPU:1, one launch (start us, length us, event | category | flops | bytes accessed | tf_op | source)
XLA Modules:
  0.0 140.4 jit_solution(9595693201816029338)
XLA Ops:
  6.5 0.7 all-gather.6.cloned.1.call-update
  7.3 2.0 %weight_gather.2 = bf16[32,5,16,128]{3,2,1,0:T(8,128)(2,1)} custom-call(bf16[3,16,512]{2,1,0:T(8,128)(2,1)} %bitcast.22, bf16[16,512]{1,0:T(8,128)(2,1)} %out_w_hbm.1, f32[128,512]{1,0:T(8,128)} %taps_hbm.1), custom_call_target="tpu_custom_call" | custom-call | tf_op jit(solution)/shard_map/weight_gather/pallas_call | solution.py:28
  9.3 10.6 %all-to-all-start = ((bf16[32,5,16,128]{3,2,1,0:T(8,128)(2,1)}), bf16[32,5,16,128]{3,2,1,0:T(8,128)(2,1)S(1)}, u32[]{:S(2)}, u32[]{:S(2)}) async-start(bf16[32,5,16,128]{3,2,1,0:T(8,128)(2,1)} %weight_gather.2), calls=%async_computation | async-start | bytes 1310720 | tf_op jit(solution)/shard_map/weight_gather/all_to_all | solution.py:352
  19.8 19.6 %all-to-all-done.got_ref = bf16[32,5,16,128]{3,2,1,0:T(8,128)(2,1)S(1)} async-done(((bf16[32,5,16,128]{3,2,1,0:T(8,128)(2,1)}), bf16[32,5,16,128]{3,2,1,0:T(8,128)(2,1)S(1)}, u32[]{:S(2)}, u32[]{:S(2)}) %all-to-all-start) | async-done | bytes 655392 | tf_op jit(solution)/shard_map/weight_gather/all_to_all | solution.py:352
  39.5 1.5 %weight_gather.3 = (bf16[4,104,16,128]{3,2,1,0:T(8,128)(2,1)}, bf16[32,16,128]{2,1,0:T(8,128)(2,1)}) custom-call(bf16[32,5,16,128]{3,2,1,0:T(8,128)(2,1)S(1)} %all-to-all-done.got_ref), custom_call_target="tpu_custom_call" | custom-call | tf_op jit(solution)/shard_map/weight_gather/pallas_call | solution.py:28
  41.0 4.0 %all-to-all-start.1 = ((bf16[4,104,16,128]{3,2,1,0:T(8,128)(2,1)}), bf16[4,104,16,128]{3,2,1,0:T(8,128)(2,1)S(1)}, u32[]{:S(2)}, u32[]{:S(2)}) async-start(bf16[4,104,16,128]{3,2,1,0:T(8,128)(2,1)} %get-tuple-element.11), calls=%async_computation.1 | async-start | bytes 3407872 | tf_op jit(solution)/shard_map/weight_gather/all_to_all | solution.py:358
  45.0 0.7 all-gather.4.cloned.1.call-update
  45.7 8.9 %all-gather.6.cloned.1.call-done = bf16[1024,512]{1,0:T(8,128)(2,1)} async-done(((bf16[128,512]{1,0:T(8,128)(2,1)}), bf16[1024,512]{1,0:T(8,128)(2,1)}) %all-gather.6.cloned.1.call-update) | async-done | bytes 1048592 | tf_op jit(solution)/shard_map/token_gather/all_gather | solution.py:339
  54.6 5.5 %collective-permute-start = (bf16[8,128,512]{2,1,0:T(8,128)(2,1)}, bf16[8,128,512]{2,1,0:T(8,128)(2,1)S(1)}, u32[]{:S(2)}, u32[]{:S(2)}) collective-permute-start(bf16[8,128,512]{2,1,0:T(8,128)(2,1)} %bitcast.14), channel_id=1, source_target_pairs={{0,4},{4,0},{1,5},{5,1},{2,6},{6,2},{3,7},{7,3},{8,12},{12,8},{9,1... | collective-permute-start | bytes 3145736 | tf_op jit(solution)/shard_map/token_swap/ppermute | solution.py:313
  60.1 0.8 token_swap.5
  60.9 3.1 %collective-permute-start.1 = (bf16[4,16,512]{2,1,0:T(8,128)(2,1)S(1)}, bf16[4,16,512]{2,1,0:T(8,128)(2,1)S(1)}, u32[]{:S(2)}, u32[]{:S(2)}) collective-permute-start(bf16[4,16,512]{2,1,0:T(8,128)(2,1)S(1)} %token_swap.5), channel_id=1, source_target_pairs={{0,16},{16,32},{32,48},{48,64},{64,80},{80,96},{96,112},{112,128},... | collective-permute-start | bytes 196616 | tf_op jit(solution)/shard_map/token_swap/ppermute | solution.py:370
  64.0 3.3 %collective-permute-start.2 = (bf16[4,16,512]{2,1,0:T(8,128)(2,1)S(1)}, bf16[4,16,512]{2,1,0:T(8,128)(2,1)S(1)}, u32[]{:S(2)}, u32[]{:S(2)}) collective-permute-start(bf16[4,16,512]{2,1,0:T(8,128)(2,1)S(1)} %token_swap.5), channel_id=1, source_target_pairs={{4,16},{20,32},{36,48},{52,64},{68,80},{84,96},{100,112},{116,128}... | collective-permute-start | bytes 196616 | tf_op jit(solution)/shard_map/token_swap/ppermute | solution.py:371
  67.3 0.1 add_bitcast_fusion.place_ref
  67.4 0.0 copy-start.11
  67.4 0.4 token_swap.3.own_ref
  67.8 0.4 token_swap.4.other_ref
  68.2 1.0 copy-done
  69.2 0.0 collective-permute-done.1.halo_own_ref
  69.3 1.2 copy-done.1
  70.5 0.0 copy-start.9
  70.5 2.3 %project.1 = (f32[512,256]{1,0:T(8,128)S(1)}, bf16[32,16,128]{2,1,0:T(8,128)(2,1)S(1)}, bf16[512,128]{1,0:T(8,128)(2,1)S(1)}) custom-call(s32[1,3]{1,0:T(1,128)S(1)} %add_bitcast_fusion.place_ref, bf16[2,128,2048]{2,1,0:T(8,128)(2,1)S(1)} %token_swap.3.own_ref, bf16[2,128,2048]{2,1,0:T(8,128)(2,1)S(1)} %copy-done.1, ...), custom_call_target="tpu_custom_call" | custom-call | tf_op jit(solution)/shard_map/project/pallas_call | solution.py:28
  72.8 18.1 %all_to_all.25.sig_ref = bf16[32,16,128]{2,1,0:T(8,128)(2,1)S(1)} all-to-all(bf16[32,16,128]{2,1,0:T(8,128)(2,1)S(1)} %get-tuple-element.13), channel_id=1, replica_groups=mesh['y'=8,'x'=4,'zl'=2,'co'=2,'tp'=4] {'y','x'}, dimensions={0} | all-to-all | bytes 262144 | tf_op jit(solution)/shard_map/conv/all_to_all | solution.py:399
  90.9 1.6 %conv.1 = bf16[32,16,128]{2,1,0:T(8,128)(2,1)} custom-call(bf16[32,16,128]{2,1,0:T(8,128)(2,1)S(1)} %all_to_all.25.sig_ref, bf16[512,128]{1,0:T(8,128)(2,1)S(1)} %get-tuple-element.14.taps_ref, bf16[256,128]{1,0:T(8,128)(2,1)S(1)} %copy-done.8, bf16[256,256]{1,0:T(8,128)(2,1)S(1)} %copy-done.4, f32[2,128,128]{2,1,0:T(8,128)S(1)} %copy-done.5, ...), custom_call_target="tpu_custom_call" | custom-call | tf_op jit(solution)/shard_map/conv/pallas_call | solution.py:28
  92.5 3.9 %all-to-all-start.3 = ((bf16[32,16,128]{2,1,0:T(8,128)(2,1)}), bf16[32,16,128]{2,1,0:T(8,128)(2,1)S(1)}, u32[]{:S(2)}, u32[]{:S(2)}) async-start(bf16[32,16,128]{2,1,0:T(8,128)(2,1)} %conv.1), calls=%async_computation.3 | async-start | bytes 262144 | tf_op jit(solution)/shard_map/conv/all_to_all | solution.py:405
  96.4 2.5 %all-gather.4.cloned.1.call-done.own_ref = bf16[8,8,64,128]{3,2,1,0:T(8,128)(2,1)} async-done(((bf16[1,8,64,128]{3,2,1,0:T(8,128)(2,1)}), bf16[8,8,64,128]{3,2,1,0:T(8,128)(2,1)}) %all-gather.4.cloned.1.call-update) | async-done | bytes 1048592 | tf_op jit(solution)/shard_map/out_weight_gather/all_gather | solution.py:381
  98.9 7.3 %collective-permute-start.3 = (bf16[8,8,64,128]{3,2,1,0:T(8,128)(2,1)}, bf16[8,8,64,128]{3,2,1,0:T(8,128)(2,1)S(1)}, u32[]{:S(2)}, u32[]{:S(2)}) collective-permute-start(bf16[8,8,64,128]{3,2,1,0:T(8,128)(2,1)} %all-gather.4.cloned.1.call-done.own_ref), channel_id=1, source_target_pairs={{0,4},{4,0},{1,5},{5,1},{2,6},{6,2},{3,7},{7,3},{8,12},{12,8},{9,1... | collective-permute-start | bytes 3145736 | tf_op jit(solution)/shard_map/out_weight_swap/ppermute | solution.py:313
  106.2 0.0 all-to-all-done.3.conv_ref
  106.2 0.9 gate.1
  107.2 8.2 %all-to-all-start.4 = ((bf16[16,128,128]{2,1,0:T(8,128)(2,1)}), bf16[16,128,128]{2,1,0:T(8,128)(2,1)S(1)}, u32[]{:S(2)}, u32[]{:S(2)}) async-start(bf16[16,128,128]{2,1,0:T(8,128)(2,1)} %bitcast.8), calls=%async_computation.4 | async-start | bytes 1048576 | tf_op jit(solution)/shard_map/gate/all_to_all | solution.py:410
  115.3 0.0 collective-permute-done.3.other_ref
  115.3 17.1 %all-to-all-done.4 = bf16[16,128,128]{2,1,0:T(8,128)(2,1)S(1)} async-done(((bf16[16,128,128]{2,1,0:T(8,128)(2,1)}), bf16[16,128,128]{2,1,0:T(8,128)(2,1)S(1)}, u32[]{:S(2)}, u32[]{:S(2)}) %all-to-all-start.4) | async-done | bytes 524320 | tf_op jit(solution)/shard_map/gate/all_to_all | solution.py:410
  132.4 1.1 out_project.1
  (25 shorter events, 0.0 us)
Async XLA Ops:
  6.5 48.1 %all-gather.6.cloned.1.call-start = ((), (), s32[]{:S(2)}) async-start(), calls=%async_computation.6 | async-start | bytes 1179648 | tf_op jit(solution)/shard_map/token_gather/all_gather | solution.py:339
  9.3 30.2 %all-to-all-start = ((bf16[32,5,16,128]{3,2,1,0:T(8,128)(2,1)}), bf16[32,5,16,128]{3,2,1,0:T(8,128)(2,1)S(1)}, u32[]{:S(2)}, u32[]{:S(2)}) async-start(bf16[32,5,16,128]{3,2,1,0:T(8,128)(2,1)} %weight_gather.2), calls=%async_computation | async-start | bytes 1310720 | tf_op jit(solution)/shard_map/weight_gather/all_to_all | solution.py:352
  41.0 28.3 %all-to-all-start.1 = ((bf16[4,104,16,128]{3,2,1,0:T(8,128)(2,1)}), bf16[4,104,16,128]{3,2,1,0:T(8,128)(2,1)S(1)}, u32[]{:S(2)}, u32[]{:S(2)}) async-start(bf16[4,104,16,128]{3,2,1,0:T(8,128)(2,1)} %get-tuple-element.11), calls=%async_computation.1 | async-start | bytes 3407872 | tf_op jit(solution)/shard_map/weight_gather/all_to_all | solution.py:358
  45.0 53.9 %all-gather.4.cloned.1.call-start = ((), (), s32[]{:S(2)}) async-start(), calls=%async_computation.5 | async-start | bytes 1179648 | tf_op jit(solution)/shard_map/out_weight_gather/all_gather | solution.py:381
  54.6 12.8 %copy-start.3 = (bf16[1024,512]{1,0:T(8,128)(2,1)S(1)}, bf16[1024,512]{1,0:T(8,128)(2,1)}, u32[]{:S(2)}) copy-start(bf16[1024,512]{1,0:T(8,128)(2,1)} %all-gather.6.cloned.1.call-done) | copy-start | bytes 3145732
  54.6 12.8 %copy-start.7 = (f32[2048]{0:T(1024)S(1)}, f32[2048]{0:T(1024)}, u32[]{:S(2)}) copy-start(f32[2048]{0:T(1024)} %param.13) | copy-start | bytes 24580
  54.6 13.2 %collective-permute-start = (bf16[8,128,512]{2,1,0:T(8,128)(2,1)}, bf16[8,128,512]{2,1,0:T(8,128)(2,1)S(1)}, u32[]{:S(2)}, u32[]{:S(2)}) collective-permute-start(bf16[8,128,512]{2,1,0:T(8,128)(2,1)} %bitcast.14), channel_id=1, source_target_pairs={{0,4},{4,0},{1,5},{5,1},{2,6},{6,2},{3,7},{7,3},{8,12},{12,8},{9,1... | collective-permute-start | bytes 3145736 | tf_op jit(solution)/shard_map/token_swap/ppermute | solution.py:313
  60.9 8.3 %collective-permute-start.1 = (bf16[4,16,512]{2,1,0:T(8,128)(2,1)S(1)}, bf16[4,16,512]{2,1,0:T(8,128)(2,1)S(1)}, u32[]{:S(2)}, u32[]{:S(2)}) collective-permute-start(bf16[4,16,512]{2,1,0:T(8,128)(2,1)S(1)} %token_swap.5), channel_id=1, source_target_pairs={{0,16},{16,32},{32,48},{48,64},{64,80},{80,96},{96,112},{112,128},... | collective-permute-start | bytes 196616 | tf_op jit(solution)/shard_map/token_swap/ppermute | solution.py:370
  64.0 5.2 %collective-permute-start.2 = (bf16[4,16,512]{2,1,0:T(8,128)(2,1)S(1)}, bf16[4,16,512]{2,1,0:T(8,128)(2,1)S(1)}, u32[]{:S(2)}, u32[]{:S(2)}) collective-permute-start(bf16[4,16,512]{2,1,0:T(8,128)(2,1)S(1)} %token_swap.5), channel_id=1, source_target_pairs={{4,16},{20,32},{36,48},{52,64},{68,80},{84,96},{100,112},{116,128}... | collective-permute-start | bytes 196616 | tf_op jit(solution)/shard_map/token_swap/ppermute | solution.py:371
  67.4 1.8 %copy-start.10 = (f32[3,3,512]{2,1,0:T(4,128)S(1)}, f32[3,3,512]{2,1,0:T(4,128)}, u32[]{:S(2)}) copy-start(f32[3,3,512]{2,1,0:T(4,128)} %taps_ref.1) | copy-start | bytes 55300
  67.4 1.9 %copy-start.11 = (f32[512]{0:T(512)S(1)}, f32[512]{0:T(512)}, u32[]{:S(2)}) copy-start(f32[512]{0:T(512)} %param.17) | copy-start | bytes 6148
  68.2 1.0 copy-start
  69.2 1.2 copy-start.1
  70.5 20.4 %copy-start.4 = (bf16[256,256]{1,0:T(8,128)(2,1)S(1)}, bf16[256,256]{1,0:T(8,128)(2,1)}, u32[]{:S(2)}) copy-start(bf16[256,256]{1,0:T(8,128)(2,1)} %constant.27.clone.near_in_ref) | copy-start | bytes 393220
  70.5 20.4 %copy-start.5 = (f32[2,128,128]{2,1,0:T(8,128)S(1)}, f32[2,128,128]{2,1,0:T(8,128)}, u32[]{:S(2)}) copy-start(f32[2,128,128]{2,1,0:T(8,128)} %constant.28.clone.turn_ref) | copy-start | bytes 393220
  70.5 20.4 %copy-start.6 = (bf16[256,256]{1,0:T(8,128)(2,1)S(1)}, bf16[256,256]{1,0:T(8,128)(2,1)}, u32[]{:S(2)}) copy-start(bf16[256,256]{1,0:T(8,128)(2,1)} %constant.29.clone.near_out_ref) | copy-start | bytes 393220
  70.5 20.4 %copy-start.8 = (bf16[256,128]{1,0:T(8,128)(2,1)S(1)}, bf16[256,128]{1,0:T(8,128)(2,1)}, u32[]{:S(2)}) copy-start(bf16[256,128]{1,0:T(8,128)(2,1)} %constant.26.clone.into_ref) | copy-start | bytes 196612
  70.5 20.4 %copy-start.9 = (bf16[128,256]{1,0:T(8,128)(2,1)S(1)}, bf16[128,256]{1,0:T(8,128)(2,1)}, u32[]{:S(2)}) copy-start(bf16[128,256]{1,0:T(8,128)(2,1)} %constant.30.clone.back_ref) | copy-start | bytes 196612
  92.5 13.7 %all-to-all-start.3 = ((bf16[32,16,128]{2,1,0:T(8,128)(2,1)}), bf16[32,16,128]{2,1,0:T(8,128)(2,1)S(1)}, u32[]{:S(2)}, u32[]{:S(2)}) async-start(bf16[32,16,128]{2,1,0:T(8,128)(2,1)} %conv.1), calls=%async_computation.3 | async-start | bytes 262144 | tf_op jit(solution)/shard_map/conv/all_to_all | solution.py:405
  98.9 33.5 %copy-start.2 = (bf16[8,8,64,128]{3,2,1,0:T(8,128)(2,1)S(1)}, bf16[8,8,64,128]{3,2,1,0:T(8,128)(2,1)}, u32[]{:S(2)}) copy-start(bf16[8,8,64,128]{3,2,1,0:T(8,128)(2,1)} %all-gather.4.cloned.1.call-done.own_ref) | copy-start | bytes 3145732
  98.9 16.5 %collective-permute-start.3 = (bf16[8,8,64,128]{3,2,1,0:T(8,128)(2,1)}, bf16[8,8,64,128]{3,2,1,0:T(8,128)(2,1)S(1)}, u32[]{:S(2)}, u32[]{:S(2)}) collective-permute-start(bf16[8,8,64,128]{3,2,1,0:T(8,128)(2,1)} %all-gather.4.cloned.1.call-done.own_ref), channel_id=1, source_target_pairs={{0,4},{4,0},{1,5},{5,1},{2,6},{6,2},{3,7},{7,3},{8,12},{12,8},{9,1... | collective-permute-start | bytes 3145736 | tf_op jit(solution)/shard_map/out_weight_swap/ppermute | solution.py:313
  107.2 25.2 %all-to-all-start.4 = ((bf16[16,128,128]{2,1,0:T(8,128)(2,1)}), bf16[16,128,128]{2,1,0:T(8,128)(2,1)S(1)}, u32[]{:S(2)}, u32[]{:S(2)}) async-start(bf16[16,128,128]{2,1,0:T(8,128)(2,1)} %bitcast.8), calls=%async_computation.4 | async-start | bytes 1048576 | tf_op jit(solution)/shard_map/gate/all_to_all | solution.py:410
Sparse Core Ops, SparseCore 0:
  9.4 45.1 all-gather.5
  56.7 42.1 all-gather.3
